TPU v7x, 32 devices: a whole 2x2x4 slice. The times are simulated.
32 devices in a mesh: tm: 8 (over z, y), det: 4 (over x, core).
Axes of the slice: x: 2, y: 2, z: 4, core: 2. Of those that a mesh axis runs over, the one named last changes fastest.
Arguments:
- solution: float32 [3, 12288, 128], P(None, ('tm', 'det')), may hold values from -30 to 30
- residual: float32 [3, 12288, 128], P(None, ('tm', 'det')), may hold values from -30 to 30
- direction: float32 [3, 12288, 128], P(None, ('tm', 'det')), may hold values from -30 to 30
- preconditioner: float32 [6, 12288, 128], P(None, ('tm', 'det')), may hold values from -3 to 10, as said below
- pull_index: int32 [8, 4, 2, 4, 16], P('tm', 'det'), may hold values from 0 to 383, as said below
- block_slot: int32 [256, 512], P('det', 'tm'), may hold values from 0 to 127, as said below
- pixel_offset: int32 [256, 65536], P('det', 'tm'), may hold values from 0 to 127
- angle_index: int32 [256, 65536], P('det', 'tm'), may hold values from 0 to 63
- det_weight: float32 [256], replicated, may hold values from 1 to 10
- mode_templates: float32 [256, 16], replicated, may hold values from -6 to 6
- mode_precision: float32 [16], replicated, may hold values from 256 to 2560
Outputs:
- new_solution: float32 [3, 12288, 128], P(None, ('tm', 'det'))
- new_residual: float32 [3, 12288, 128], P(None, ('tm', 'det'))
- new_direction: float32 [3, 12288, 128], P(None, ('tm', 'det'))
Inputs may be any that keep to these rules, and one draw needn't show every extreme that they name: `preconditioner`: at every pixel the six entries form a symmetric positive definite matrix; the three diagonal entries lie in 1 to 10. `pull_index`: for each owner device, reach and det index the 16 block numbers are distinct. `block_slot`: each aligned run of 4 sample blocks of a detector points into one slot.
All inputs are finite; a program needn't handle non-finite values.
Results may differ from a plain program's by a relative error of at most 0.0003.
Values sent between devices are 32-bit elements; how exact they have to be, the bound alone decides.
No kernel may reach another device: no remote copies, remote signals or barrier semaphores. Data moves between devices by JAX's collectives and lax.ppermute only.
A program may use at most 64 MiB of HBM per device.

v0:
```python
import math

import jax
import jax.numpy as jnp
from jax import lax
from jax.sharding import PartitionSpec as P

PB = 128
SB = 128
NANG = 64


def passed_along(value, axis, steps):
    count = lax.axis_size(axis)
    pairs = [(source, (source + steps) % count) for source in range(count)]
    return lax.ppermute(value, axis, pairs)


def precondition(preconditioner, map_field):
    first = (
        preconditioner[0] * map_field[0]
        + preconditioner[3] * map_field[1]
        + preconditioner[4] * map_field[2]
    )
    second = (
        preconditioner[3] * map_field[0]
        + preconditioner[1] * map_field[1]
        + preconditioner[5] * map_field[2]
    )
    third = (
        preconditioner[4] * map_field[0]
        + preconditioner[5] * map_field[1]
        + preconditioner[2] * map_field[2]
    )
    return jnp.stack([first, second, third])


def global_dot(partial_value):
    return lax.psum(partial_value, ("tm", "det"))


def on_device(
    solution,
    residual,
    direction,
    preconditioner,
    pull_index,
    block_slot,
    pixel_offset,
    angle_index,
    det_weight,
    mode_templates,
    mode_precision,
):
    highest = lax.Precision.HIGHEST
    requests = pull_index[0, 0]
    reach_count, group_count, cap_count = requests.shape
    slot_total = reach_count * group_count * cap_count
    det_dev, samp_dev = pixel_offset.shape
    blocks_per = samp_dev // SB
    batch_size = 4
    batches = det_dev // batch_size
    pixel_iota = lax.iota(jnp.int32, PB)
    slot_iota = lax.iota(jnp.int32, slot_total)
    reduced_old = jnp.sum(residual * precondition(preconditioner, residual))
    rz_old = global_dot(reduced_old)
    outgoing = jnp.take(direction, requests, axis=1)
    grouped = lax.all_to_all(outgoing, "det", split_axis=2, concat_axis=2, tiled=True)
    near_parts = [grouped[:, 0]]
    reach = 1
    near_parts.append(passed_along(grouped[:, reach], "tm", -reach))
    local_map = jnp.stack(near_parts, axis=1).reshape(3, slot_total, PB)
    angle_rad = angle_index.astype(jnp.float32) * (2.0 * math.pi / NANG)
    cos_batches = jnp.cos(angle_rad).reshape(batches, batch_size, blocks_per, SB)
    sin_batches = jnp.sin(angle_rad).reshape(batches, batch_size, blocks_per, SB)
    slot_batches = block_slot.reshape(batches, batch_size, blocks_per)
    offset_batches = pixel_offset.reshape(batches, batch_size, blocks_per, SB)

    def read_batch(pieces):
        slot_ids, offsets, cos_vals, sin_vals = pieces
        values = jnp.take(local_map, slot_ids, axis=1)
        onehot = (offsets[..., None] == pixel_iota).astype(jnp.float32)
        picked = jnp.einsum("dbsp,kdbp->kdbs", onehot, values, precision=highest)
        return picked[0] + cos_vals * picked[1] + sin_vals * picked[2]

    timeline = lax.map(
        read_batch, (slot_batches, offset_batches, cos_batches, sin_batches)
    ).reshape(det_dev, samp_dev)
    core_matrix = jnp.diag(mode_precision) + jnp.dot(
        mode_templates.T, det_weight[:, None] * mode_templates, precision=highest
    )
    factor = jnp.linalg.cholesky(core_matrix)
    first_row = lax.axis_index("det") * det_dev
    own_modes = lax.dynamic_slice_in_dim(mode_templates, first_row, det_dev, 0)
    own_weight = lax.dynamic_slice_in_dim(det_weight, first_row, det_dev, 0)
    local_proj = jnp.dot(own_modes.T, own_weight[:, None] * timeline, precision=highest)
    projection = lax.psum(local_proj, "det")
    mode_coef = jax.scipy.linalg.cho_solve((factor, True), projection)
    filtered = own_weight[:, None] * (timeline - jnp.dot(own_modes, mode_coef, precision=highest))
    filtered_batches = filtered.reshape(batches, batch_size, blocks_per, SB)

    def bin_batch(running, pieces):
        slot_ids, offsets, cos_vals, sin_vals, filtered_part = pieces
        onehot = (offsets[..., None] == pixel_iota).astype(jnp.float32)
        spread = jnp.stack([filtered_part, cos_vals * filtered_part, sin_vals * filtered_part])
        per_block = jnp.einsum("dbsp,kdbs->kdbp", onehot, spread, precision=highest)
        slot_onehot = (slot_ids[..., None] == slot_iota).astype(jnp.float32)
        return (
            running + jnp.einsum("dbn,kdbp->knp", slot_onehot, per_block, precision=highest),
            None,
        )

    partial_map, _ = lax.scan(
        bin_batch,
        jnp.zeros((3, slot_total, PB), jnp.float32),
        (slot_batches, offset_batches, cos_batches, sin_batches, filtered_batches),
    )
    partial_split = partial_map.reshape(3, reach_count, group_count, cap_count, PB)
    back_parts = [partial_split[:, 0]]
    reach = 1
    back_parts.append(passed_along(partial_split[:, reach], "tm", reach))
    returning = jnp.stack(back_parts, axis=1)
    arrived = lax.all_to_all(returning, "det", split_axis=2, concat_axis=2, tiled=True)
    operated = (
        jnp.zeros_like(direction)
        .at[:, requests.reshape(-1)]
        .add(arrived.reshape(3, slot_total, PB))
    )
    curvature = jnp.sum(direction * operated)
    curv_sum = global_dot(curvature)
    step_size = rz_old / curv_sum
    new_solution = solution + step_size * direction
    new_residual = residual - step_size * operated
    applied = precondition(preconditioner, new_residual)
    rz_new = global_dot(jnp.sum(new_residual * applied))
    new_direction = applied + rz_new / rz_old * direction
    return (new_solution, new_residual, new_direction)


def solution(mesh):
    in_specs = (
        P(None, ("tm", "det"), None),
        P(None, ("tm", "det"), None),
        P(None, ("tm", "det"), None),
        P(None, ("tm", "det"), None),
        P("tm", "det", None, None, None),
        P("det", "tm"),
        P("det", "tm"),
        P("det", "tm"),
        P(),
        P(),
        P(),
    )
    out_specs = (
        P(None, ("tm", "det"), None),
        P(None, ("tm", "det"), None),
        P(None, ("tm", "det"), None),
    )
    return jax.shard_map(
        on_device, mesh=mesh, in_specs=in_specs, out_specs=out_specs, check_vma=False
    )
```

profile of v0, /device:TPU:0, one launch (start us, length us, event | category | flops | bytes accessed | tf_op | source)
XLA Modules:
  0.0 824.3 jit_solution(5135217927251326295)
XLA Ops:
  11.4 4.2 all-to-all-start
  15.7 9.5 %sine_bitcast_fusion = (f32[8,8,64,128]{3,1,2,0:T(8,128)S(1)}, f32[8,8,64,128]{3,1,2,0:T(8,128)}) fusion(s32[64,8192]{1,0:T(8,128)} %param.22), kind=kLoop, calls=%fused_computation.49 | loop fusion | flops 1048576 | bytes 6291456
  36.2 5.4 collective-permute-start
  44.5 347.3 %while.24 = (s32[]{:T(128)}, f32[16,4,64,128]{3,2,1,0:T(8,128)S(1)}, s32[16,4,64]{2,1,0:T(4,128)}, f32[3,128,128]{2,0,1:T(4,128)S(1)}, s32[16,4,64,128]{3,2,1,0:...) while((s32[]{:T(128)}, f32[16,4,64,128]{3,2,1,0:T(8,128)S(1)}, ...), condition=%wide.region_3.4_spmd.clone, body=%wide.region_2.3_spmd.clone.sunk | while | flops 155421952 | bytes 3026537 | solution.py:86
  47.9 16.3 %fusion.69 = f32[3,4,64,128]{3,0,2,1:T(4,128)S(1)} fusion(s32[4,64,128]{2,1,0:T(8,128)S(1)} %dynamic-slice_bitcast_fusion.6, f32[4,64,3,128]{3,2,1,0:T(4,128)S(1)} %bitcast.141, pred[4,64]{1,0:T(4,128)(4,1)S(1)} %compare_and_fusion.3), kind=kOutput, calls=%fused_computation.8.clone.1 | convolution fusion | flops 155287552 | bytes 917760 | tf_op jit(solution)/shard_map/while/body/eval_jaxpr/dbsp,kdbp->kdbs/dot_general | solution.py:83
  69.6 16.3 %fusion.69 = f32[3,4,64,128]{3,0,2,1:T(4,128)S(1)} fusion(s32[4,64,128]{2,1,0:T(8,128)S(1)} %dynamic-slice_bitcast_fusion.6, f32[4,64,3,128]{3,2,1,0:T(4,128)S(1)} %bitcast.141, pred[4,64]{1,0:T(4,128)(4,1)S(1)} %compare_and_fusion.3), kind=kOutput, calls=%fused_computation.8.clone.1 | convolution fusion | flops 155287552 | bytes 917760 | tf_op jit(solution)/shard_map/while/body/eval_jaxpr/dbsp,kdbp->kdbs/dot_general | solution.py:83
  91.3 16.3 %fusion.69 = f32[3,4,64,128]{3,0,2,1:T(4,128)S(1)} fusion(s32[4,64,128]{2,1,0:T(8,128)S(1)} %dynamic-slice_bitcast_fusion.6, f32[4,64,3,128]{3,2,1,0:T(4,128)S(1)} %bitcast.141, pred[4,64]{1,0:T(4,128)(4,1)S(1)} %compare_and_fusion.3), kind=kOutput, calls=%fused_computation.8.clone.1 | convolution fusion | flops 155287552 | bytes 917760 | tf_op jit(solution)/shard_map/while/body/eval_jaxpr/dbsp,kdbp->kdbs/dot_general | solution.py:83
  113.0 16.3 %fusion.69 = f32[3,4,64,128]{3,0,2,1:T(4,128)S(1)} fusion(s32[4,64,128]{2,1,0:T(8,128)S(1)} %dynamic-slice_bitcast_fusion.6, f32[4,64,3,128]{3,2,1,0:T(4,128)S(1)} %bitcast.141, pred[4,64]{1,0:T(4,128)(4,1)S(1)} %compare_and_fusion.3), kind=kOutput, calls=%fused_computation.8.clone.1 | convolution fusion | flops 155287552 | bytes 917760 | tf_op jit(solution)/shard_map/while/body/eval_jaxpr/dbsp,kdbp->kdbs/dot_general | solution.py:83
  134.7 16.3 %fusion.69 = f32[3,4,64,128]{3,0,2,1:T(4,128)S(1)} fusion(s32[4,64,128]{2,1,0:T(8,128)S(1)} %dynamic-slice_bitcast_fusion.6, f32[4,64,3,128]{3,2,1,0:T(4,128)S(1)} %bitcast.141, pred[4,64]{1,0:T(4,128)(4,1)S(1)} %compare_and_fusion.3), kind=kOutput, calls=%fused_computation.8.clone.1 | convolution fusion | flops 155287552 | bytes 917760 | tf_op jit(solution)/shard_map/while/body/eval_jaxpr/dbsp,kdbp->kdbs/dot_general | solution.py:83
  156.4 16.3 %fusion.69 = f32[3,4,64,128]{3,0,2,1:T(4,128)S(1)} fusion(s32[4,64,128]{2,1,0:T(8,128)S(1)} %dynamic-slice_bitcast_fusion.6, f32[4,64,3,128]{3,2,1,0:T(4,128)S(1)} %bitcast.141, pred[4,64]{1,0:T(4,128)(4,1)S(1)} %compare_and_fusion.3), kind=kOutput, calls=%fused_computation.8.clone.1 | convolution fusion | flops 155287552 | bytes 917760 | tf_op jit(solution)/shard_map/while/body/eval_jaxpr/dbsp,kdbp->kdbs/dot_general | solution.py:83
  178.1 16.3 %fusion.69 = f32[3,4,64,128]{3,0,2,1:T(4,128)S(1)} fusion(s32[4,64,128]{2,1,0:T(8,128)S(1)} %dynamic-slice_bitcast_fusion.6, f32[4,64,3,128]{3,2,1,0:T(4,128)S(1)} %bitcast.141, pred[4,64]{1,0:T(4,128)(4,1)S(1)} %compare_and_fusion.3), kind=kOutput, calls=%fused_computation.8.clone.1 | convolution fusion | flops 155287552 | bytes 917760 | tf_op jit(solution)/shard_map/while/body/eval_jaxpr/dbsp,kdbp->kdbs/dot_general | solution.py:83
  199.8 16.3 %fusion.69 = f32[3,4,64,128]{3,0,2,1:T(4,128)S(1)} fusion(s32[4,64,128]{2,1,0:T(8,128)S(1)} %dynamic-slice_bitcast_fusion.6, f32[4,64,3,128]{3,2,1,0:T(4,128)S(1)} %bitcast.141, pred[4,64]{1,0:T(4,128)(4,1)S(1)} %compare_and_fusion.3), kind=kOutput, calls=%fused_computation.8.clone.1 | convolution fusion | flops 155287552 | bytes 917760 | tf_op jit(solution)/shard_map/while/body/eval_jaxpr/dbsp,kdbp->kdbs/dot_general | solution.py:83
  221.5 16.3 %fusion.69 = f32[3,4,64,128]{3,0,2,1:T(4,128)S(1)} fusion(s32[4,64,128]{2,1,0:T(8,128)S(1)} %dynamic-slice_bitcast_fusion.6, f32[4,64,3,128]{3,2,1,0:T(4,128)S(1)} %bitcast.141, pred[4,64]{1,0:T(4,128)(4,1)S(1)} %compare_and_fusion.3), kind=kOutput, calls=%fused_computation.8.clone.1 | convolution fusion | flops 155287552 | bytes 917760 | tf_op jit(solution)/shard_map/while/body/eval_jaxpr/dbsp,kdbp->kdbs/dot_general | solution.py:83
  243.2 16.3 %fusion.69 = f32[3,4,64,128]{3,0,2,1:T(4,128)S(1)} fusion(s32[4,64,128]{2,1,0:T(8,128)S(1)} %dynamic-slice_bitcast_fusion.6, f32[4,64,3,128]{3,2,1,0:T(4,128)S(1)} %bitcast.141, pred[4,64]{1,0:T(4,128)(4,1)S(1)} %compare_and_fusion.3), kind=kOutput, calls=%fused_computation.8.clone.1 | convolution fusion | flops 155287552 | bytes 917760 | tf_op jit(solution)/shard_map/while/body/eval_jaxpr/dbsp,kdbp->kdbs/dot_general | solution.py:83
  264.9 16.3 %fusion.69 = f32[3,4,64,128]{3,0,2,1:T(4,128)S(1)} fusion(s32[4,64,128]{2,1,0:T(8,128)S(1)} %dynamic-slice_bitcast_fusion.6, f32[4,64,3,128]{3,2,1,0:T(4,128)S(1)} %bitcast.141, pred[4,64]{1,0:T(4,128)(4,1)S(1)} %compare_and_fusion.3), kind=kOutput, calls=%fused_computation.8.clone.1 | convolution fusion | flops 155287552 | bytes 917760 | tf_op jit(solution)/shard_map/while/body/eval_jaxpr/dbsp,kdbp->kdbs/dot_general | solution.py:83
  286.6 16.3 %fusion.69 = f32[3,4,64,128]{3,0,2,1:T(4,128)S(1)} fusion(s32[4,64,128]{2,1,0:T(8,128)S(1)} %dynamic-slice_bitcast_fusion.6, f32[4,64,3,128]{3,2,1,0:T(4,128)S(1)} %bitcast.141, pred[4,64]{1,0:T(4,128)(4,1)S(1)} %compare_and_fusion.3), kind=kOutput, calls=%fused_computation.8.clone.1 | convolution fusion | flops 155287552 | bytes 917760 | tf_op jit(solution)/shard_map/while/body/eval_jaxpr/dbsp,kdbp->kdbs/dot_general | solution.py:83
  308.3 16.3 %fusion.69 = f32[3,4,64,128]{3,0,2,1:T(4,128)S(1)} fusion(s32[4,64,128]{2,1,0:T(8,128)S(1)} %dynamic-slice_bitcast_fusion.6, f32[4,64,3,128]{3,2,1,0:T(4,128)S(1)} %bitcast.141, pred[4,64]{1,0:T(4,128)(4,1)S(1)} %compare_and_fusion.3), kind=kOutput, calls=%fused_computation.8.clone.1 | convolution fusion | flops 155287552 | bytes 917760 | tf_op jit(solution)/shard_map/while/body/eval_jaxpr/dbsp,kdbp->kdbs/dot_general | solution.py:83
  330.0 16.3 %fusion.69 = f32[3,4,64,128]{3,0,2,1:T(4,128)S(1)} fusion(s32[4,64,128]{2,1,0:T(8,128)S(1)} %dynamic-slice_bitcast_fusion.6, f32[4,64,3,128]{3,2,1,0:T(4,128)S(1)} %bitcast.141, pred[4,64]{1,0:T(4,128)(4,1)S(1)} %compare_and_fusion.3), kind=kOutput, calls=%fused_computation.8.clone.1 | convolution fusion | flops 155287552 | bytes 917760 | tf_op jit(solution)/shard_map/while/body/eval_jaxpr/dbsp,kdbp->kdbs/dot_general | solution.py:83
  351.7 16.3 %fusion.69 = f32[3,4,64,128]{3,0,2,1:T(4,128)S(1)} fusion(s32[4,64,128]{2,1,0:T(8,128)S(1)} %dynamic-slice_bitcast_fusion.6, f32[4,64,3,128]{3,2,1,0:T(4,128)S(1)} %bitcast.141, pred[4,64]{1,0:T(4,128)(4,1)S(1)} %compare_and_fusion.3), kind=kOutput, calls=%fused_computation.8.clone.1 | convolution fusion | flops 155287552 | bytes 917760 | tf_op jit(solution)/shard_map/while/body/eval_jaxpr/dbsp,kdbp->kdbs/dot_general | solution.py:83
  373.4 16.3 %fusion.69 = f32[3,4,64,128]{3,0,2,1:T(4,128)S(1)} fusion(s32[4,64,128]{2,1,0:T(8,128)S(1)} %dynamic-slice_bitcast_fusion.6, f32[4,64,3,128]{3,2,1,0:T(4,128)S(1)} %bitcast.141, pred[4,64]{1,0:T(4,128)(4,1)S(1)} %compare_and_fusion.3), kind=kOutput, calls=%fused_computation.8.clone.1 | convolution fusion | flops 155287552 | bytes 917760 | tf_op jit(solution)/shard_map/while/body/eval_jaxpr/dbsp,kdbp->kdbs/dot_general | solution.py:83
  391.7 3.0 fusion.29
  398.9 31.3 %all-reduce.3.cloned.1.call-done = f32[16,8192]{1,0:T(8,128)} async-done(((f32[16,8192]{1,0:T(8,128)}), f32[16,8192]{1,0:T(8,128)}) %all-reduce.3.cloned.1.call-update) | async-done | bytes 524304 | tf_op jit(solution)/shard_map/psum | solution.py:97
  432.4 3.0 fusion.31
  437.2 267.2 %while.25 = (s32[]{:T(128)}, f32[3,128,128]{1,2,0:T(8,128)S(1)}, f32[16,4,64,128]{3,2,1,0:T(8,128)}, f32[16,4,64,128]{3,0,2,1:T(8,128)}, f32[16,4,64,128]{3,0,2,...) while((s32[]{:T(128)}, f32[3,128,128]{1,2,0:T(8,128)S(1)}, ...), condition=%wide.region_8.9_spmd.clone.clone, body=%wide.region_7.8_spmd.clone.clone.sunk | while | flops 306577408 | bytes 2886775 | solution.py:113
  440.9 11.8 %fusion.74 = f32[3,4,64,128]{3,0,2,1:T(4,128)S(1)} fusion(s32[4,64,128]{2,1,0:T(8,128)S(1)} %dynamic-slice_bitcast_fusion.7, f32[1,4,64,128]{3,0,2,1:T(1,128)S(1)} %get-tuple-element.399, f32[1,4,64,128]{3,0,2,1:T(1,128)S(1)} %get-tuple-element.400, f32[1,4,64,128]{3,0,2,1:T(1,128)S(1)} %bitcast.135), kind=kOutput, calls=%fused_computation.27.clone.1 | convolution fusion | flops 155385856 | bytes 917504 | tf_op jit(solution)/shard_map/while/body/eval_jaxpr/dbsp,kdbs->kdbp/dot_general | solution.py:106
  457.6 11.8 %fusion.74 = f32[3,4,64,128]{3,0,2,1:T(4,128)S(1)} fusion(s32[4,64,128]{2,1,0:T(8,128)S(1)} %dynamic-slice_bitcast_fusion.7, f32[1,4,64,128]{3,0,2,1:T(1,128)S(1)} %get-tuple-element.399, f32[1,4,64,128]{3,0,2,1:T(1,128)S(1)} %get-tuple-element.400, f32[1,4,64,128]{3,0,2,1:T(1,128)S(1)} %bitcast.135), kind=kOutput, calls=%fused_computation.27.clone.1 | convolution fusion | flops 155385856 | bytes 917504 | tf_op jit(solution)/shard_map/while/body/eval_jaxpr/dbsp,kdbs->kdbp/dot_general | solution.py:106
  474.3 11.8 %fusion.74 = f32[3,4,64,128]{3,0,2,1:T(4,128)S(1)} fusion(s32[4,64,128]{2,1,0:T(8,128)S(1)} %dynamic-slice_bitcast_fusion.7, f32[1,4,64,128]{3,0,2,1:T(1,128)S(1)} %get-tuple-element.399, f32[1,4,64,128]{3,0,2,1:T(1,128)S(1)} %get-tuple-element.400, f32[1,4,64,128]{3,0,2,1:T(1,128)S(1)} %bitcast.135), kind=kOutput, calls=%fused_computation.27.clone.1 | convolution fusion | flops 155385856 | bytes 917504 | tf_op jit(solution)/shard_map/while/body/eval_jaxpr/dbsp,kdbs->kdbp/dot_general | solution.py:106
  491.0 11.8 %fusion.74 = f32[3,4,64,128]{3,0,2,1:T(4,128)S(1)} fusion(s32[4,64,128]{2,1,0:T(8,128)S(1)} %dynamic-slice_bitcast_fusion.7, f32[1,4,64,128]{3,0,2,1:T(1,128)S(1)} %get-tuple-element.399, f32[1,4,64,128]{3,0,2,1:T(1,128)S(1)} %get-tuple-element.400, f32[1,4,64,128]{3,0,2,1:T(1,128)S(1)} %bitcast.135), kind=kOutput, calls=%fused_computation.27.clone.1 | convolution fusion | flops 155385856 | bytes 917504 | tf_op jit(solution)/shard_map/while/body/eval_jaxpr/dbsp,kdbs->kdbp/dot_general | solution.py:106
  507.7 11.8 %fusion.74 = f32[3,4,64,128]{3,0,2,1:T(4,128)S(1)} fusion(s32[4,64,128]{2,1,0:T(8,128)S(1)} %dynamic-slice_bitcast_fusion.7, f32[1,4,64,128]{3,0,2,1:T(1,128)S(1)} %get-tuple-element.399, f32[1,4,64,128]{3,0,2,1:T(1,128)S(1)} %get-tuple-element.400, f32[1,4,64,128]{3,0,2,1:T(1,128)S(1)} %bitcast.135), kind=kOutput, calls=%fused_computation.27.clone.1 | convolution fusion | flops 155385856 | bytes 917504 | tf_op jit(solution)/shard_map/while/body/eval_jaxpr/dbsp,kdbs->kdbp/dot_general | solution.py:106
  524.4 11.8 %fusion.74 = f32[3,4,64,128]{3,0,2,1:T(4,128)S(1)} fusion(s32[4,64,128]{2,1,0:T(8,128)S(1)} %dynamic-slice_bitcast_fusion.7, f32[1,4,64,128]{3,0,2,1:T(1,128)S(1)} %get-tuple-element.399, f32[1,4,64,128]{3,0,2,1:T(1,128)S(1)} %get-tuple-element.400, f32[1,4,64,128]{3,0,2,1:T(1,128)S(1)} %bitcast.135), kind=kOutput, calls=%fused_computation.27.clone.1 | convolution fusion | flops 155385856 | bytes 917504 | tf_op jit(solution)/shard_map/while/body/eval_jaxpr/dbsp,kdbs->kdbp/dot_general | solution.py:106
  541.1 11.8 %fusion.74 = f32[3,4,64,128]{3,0,2,1:T(4,128)S(1)} fusion(s32[4,64,128]{2,1,0:T(8,128)S(1)} %dynamic-slice_bitcast_fusion.7, f32[1,4,64,128]{3,0,2,1:T(1,128)S(1)} %get-tuple-element.399, f32[1,4,64,128]{3,0,2,1:T(1,128)S(1)} %get-tuple-element.400, f32[1,4,64,128]{3,0,2,1:T(1,128)S(1)} %bitcast.135), kind=kOutput, calls=%fused_computation.27.clone.1 | convolution fusion | flops 155385856 | bytes 917504 | tf_op jit(solution)/shard_map/while/body/eval_jaxpr/dbsp,kdbs->kdbp/dot_general | solution.py:106
  557.8 11.8 %fusion.74 = f32[3,4,64,128]{3,0,2,1:T(4,128)S(1)} fusion(s32[4,64,128]{2,1,0:T(8,128)S(1)} %dynamic-slice_bitcast_fusion.7, f32[1,4,64,128]{3,0,2,1:T(1,128)S(1)} %get-tuple-element.399, f32[1,4,64,128]{3,0,2,1:T(1,128)S(1)} %get-tuple-element.400, f32[1,4,64,128]{3,0,2,1:T(1,128)S(1)} %bitcast.135), kind=kOutput, calls=%fused_computation.27.clone.1 | convolution fusion | flops 155385856 | bytes 917504 | tf_op jit(solution)/shard_map/while/body/eval_jaxpr/dbsp,kdbs->kdbp/dot_general | solution.py:106
  574.5 11.8 %fusion.74 = f32[3,4,64,128]{3,0,2,1:T(4,128)S(1)} fusion(s32[4,64,128]{2,1,0:T(8,128)S(1)} %dynamic-slice_bitcast_fusion.7, f32[1,4,64,128]{3,0,2,1:T(1,128)S(1)} %get-tuple-element.399, f32[1,4,64,128]{3,0,2,1:T(1,128)S(1)} %get-tuple-element.400, f32[1,4,64,128]{3,0,2,1:T(1,128)S(1)} %bitcast.135), kind=kOutput, calls=%fused_computation.27.clone.1 | convolution fusion | flops 155385856 | bytes 917504 | tf_op jit(solution)/shard_map/while/body/eval_jaxpr/dbsp,kdbs->kdbp/dot_general | solution.py:106
  591.1 11.8 %fusion.74 = f32[3,4,64,128]{3,0,2,1:T(4,128)S(1)} fusion(s32[4,64,128]{2,1,0:T(8,128)S(1)} %dynamic-slice_bitcast_fusion.7, f32[1,4,64,128]{3,0,2,1:T(1,128)S(1)} %get-tuple-element.399, f32[1,4,64,128]{3,0,2,1:T(1,128)S(1)} %get-tuple-element.400, f32[1,4,64,128]{3,0,2,1:T(1,128)S(1)} %bitcast.135), kind=kOutput, calls=%fused_computation.27.clone.1 | convolution fusion | flops 155385856 | bytes 917504 | tf_op jit(solution)/shard_map/while/body/eval_jaxpr/dbsp,kdbs->kdbp/dot_general | solution.py:106
  607.8 11.8 %fusion.74 = f32[3,4,64,128]{3,0,2,1:T(4,128)S(1)} fusion(s32[4,64,128]{2,1,0:T(8,128)S(1)} %dynamic-slice_bitcast_fusion.7, f32[1,4,64,128]{3,0,2,1:T(1,128)S(1)} %get-tuple-element.399, f32[1,4,64,128]{3,0,2,1:T(1,128)S(1)} %get-tuple-element.400, f32[1,4,64,128]{3,0,2,1:T(1,128)S(1)} %bitcast.135), kind=kOutput, calls=%fused_computation.27.clone.1 | convolution fusion | flops 155385856 | bytes 917504 | tf_op jit(solution)/shard_map/while/body/eval_jaxpr/dbsp,kdbs->kdbp/dot_general | solution.py:106
  624.5 11.8 %fusion.74 = f32[3,4,64,128]{3,0,2,1:T(4,128)S(1)} fusion(s32[4,64,128]{2,1,0:T(8,128)S(1)} %dynamic-slice_bitcast_fusion.7, f32[1,4,64,128]{3,0,2,1:T(1,128)S(1)} %get-tuple-element.399, f32[1,4,64,128]{3,0,2,1:T(1,128)S(1)} %get-tuple-element.400, f32[1,4,64,128]{3,0,2,1:T(1,128)S(1)} %bitcast.135), kind=kOutput, calls=%fused_computation.27.clone.1 | convolution fusion | flops 155385856 | bytes 917504 | tf_op jit(solution)/shard_map/while/body/eval_jaxpr/dbsp,kdbs->kdbp/dot_general | solution.py:106
  641.2 11.8 %fusion.74 = f32[3,4,64,128]{3,0,2,1:T(4,128)S(1)} fusion(s32[4,64,128]{2,1,0:T(8,128)S(1)} %dynamic-slice_bitcast_fusion.7, f32[1,4,64,128]{3,0,2,1:T(1,128)S(1)} %get-tuple-element.399, f32[1,4,64,128]{3,0,2,1:T(1,128)S(1)} %get-tuple-element.400, f32[1,4,64,128]{3,0,2,1:T(1,128)S(1)} %bitcast.135), kind=kOutput, calls=%fused_computation.27.clone.1 | convolution fusion | flops 155385856 | bytes 917504 | tf_op jit(solution)/shard_map/while/body/eval_jaxpr/dbsp,kdbs->kdbp/dot_general | solution.py:106
  657.9 11.8 %fusion.74 = f32[3,4,64,128]{3,0,2,1:T(4,128)S(1)} fusion(s32[4,64,128]{2,1,0:T(8,128)S(1)} %dynamic-slice_bitcast_fusion.7, f32[1,4,64,128]{3,0,2,1:T(1,128)S(1)} %get-tuple-element.399, f32[1,4,64,128]{3,0,2,1:T(1,128)S(1)} %get-tuple-element.400, f32[1,4,64,128]{3,0,2,1:T(1,128)S(1)} %bitcast.135), kind=kOutput, calls=%fused_computation.27.clone.1 | convolution fusion | flops 155385856 | bytes 917504 | tf_op jit(solution)/shard_map/while/body/eval_jaxpr/dbsp,kdbs->kdbp/dot_general | solution.py:106
  674.6 11.8 %fusion.74 = f32[3,4,64,128]{3,0,2,1:T(4,128)S(1)} fusion(s32[4,64,128]{2,1,0:T(8,128)S(1)} %dynamic-slice_bitcast_fusion.7, f32[1,4,64,128]{3,0,2,1:T(1,128)S(1)} %get-tuple-element.399, f32[1,4,64,128]{3,0,2,1:T(1,128)S(1)} %get-tuple-element.400, f32[1,4,64,128]{3,0,2,1:T(1,128)S(1)} %bitcast.135), kind=kOutput, calls=%fused_computation.27.clone.1 | convolution fusion | flops 155385856 | bytes 917504 | tf_op jit(solution)/shard_map/while/body/eval_jaxpr/dbsp,kdbs->kdbp/dot_general | solution.py:106
  691.3 11.8 %fusion.74 = f32[3,4,64,128]{3,0,2,1:T(4,128)S(1)} fusion(s32[4,64,128]{2,1,0:T(8,128)S(1)} %dynamic-slice_bitcast_fusion.7, f32[1,4,64,128]{3,0,2,1:T(1,128)S(1)} %get-tuple-element.399, f32[1,4,64,128]{3,0,2,1:T(1,128)S(1)} %get-tuple-element.400, f32[1,4,64,128]{3,0,2,1:T(1,128)S(1)} %bitcast.135), kind=kOutput, calls=%fused_computation.27.clone.1 | convolution fusion | flops 155385856 | bytes 917504 | tf_op jit(solution)/shard_map/while/body/eval_jaxpr/dbsp,kdbs->kdbp/dot_general | solution.py:106
  706.1 2.7 multiply_add_fusion.5
  708.8 3.1 collective-permute-done.1
  712.6 3.6 all-to-all-start.1
  716.2 5.1 all-to-all-done.1
  721.6 4.9 scatter_fusion
  726.6 2.8 fusion.33
  729.4 37.8 %all-reduce = (f32[]{:T(128)}, f32[]{:T(128)}) all-reduce(f32[]{:T(128)} %get-tuple-element.310, f32[]{:T(128)} %get-tuple-element.309), channel_id=1, replica_groups=mesh['tm'=8,'det'=4] {'tm','det'}, use_global_device_ids=true, to_apply=%region_1.0 | all-reduce | flops 2 | bytes 16 | tf_op jit(solution)/shard_map/psum | solution.py:39
  772.2 40.9 %psum.31 = f32[]{:T(128)} all-reduce(f32[]{:T(128)} %multiply_reduce_fusion), channel_id=1, replica_groups=mesh['tm'=8,'det'=4] {'tm','det'}, use_global_device_ids=true, to_apply=%region_13.14 | all-reduce | flops 1 | bytes 8 | tf_op jit(solution)/shard_map/psum | solution.py:39
  (289 shorter events, 199.5 us)
Async XLA Ops:
  11.4 24.8 %all-to-all-start = ((f32[3,2,4,16,128]{4,3,1,0,2:T(8,128)}), f32[3,2,4,16,128]{4,3,1,0,2:T(8,128)S(1)}, u32[]{:S(2)}, u32[]{:S(2)}) async-start(f32[3,2,4,16,128]{4,3,1,0,2:T(8,128)} %fusion.37), calls=%async_computation | async-start | bytes 393216 | tf_op jit(solution)/shard_map/all_to_all | solution.py:68
  15.6 9.6 %copy-start.10 = (f32[256,16]{0,1:T(8,128)S(1)}, f32[256,16]{0,1:T(8,128)}, u32[]{:S(2)}) copy-start(f32[256,16]{0,1:T(8,128)} %param.24) | copy-start | bytes 49156
  15.6 9.6 %copy-start.13 = (f32[256]{0:T(256)S(1)}, f32[256]{0:T(256)}, u32[]{:S(2)}) copy-start(f32[256]{0:T(256)} %param.23) | copy-start | bytes 3076
  15.6 9.8 %copy-start.12 = (f32[16]{0:T(128)S(1)}, f32[16]{0:T(128)}, u32[]{:S(2)}) copy-start(f32[16]{0:T(128)} %param.25) | copy-start | bytes 196
  15.6 414.6 %all-reduce.3.cloned.1.call-start = ((), (), s32[]{:S(2)}) async-start(), calls=%async_computation.2 | async-start | bytes 1048576 | tf_op jit(solution)/shard_map/psum | solution.py:97
  30.3 2.6 copy-start.4
  32.9 11.6 %copy-start.1 = (f32[16,4,64,128]{3,2,1,0:T(8,128)S(1)}, f32[16,4,64,128]{3,2,1,0:T(8,128)}, u32[]{:S(2)}) copy-start(f32[16,4,64,128]{3,2,1,0:T(8,128)} %custom-call.16) | copy-start | bytes 6291460
  36.2 8.1 collective-permute-start
  391.7 5.0 copy-start.2
  396.7 1.4 copy-start.8
  437.2 268.9 %copy-start.3 = (f32[3,384,128]{2,0,1:T(4,128)S(1)}, f32[3,384,128]{2,0,1:T(4,128)}, u32[]{:S(2)}) copy-start(f32[3,384,128]{2,0,1:T(4,128)} %copy.171) | copy-start | bytes 1769476
  437.2 268.9 %copy-start.5 = (f32[1,384,128]{2,1,0:T(8,128)S(1)}, f32[1,384,128]{2,1,0:T(8,128)}, u32[]{:S(2)}) copy-start(f32[1,384,128]{2,1,0:T(8,128)} %get-tuple-element.294) | copy-start | bytes 589828
  704.4 4.4 copy-start.11
  704.6 7.4 collective-permute-start.1
  708.8 17.8 %copy-start = (f32[3,384,128]{2,1,0:T(8,128)S(1)}, f32[3,384,128]{2,1,0:T(8,128)}, u32[]{:S(2)}) copy-start(f32[3,384,128]{2,1,0:T(8,128)} %param.17) | copy-start | bytes 1769476
  712.6 8.7 %all-to-all-start.1 = ((f32[3,2,4,16,128]{4,3,0,1,2:T(8,128)}), f32[3,2,4,16,128]{4,3,0,1,2:T(8,128)S(1)}, u32[]{:S(2)}, u32[]{:S(2)}) async-start(f32[3,2,4,16,128]{4,3,0,1,2:T(8,128)} %copy.186), calls=%async_computation.1 | async-start | bytes 393216 | tf_op jit(solution)/shard_map/all_to_all | solution.py:123
  726.5 42.5 %copy-start.6 = (f32[1,384,128]{2,1,0:T(8,128)S(1)}, f32[1,384,128]{2,1,0:T(8,128)}, u32[]{:S(2)}) copy-start(f32[1,384,128]{2,1,0:T(8,128)} %get-tuple-element.295) | copy-start | bytes 589828
  726.5 42.5 %copy-start.7 = (f32[1,384,128]{2,1,0:T(8,128)S(1)}, f32[1,384,128]{2,1,0:T(8,128)}, u32[]{:S(2)}) copy-start(f32[1,384,128]{2,1,0:T(8,128)} %get-tuple-element.296) | copy-start | bytes 589828
  769.1 45.4 %copy-start.9 = (f32[3,384,128]{2,1,0:T(8,128)S(1)}, f32[3,384,128]{2,1,0:T(8,128)}, u32[]{:S(2)}) copy-start(f32[3,384,128]{2,1,0:T(8,128)} %param.15) | copy-start | bytes 1769476
Sparse Core Ops, SparseCore 0:
  394.9 35.1 all-reduce.2
where the time goes:
time: 828 us; the launch traced here: 824 us
  matrix products  467 us (56%)
  other arithmetic  112 us (14%)
  local copies, waits for them, and re-layouts  91.8 us (11%)
  blocking collectives  78.7 us (10%)
  waiting for transfers between devices  41.5 us (5%)
  between operations  17.1 us (2%)
  starting transfers between devices  14.8 us (2%)
    dot_general x16, matrix products, read_batch(): picked = jnp.einsum('dbsp,kdbp->kdbs', onehot, values, precision=highest)  261 us
    dot_general x16, matrix products, bin_batch(): per_block = jnp.einsum('dbsp,kdbs->kdbp', onehot, spread, precision=highest)  188 us
    psum x2, blocking collectives, global_dot(): return lax.psum(partial_value, ('tm', 'det'))  78.7 us
    add x16, other arithmetic, read_batch(): return picked[0] + cos_vals * picked[1] + sin_vals * picked[2]  31.6 us
    psum x1, waiting for transfers between devices, on_device(): projection = lax.psum(local_proj, 'det')  31.3 us
    mul x16, other arithmetic, bin_batch(): cos_vals * filtered_part  28.5 us
  transfers between devices with their start and end apart: 5, of which 4 were waited for; matrix products, arithmetic and copies ran while one was open for 3% of the time, Pallas kernels for 0%

commit v1 on v0

v1 whole, which is shorter than its diff:
```python
import functools
import math

import jax
import jax.numpy as jnp
from jax import lax
from jax.experimental import pallas as pl
from jax.experimental.pallas import tpu as pltpu
from jax.sharding import PartitionSpec as P

PB = 128
SB = 128
RUN = 4
NANG = 64
GROUP = 8
RUN_LEN = RUN * SB
ROWS = 8
LOW = 32
HIGH = PB // LOW
F32 = jnp.float32
BF16 = jnp.bfloat16
HIGHEST = lax.Precision.HIGHEST
VMEM_LIMIT = 48 * 1024 * 1024


def vmem_spec():
    return pl.BlockSpec(memory_space=pltpu.VMEM)


def smem_spec():
    return pl.BlockSpec(memory_space=pltpu.SMEM)


def params():
    return pltpu.CompilerParams(vmem_limit_bytes=VMEM_LIMIT)


def lane_pick(table, index):
    return jnp.take_along_axis(table, index, axis=1, mode="promise_in_bounds")


def wide_pick(table, index):
    parts = [
        lane_pick(table, index[:, PB * part : PB * (part + 1)])
        for part in range(index.shape[1] // PB)
    ]
    return jnp.concatenate(parts, axis=1)


def precondition(pre, field):
    return (
        pre[0] * field[0] + pre[3] * field[1] + pre[4] * field[2],
        pre[3] * field[0] + pre[1] * field[1] + pre[5] * field[2],
        pre[4] * field[0] + pre[5] * field[1] + pre[2] * field[2],
    )


def pull_kernel(request_ref, direction_ref, piece_ref):
    reach_count, group_count, cap_count = request_ref.shape
    for reach in range(reach_count):
        for group in range(group_count):
            for slot in range(cap_count):
                block = request_ref[reach, group, slot]
                for k in range(3):
                    piece_ref[reach, group, pl.ds(k * cap_count + slot, 1), :] = direction_ref[
                        k, pl.ds(block, 1), :
                    ]


def pull_blocks(requests, direction):
    reach_count, group_count, cap_count = requests.shape
    return pl.pallas_call(
        pull_kernel,
        out_shape=jax.ShapeDtypeStruct((reach_count, group_count, 3 * cap_count, PB), F32),
        in_specs=[smem_spec(), vmem_spec()],
        out_specs=vmem_spec(),
        compiler_params=params(),
        name="pull_blocks",
    )(requests, direction)


def timeline_kernel(
    slot_ref, near_ref, far_ref, trig_ref, weighted_ref, offset_ref, angle_ref, time_ref, proj_ref, map_ref, table_ref
):
    step = pl.program_id(0)
    cap_count = near_ref.shape[1] // 3
    group_count = near_ref.shape[0]
    det_count, chunk = offset_ref.shape
    runs = chunk // RUN_LEN

    @pl.when(step == 0)
    def _():
        for reach, ref in enumerate((near_ref, far_ref)):
            for group in range(group_count):
                first = (reach * group_count + group) * cap_count * ROWS
                for k in range(3):
                    map_ref[pl.ds(first + k, cap_count, stride=ROWS), :] = ref[
                        group, pl.ds(k * cap_count, cap_count), :
                    ]

    trig = trig_ref[...]

    def body(group, carry):
        first = pl.multiple_of(group * GROUP, GROUP)
        for run in range(runs):
            for det in range(GROUP):
                slot = slot_ref[first + det, (step * runs + run) * RUN]
                table_ref[run, pl.ds(det * ROWS, ROWS), :] = map_ref[
                    pl.ds(pl.multiple_of(slot * ROWS, ROWS), ROWS), :
                ]
            tables = [table_ref[run, pl.ds(k, GROUP, stride=ROWS), :] for k in range(3)]
            for part in range(RUN):
                lanes = pl.ds(run * RUN_LEN + part * SB, SB)
                offset = offset_ref[pl.ds(first, GROUP), lanes]
                angle = angle_ref[pl.ds(first, GROUP), lanes]
                cos_vals = lane_pick(trig, angle)
                sin_vals = lane_pick(trig, angle + NANG)
                time_ref[pl.ds(first, GROUP), lanes] = (
                    lane_pick(tables[0], offset)
                    + cos_vals * lane_pick(tables[1], offset)
                    + sin_vals * lane_pick(tables[2], offset)
                )
        return carry

    lax.fori_loop(0, det_count // GROUP, body, 0, unroll=2)
    proj_ref[...] = jnp.dot(
        weighted_ref[...], time_ref[...], precision=HIGHEST, preferred_element_type=F32
    )


def make_timeline(block_slot, near, far, trig, weighted, pixel_offset, angle_index, chunk):
    det_dev, samp_dev = pixel_offset.shape
    modes = weighted.shape[0]
    slot_total = 2 * near.shape[0] * (near.shape[1] // 3)
    runs = chunk // RUN_LEN
    wide = pl.BlockSpec((det_dev, chunk), lambda i: (0, i))
    return pl.pallas_call(
        timeline_kernel,
        grid=(samp_dev // chunk,),
        out_shape=(
            jax.ShapeDtypeStruct((det_dev, samp_dev), F32),
            jax.ShapeDtypeStruct((modes, samp_dev), F32),
        ),
        in_specs=[smem_spec()] + [vmem_spec()] * 4 + [wide, wide],
        out_specs=(wide, pl.BlockSpec((modes, chunk), lambda i: (0, i))),
        scratch_shapes=[
            pltpu.VMEM((slot_total * ROWS, PB), F32),
            pltpu.VMEM((runs, GROUP * ROWS, PB), F32),
        ],
        compiler_params=params(),
        name="make_timeline",
    )(block_slot, near, far, trig, weighted, pixel_offset, angle_index)


def bin_kernel(
    slot_ref, proj_ref, trig_ref, back_ref, weight_ref, offset_ref, angle_ref, time_ref, piece_ref, map_ref, row_ref, filt_ref
):
    step = pl.program_id(0)
    reach_count, group_count, rows, _ = piece_ref.shape
    cap_count = rows // 3
    det_count, chunk = offset_ref.shape
    runs = chunk // RUN_LEN

    @pl.when(step == 0)
    def _():
        map_ref[...] = jnp.zeros_like(map_ref)
        row_ref[...] = jnp.zeros_like(row_ref)

    common = jnp.dot(back_ref[...], proj_ref[...], precision=HIGHEST, preferred_element_type=F32)
    filt_ref[...] = weight_ref[...] * (time_ref[...] - common)
    trig = trig_ref[...]
    det_iota = lax.broadcasted_iota(jnp.int32, (GROUP, RUN_LEN), 0)
    low_iota = lax.broadcasted_iota(jnp.int32, (LOW, RUN_LEN), 0).astype(F32).astype(BF16)
    row_iota = lax.broadcasted_iota(jnp.int32, (GROUP, PB), 0)
    lane_iota = lax.broadcasted_iota(jnp.int32, (GROUP, PB), 1)
    own_lanes = lane_iota // LOW == row_iota % HIGH
    zero = jnp.zeros((), BF16)
    one = jnp.ones((), BF16)

    def body(group, carry):
        first = pl.multiple_of(group * GROUP, GROUP)
        for run in range(runs):
            lanes = pl.ds(run * RUN_LEN, RUN_LEN)
            offset = offset_ref[pl.ds(first, GROUP), lanes]
            angle = angle_ref[pl.ds(first, GROUP), lanes]
            filtered = filt_ref[pl.ds(first, GROUP), lanes]
            cos_vals = wide_pick(trig, angle)
            sin_vals = wide_pick(trig, angle + NANG)
            packed = []
            for value in (filtered, cos_vals * filtered, sin_vals * filtered):
                upper = value.astype(BF16).astype(F32)
                packed.append(jnp.concatenate([upper, value - upper], axis=0).astype(BF16))
            turn = ((offset // LOW) - det_iota) & (HIGH - 1)
            turn = turn.astype(F32)
            turn = jnp.concatenate([turn, turn], axis=0).astype(BF16)
            left = jnp.concatenate(
                [jnp.where(turn == jnp.asarray(j, BF16), value, zero) for j in range(HIGH) for value in packed],
                axis=0,
            )
            low = (offset & (LOW - 1)).astype(F32)
            hots = []
            for det in range(GROUP):
                line = jnp.broadcast_to(low[det : det + 1, :], (LOW, RUN_LEN)).astype(BF16)
                hots.append(jnp.where(line == low_iota, one, zero))
            right = jnp.concatenate(hots, axis=0)
            product = lax.dot_general(
                left, right, (((1,), (1,)), ((), ())), preferred_element_type=F32
            )
            for k in range(3):
                total = None
                for j in range(HIGH):
                    top = (j * 3 + k) * 2 * GROUP
                    pair = product[top : top + GROUP] + product[top + GROUP : top + 2 * GROUP]
                    part = jnp.where(row_iota < HIGH, pair[:, :PB], pair[:, PB:])
                    part = jnp.where(own_lanes, part, 0.0)
                    if j:
                        part = pltpu.roll(part, LOW * j, 1)
                    total = part if total is None else total + part
                row_ref[run, pl.ds(k, GROUP, stride=ROWS), :] = total
            for det in range(GROUP):
                slot = slot_ref[first + det, (step * runs + run) * RUN]
                at = pl.ds(pl.multiple_of(slot * ROWS, ROWS), ROWS)
                map_ref[at, :] += row_ref[run, pl.ds(det * ROWS, ROWS), :]
        return carry

    lax.fori_loop(0, det_count // GROUP, body, 0, unroll=1)

    @pl.when(step == pl.num_programs(0) - 1)
    def _():
        for reach in range(reach_count):
            for group in range(group_count):
                start = (reach * group_count + group) * cap_count * ROWS
                for k in range(3):
                    piece_ref[reach, group, pl.ds(k * cap_count, cap_count), :] = map_ref[
                        pl.ds(start + k, cap_count, stride=ROWS), :
                    ]


def bin_samples(block_slot, projection, trig, back, weight, pixel_offset, angle_index, timeline, shape, chunk):
    det_dev, samp_dev = pixel_offset.shape
    modes = projection.shape[0]
    reach_count, group_count, cap_count = shape
    slot_total = reach_count * group_count * cap_count
    runs = chunk // RUN_LEN
    wide = pl.BlockSpec((det_dev, chunk), lambda i: (0, i))
    return pl.pallas_call(
        bin_kernel,
        grid=(samp_dev // chunk,),
        out_shape=jax.ShapeDtypeStruct((reach_count, group_count, 3 * cap_count, PB), F32),
        in_specs=[smem_spec(), pl.BlockSpec((modes, chunk), lambda i: (0, i))]
        + [vmem_spec()] * 3
        + [wide, wide, wide],
        out_specs=vmem_spec(),
        scratch_shapes=[
            pltpu.VMEM((slot_total * ROWS, PB), F32),
            pltpu.VMEM((runs, GROUP * ROWS, PB), F32),
            pltpu.VMEM((det_dev, chunk), F32),
        ],
        compiler_params=params(),
        name="bin_samples",
    )(block_slot, projection, trig, back, weight, pixel_offset, angle_index, timeline)


def push_kernel(request_ref, near_ref, far_ref, operated_ref):
    reach_count, group_count, cap_count = request_ref.shape
    operated_ref[...] = jnp.zeros_like(operated_ref)
    for reach, ref in enumerate((near_ref, far_ref)):
        for group in range(group_count):
            sums = []
            for slot in range(cap_count):
                block = request_ref[reach, group, slot]
                for k in range(3):
                    line = operated_ref[k, pl.ds(block, 1), :]
                    sums.append((block, k, line + ref[group, pl.ds(k * cap_count + slot, 1), :]))
            for block, k, line in sums:
                operated_ref[k, pl.ds(block, 1), :] = line


def push_blocks(requests, near, far, shape):
    return pl.pallas_call(
        push_kernel,
        out_shape=jax.ShapeDtypeStruct(shape, F32),
        in_specs=[smem_spec(), vmem_spec(), vmem_spec()],
        out_specs=vmem_spec(),
        compiler_params=params(),
        name="push_blocks",
    )(requests, near, far)


def exchanged(value, axis, bit):
    count = lax.axis_size(axis)
    return lax.ppermute(value, axis, [(source, source ^ bit) for source in range(count)])


def passed_along(value, axis, steps):
    count = lax.axis_size(axis)
    return lax.ppermute(value, axis, [(source, (source + steps) % count) for source in range(count)])


def summed_over_det(value):
    count = lax.axis_size("det")
    modes, samples = value.shape
    half = samples // 2
    core = lax.axis_index("det") % 2
    own = lax.dynamic_slice_in_dim(value, core * half, half, 1)
    other = lax.dynamic_slice_in_dim(value, (1 - core) * half, half, 1)
    own = own + exchanged(other, "det", 1)
    bit = 2
    while bit < count:
        own = own + exchanged(own, "det", bit)
        bit *= 2
    other = exchanged(own, "det", 1)
    lower = jnp.where(core == 0, own, other)
    upper = jnp.where(core == 0, other, own)
    return jnp.concatenate([lower, upper], axis=1)


def on_device(
    solution,
    residual,
    direction,
    preconditioner,
    pull_index,
    block_slot,
    pixel_offset,
    angle_index,
    det_weight,
    mode_templates,
    mode_precision,
):
    requests = pull_index[0, 0]
    det_dev, samp_dev = pixel_offset.shape
    modes = mode_templates.shape[1]
    device_count = lax.axis_size("tm") * lax.axis_size("det")
    chunk = 1024

    pieces = pull_blocks(requests, direction)
    pieces = lax.all_to_all(pieces, "det", split_axis=1, concat_axis=1, tiled=True)
    near = pieces[0]
    far = passed_along(pieces[1], "tm", -1)

    angles = lax.iota(jnp.int32, NANG).astype(F32) * (2.0 * math.pi / NANG)
    trig = jnp.concatenate([jnp.cos(angles), jnp.sin(angles)])
    trig = jnp.broadcast_to(trig[None, :], (GROUP, PB))
    core_matrix = jnp.diag(mode_precision) + jnp.dot(
        mode_templates.T, det_weight[:, None] * mode_templates, precision=HIGHEST
    )
    factor = jnp.linalg.cholesky(core_matrix)
    first_row = lax.axis_index("det") * det_dev
    own_modes = lax.dynamic_slice_in_dim(mode_templates, first_row, det_dev, 0)
    own_weight = lax.dynamic_slice_in_dim(det_weight, first_row, det_dev, 0)
    inverse = jax.scipy.linalg.cho_solve((factor, True), jnp.eye(modes, dtype=F32))
    back = jnp.dot(own_modes, inverse, precision=HIGHEST)
    weighted = (own_weight[:, None] * own_modes).T

    timeline, local_proj = make_timeline(
        block_slot, near, far, trig, weighted, pixel_offset, angle_index, chunk
    )
    projection = summed_over_det(local_proj)
    binned = bin_samples(
        block_slot, projection, trig, back, own_weight[:, None], pixel_offset, angle_index, timeline,
        requests.shape, chunk,
    )
    returning = jnp.stack([binned[0], passed_along(binned[1], "tm", 1)])
    arrived = lax.all_to_all(returning, "det", split_axis=1, concat_axis=1, tiled=True)
    operated = push_blocks(requests, arrived[0], arrived[1], direction.shape)

    old_applied = jnp.stack(precondition(preconditioner, residual))
    operated_applied = jnp.stack(precondition(preconditioner, operated))
    partial = jnp.stack(
        [
            jnp.sum(residual * old_applied),
            jnp.sum(direction * operated),
            jnp.sum(operated * old_applied),
            jnp.sum(operated * operated_applied),
        ]
    )
    sent = jnp.broadcast_to(jnp.pad(partial, (0, PB - 4))[None, :], (device_count, PB))
    totals = jnp.sum(
        lax.all_to_all(sent, ("tm", "det"), split_axis=0, concat_axis=0, tiled=True), axis=0
    )
    rz_old, curv_sum, cross, square = totals[0], totals[1], totals[2], totals[3]
    step_size = rz_old / curv_sum
    rz_new = rz_old - 2.0 * step_size * cross + step_size * step_size * square
    new_solution = solution + step_size * direction
    new_residual = residual - step_size * operated
    applied = jnp.stack(precondition(preconditioner, new_residual))
    new_direction = applied + rz_new / rz_old * direction
    return (new_solution, new_residual, new_direction)


def solution(mesh):
    maps = P(None, ("tm", "det"), None)
    samples = P("det", "tm")
    in_specs = (maps,) * 4 + (P("tm", "det", None, None, None),) + (samples,) * 3 + (P(),) * 3
    return jax.shard_map(
        on_device, mesh=mesh, in_specs=in_specs, out_specs=(maps,) * 3, check_vma=False
    )
```

time: 828 us -> 122 us (0.15)
  matrix products: 467 us -> 1.56 us
  other arithmetic: 112 us -> 13.6 us
  local copies, waits for them, and re-layouts: 91.8 us -> 7.51 us
  blocking collectives: 78.7 us -> 9.06 us
  Pallas kernels: 0 us -> 46.5 us
  waiting for transfers between devices: 41.5 us -> 23.2 us
  between operations: 17.1 us -> 4.81 us
    dot_general x50 -> x1, matrix products: 464 us -> 0.32 us  [on_device(): back = jnp.dot(own_modes, inverse, precision=HIGHEST)]
    psum x2 -> x0, blocking collectives: 78.7 us -> none  [global_dot(): return lax.psum(partial_value, ('tm', 'det'))]
    pallas_call x0 -> x4, Pallas kernels: none -> 46.5 us  [the longest x1 32.3 us: bin_samples(): pl.pallas_call(bin_kernel, grid=(samp_dev // chunk,), out_shape=jax.Shape...]
    eq x48 -> x0, local copies, waits for them, and re-layouts: 40.4 us -> none  [the longest x16 14.7 us: bin_batch(): onehot = (offsets[..., None] == pixel_iota).astype(jnp.float32)]
    add x18 -> x5, other arithmetic: 35.2 us -> 2.24 us  [the longest x3 2.16 us: precondition(): pre[0] * field[0] + pre[3] * field[1] + pre[4] * field[2]]
    psum x1 -> x0, waiting for transfers between devices: 31.3 us -> none  [on_device(): projection = lax.psum(local_proj, 'det')]
    mul x16 -> x0, other arithmetic: 28.5 us -> none  [bin_batch(): cos_vals * filtered_part]
    gather x17 -> x0, local copies, waits for them, and re-layouts: 17.9 us -> none  [the longest x16 15.9 us: read_batch(): values = jnp.take(local_map, slot_ids, axis=1)]
  transfers between devices with their start and end apart: 5 -> 7, of which waited for: 4 -> 6; matrix products, arithmetic and copies ran while one was open for 3% -> 7% of each run, Pallas kernels for 0% -> 0%
where the time goes in v1:
time: 122 us; the launch traced here: 121 us
  Pallas kernels  46.5 us (38%)
  waiting for transfers between devices  23.2 us (19%)
  starting transfers between devices  15 us (12%)
  other arithmetic  13.6 us (11%)
  blocking collectives  9.06 us (7%)
  local copies, waits for them, and re-layouts  7.51 us (6%)
  between operations  4.81 us (4%)
  matrix products  1.56 us (1%)
    pallas_call x1, Pallas kernels, bin_samples(): pl.pallas_call(bin_kernel, grid=(samp_dev // chunk,), out_shape=jax.Shape...  32.3 us
    pallas_call x1, Pallas kernels, make_timeline(): pl.pallas_call(timeline_kernel, grid=(samp_dev // chunk,), out_shape=(jax...  12.4 us
    ppermute x2, waiting for transfers between devices, passed_along(): lax.ppermute(value, axis, [(source, (source + steps) % count) for source...  10.5 us
    all_to_all x1, blocking collectives, on_device(): lax.all_to_all(sent, ('tm', 'det'), split_axis=0, concat_axis=0, tiled=True)  9.06 us
    ppermute x3, waiting for transfers between devices, exchanged(): lax.ppermute(value, axis, [(source, source ^ bit) for source in range(cou...  7.72 us
    ppermute x2, starting transfers between devices, passed_along(): lax.ppermute(value, axis, [(source, (source + steps) % count) for source...  5.59 us
    all_to_all x1, waiting for transfers between devices, on_device(): lax.all_to_all(returning, 'det', split_axis=1, concat_axis=1, tiled=True)  4.49 us
    unnamed x28, local copies, waits for them, and re-layouts  4.46 us
  transfers between devices with their start and end apart: 7, of which 6 were waited for; matrix products, arithmetic and copies ran while one was open for 7% of the time, Pallas kernels for 0%

profile of v1, /device:TPU:0, one launch (start us, length us, event | category | flops | bytes accessed | tf_op | source)
XLA Modules:
  0.0 121.3 jit_solution(1774531864703355345)
XLA Ops:
  0.7 1.2 copy-done.2
  1.9 0.7 copy-done.6
  2.5 0.8 pull_blocks.1
  3.4 0.7 copy.35
  4.0 4.2 %all-to-all-start = ((f32[2,4,48,128]{3,2,0,1:T(8,128)}), f32[2,4,48,128]{3,2,0,1:T(8,128)S(1)}, u32[]{:S(2)}, u32[]{:S(2)}) async-start(f32[2,4,48,128]{3,2,0,1:T(8,128)} %copy.35), calls=%async_computation | async-start | bytes 393216 | tf_op jit(solution)/shard_map/all_to_all | solution.py:338
  8.3 0.8 dynamic_slice.12
  9.0 0.9 fusion.1
  9.9 0.8 multiply_bitcast_fusion.weighted_ref
  10.7 0.1 copy.38
  10.8 0.8 fusion.9
  11.6 1.4 %cholesky.17 = f32[16,16]{1,0:T(8,128)S(1)} custom-call(f32[16,16]{1,0:T(8,128)S(1)} %fusion.9), custom_call_target="Cholesky" | custom-call | tf_op jit(solution)/shard_map/jit(cholesky)/cholesky | solution.py:348
  13.1 0.5 all-to-all-done
  13.6 5.2 %collective-permute-start = (f32[4,48,128]{2,1,0:T(8,128)S(1)}, f32[4,48,128]{2,1,0:T(8,128)S(1)}, u32[]{:S(2)}, u32[]{:S(2)}) collective-permute-start(f32[4,48,128]{2,1,0:T(8,128)S(1)} %get-tuple-element.28), channel_id=1, source_target_pairs={{0,28},{4,0},{8,4},{12,8},{16,12},{20,16},{24,20},{28,24},{1,29},{... | collective-permute-start | bytes 294920 | tf_op jit(solution)/shard_map/ppermute | solution.py:297
  18.8 0.1 pad_maximum_fusion.3
  18.9 2.2 %collective-permute-done.far_ref = f32[4,48,128]{2,1,0:T(8,128)S(1)} collective-permute-done((f32[4,48,128]{2,1,0:T(8,128)S(1)}, f32[4,48,128]{2,1,0:T(8,128)S(1)}, u32[]{:S(2)}, u32[]{:S(2)}) %collective-permute-start) | collective-permute-done | bytes 98336 | tf_op jit(solution)/shard_map/ppermute | solution.py:297
  21.1 12.4 %make_timeline.1 = (f32[64,8192]{1,0:T(8,128)S(1)}, f32[16,8192]{1,0:T(8,128)S(1)}) custom-call(s32[64,64]{1,0:T(8,128)S(1)} %copy-done.5, f32[4,48,128]{2,1,0:T(8,128)S(1)} %get-tuple-element.29.near_ref, f32[4,48,128]{2,1,0:T(8,128)S(1)} %collective-permute-done.far_ref, f32[8,128]{1,0:T(8,128)S(1)} %broadcast_in_dim.39.trig_ref, ...), custom_call_target="tpu_custom_call" | custom-call | tf_op jit(solution)/shard_map/make_timeline/pallas_call | solution.py:137
  33.5 1.3 %copy-done.4 = f32[64,8192]{1,0:T(8,128)} copy-done((f32[64,8192]{1,0:T(8,128)}, f32[64,8192]{1,0:T(8,128)S(1)}, u32[]{:S(2)}) %copy-start.4) | copy-done | bytes 2097176
  34.9 0.1 collective-permute-start.1
  35.0 0.6 compare_reduce_fusion
  35.6 0.6 fusion.3
  36.2 1.2 %custom-call.10 = f32[1,16,16]{1,2,0:T(8,128)S(1)} custom-call(f32[1,16,16]{2,1,0:T(8,128)S(1)} %fusion.3), custom_call_target="InvertDiagBlocksLowerTriangular" | custom-call | tf_op jit(solution)/shard_map/jit(_cho_solve)/triangular_solve | solution.py:352
  37.5 1.7 %collective-permute-start.2 = (f32[16,4096]{1,0:T(8,128)S(1)}, f32[16,4096]{1,0:T(8,128)S(1)}, u32[]{:S(2)}, u32[]{:S(2)}) collective-permute-start(f32[16,4096]{1,0:T(8,128)S(1)} %dynamic-slice_add_fusion), channel_id=1, source_target_pairs={{0,2},{1,3},{2,0},{3,1},{4,6},{5,7},{6,4},{7,5},{8,10},{9,11},{10,... | collective-permute-start | bytes 786440 | tf_op jit(solution)/shard_map/ppermute | solution.py:292
  39.3 0.2 fusion.6
  39.4 0.1 fusion.4
  39.6 6.7 %collective-permute-done.2 = f32[16,4096]{1,0:T(8,128)S(1)} collective-permute-done((f32[16,4096]{1,0:T(8,128)S(1)}, f32[16,4096]{1,0:T(8,128)S(1)}, u32[]{:S(2)}, u32[]{:S(2)}) %collective-permute-start.2) | collective-permute-done | bytes 262176 | tf_op jit(solution)/shard_map/ppermute | solution.py:292
  46.3 0.1 collective-permute-start.3
  46.4 0.1 dynamic-slice_bitcast_fusion
  46.5 0.1 copy.40.weight_ref
  46.6 0.3 fusion.11.back_ref
  46.9 1.0 collective-permute-done.3
  48.0 0.2 copy-done.1
  48.2 32.3 %bin_samples.1 = f32[2,4,48,128]{3,2,1,0:T(8,128)S(1)} custom-call(s32[64,64]{1,0:T(8,128)S(1)} %copy-done.5, f32[16,8192]{1,0:T(8,128)S(1)} %pad_maximum_fusion.1.proj_ref, f32[8,128]{1,0:T(8,128)S(1)} %broadcast_in_dim.39.trig_ref, f32[64,16]{1,0:T(8,128)S(1)} %fusion.11.back_ref, f32[64,1]{1,0:T(8,128)S(1)} %copy.40.weight_ref, s32[64,8192]{1,0:T(8,128)S(1)} %copy-done, ...), custom_call_target="tpu_custom_call" | custom-call | tf_op jit(solution)/shard_map/bin_samples/pallas_call | solution.py:246
  80.6 0.4 collective-permute-start.4
  81.0 8.3 %collective-permute-done.4 = f32[4,48,128]{2,1,0:T(8,128)S(1)} collective-permute-done((f32[4,48,128]{2,1,0:T(8,128)S(1)}, f32[4,48,128]{2,1,0:T(8,128)S(1)}, u32[]{:S(2)}, u32[]{:S(2)}) %collective-permute-start.4) | collective-permute-done | bytes 98336 | tf_op jit(solution)/shard_map/ppermute | solution.py:297
  89.3 0.7 copy.41
  90.0 3.4 %all-to-all-start.1 = ((f32[2,4,48,128]{3,2,0,1:T(8,128)}), f32[2,4,48,128]{3,2,0,1:T(8,128)S(1)}, u32[]{:S(2)}, u32[]{:S(2)}) async-start(f32[2,4,48,128]{3,2,0,1:T(8,128)} %copy.41), calls=%async_computation.1 | async-start | bytes 393216 | tf_op jit(solution)/shard_map/all_to_all | solution.py:365
  93.4 0.8 multiply_add_fusion.9
  94.2 4.5 %all-to-all-done.1 = f32[2,4,48,128]{3,2,0,1:T(8,128)S(1)} async-done(((f32[2,4,48,128]{3,2,0,1:T(8,128)}), f32[2,4,48,128]{3,2,0,1:T(8,128)S(1)}, u32[]{:S(2)}, u32[]{:S(2)}) %all-to-all-start.1) | async-done | bytes 196640 | tf_op jit(solution)/shard_map/all_to_all | solution.py:365
  98.7 1.0 push_blocks.1
  99.7 0.1 multiply_add_fusion.6
  99.8 0.9 copy-done.3
  100.8 0.9 multiply_reduce_fusion.2
  101.7 2.6 %select_maximum_fusion = f32[128]{0:T(128)S(1)} fusion(f32[1]{0:T(128)} %bitcast.15, f32[1]{0:T(128)} %bitcast.14, f32[1]{0:T(128)} %bitcast.13, f32[1]{0:T(128)} %bitcast), kind=kLoop, calls=%fused_computation.50 | loop fusion | flops 1024 | bytes 528 | tf_op jit(solution)/shard_map/stack | solution.py:370
  104.4 9.1 %all_to_all.16 = f32[32,1,128]{2,1,0:T(1,128)S(1)} all-to-all(f32[32,1,128]{2,1,0:T(1,128)S(1)} %broadcast_in_dim.44), channel_id=1, replica_groups=mesh['tm'=8,'det'=4] {'tm','det'}, dimensions={0} | all-to-all | bytes 32768 | tf_op jit(solution)/shard_map/all_to_all | solution.py:380
  113.5 0.6 fusion.17
  115.4 0.9 multiply_subtract_fusion
  118.9 1.3 %multiply_add_fusion.3 = (f32[1,384,128]{2,1,0:T(8,128)S(1)}, f32[1,384,128]{2,1,0:T(8,128)S(1)}, f32[1,384,128]{2,1,0:T(8,128)S(1)}) fusion(f32[3,384,128]{2,1,0:T(8,128)} %multiply_subtract_fusion, f32[6,384,128]{2,1,0:T(8,128)S(1)} %copy-done.8), kind=kLoop, calls=%fused_computation.14 | loop fusion | flops 737280 | bytes 2359296 | tf_op jit(solution)/shard_map/add | solution.py:52
  120.2 1.1 maximum_add_fusion
  (38 shorter events, 0.5 us)
Async XLA Ops:
  0.6 20.4 %copy-start = (s32[64,8192]{1,0:T(8,128)S(1)}, s32[64,8192]{1,0:T(8,128)}, u32[]{:S(2)}) copy-start(s32[64,8192]{1,0:T(8,128)} %offset_ref.3) | copy-start | bytes 6291460
  0.6 1.2 %copy-start.2 = (f32[3,384,128]{2,1,0:T(8,128)S(1)}, f32[3,384,128]{2,1,0:T(8,128)}, u32[]{:S(2)}) copy-start(f32[3,384,128]{2,1,0:T(8,128)} %direction_ref.1) | copy-start | bytes 1769476
  1.9 0.7 copy-start.6
  2.5 18.5 %copy-start.5 = (s32[64,64]{1,0:T(8,128)S(1)}, s32[64,64]{1,0:T(8,128)}, u32[]{:S(2)}) copy-start(s32[64,64]{1,0:T(8,128)} %slot_ref.3) | copy-start | bytes 49156
  4.0 9.5 %all-to-all-start = ((f32[2,4,48,128]{3,2,0,1:T(8,128)}), f32[2,4,48,128]{3,2,0,1:T(8,128)S(1)}, u32[]{:S(2)}, u32[]{:S(2)}) async-start(f32[2,4,48,128]{3,2,0,1:T(8,128)} %copy.35), calls=%async_computation | async-start | bytes 393216 | tf_op jit(solution)/shard_map/all_to_all | solution.py:338
  13.6 7.5 %collective-permute-start = (f32[4,48,128]{2,1,0:T(8,128)S(1)}, f32[4,48,128]{2,1,0:T(8,128)S(1)}, u32[]{:S(2)}, u32[]{:S(2)}) collective-permute-start(f32[4,48,128]{2,1,0:T(8,128)S(1)} %get-tuple-element.28), channel_id=1, source_target_pairs={{0,28},{4,0},{8,4},{12,8},{16,12},{20,16},{24,20},{28,24},{1,29},{... | collective-permute-start | bytes 294920 | tf_op jit(solution)/shard_map/ppermute | solution.py:297
  33.5 1.3 %copy-start.4 = (f32[64,8192]{1,0:T(8,128)}, f32[64,8192]{1,0:T(8,128)S(1)}, u32[]{:S(2)}) copy-start(f32[64,8192]{1,0:T(8,128)S(1)} %get-tuple-element.6.time_ref) | copy-start | bytes 6291460
  34.9 11.6 %copy-start.13 = (f32[256]{0:T(256)S(1)}, f32[256]{0:T(256)}, u32[]{:S(2)}) copy-start(f32[256]{0:T(256)} %param.19) | copy-start | bytes 3076
  34.9 11.8 %copy-start.12 = (f32[256,16]{0,1:T(8,128)S(1)}, f32[256,16]{0,1:T(8,128)}, u32[]{:S(2)}) copy-start(f32[256,16]{0,1:T(8,128)} %param.20) | copy-start | bytes 49156
  34.9 2.6 %collective-permute-start.1 = (f32[16,4096]{1,0:T(8,128)S(1)}, f32[16,4096]{1,0:T(8,128)S(1)}, u32[]{:S(2)}, u32[]{:S(2)}) collective-permute-start(f32[16,4096]{1,0:T(8,128)S(1)} %constant_dynamic-slice_fusion), channel_id=1, source_target_pairs={{0,1},{1,0},{2,3},{3,2},{4,5},{5,4},{6,7},{7,6},{8,9},{9,8},{10,11... | collective-permute-start | bytes 786440 | tf_op jit(solution)/shard_map/ppermute | solution.py:292
  37.5 8.8 %collective-permute-start.2 = (f32[16,4096]{1,0:T(8,128)S(1)}, f32[16,4096]{1,0:T(8,128)S(1)}, u32[]{:S(2)}, u32[]{:S(2)}) collective-permute-start(f32[16,4096]{1,0:T(8,128)S(1)} %dynamic-slice_add_fusion), channel_id=1, source_target_pairs={{0,2},{1,3},{2,0},{3,1},{4,6},{5,7},{6,4},{7,5},{8,10},{9,11},{10,... | collective-permute-start | bytes 786440 | tf_op jit(solution)/shard_map/ppermute | solution.py:292
  46.3 1.6 %collective-permute-start.3 = (f32[16,4096]{1,0:T(8,128)S(1)}, f32[16,4096]{1,0:T(8,128)S(1)}, u32[]{:S(2)}, u32[]{:S(2)}) collective-permute-start(f32[16,4096]{1,0:T(8,128)S(1)} %add.135), channel_id=1, source_target_pairs={{0,1},{1,0},{2,3},{3,2},{4,5},{5,4},{6,7},{7,6},{8,9},{9,8},{10,11... | collective-permute-start | bytes 786440 | tf_op jit(solution)/shard_map/ppermute | solution.py:292
  46.6 1.6 %copy-start.1 = (s32[64,8192]{1,0:T(8,128)S(1)}, s32[64,8192]{1,0:T(8,128)}, u32[]{:S(2)}) copy-start(s32[64,8192]{1,0:T(8,128)} %angle_ref.3) | copy-start | bytes 6291460
  48.2 45.2 %copy-start.9 = (f32[3,384,128]{2,1,0:T(8,128)S(1)}, f32[3,384,128]{2,1,0:T(8,128)}, u32[]{:S(2)}) copy-start(f32[3,384,128]{2,1,0:T(8,128)} %param.12) | copy-start | bytes 1769476
  80.5 12.8 %copy-start.8 = (f32[6,384,128]{2,1,0:T(8,128)S(1)}, f32[6,384,128]{2,1,0:T(8,128)}, u32[]{:S(2)}) copy-start(f32[6,384,128]{2,1,0:T(8,128)} %param.14) | copy-start | bytes 3538948
  80.6 8.7 %collective-permute-start.4 = (f32[4,48,128]{2,1,0:T(8,128)S(1)}, f32[4,48,128]{2,1,0:T(8,128)S(1)}, u32[]{:S(2)}, u32[]{:S(2)}) collective-permute-start(f32[4,48,128]{2,1,0:T(8,128)S(1)} %get-tuple-element.27), channel_id=1, source_target_pairs={{0,4},{4,8},{8,12},{12,16},{16,20},{20,24},{24,28},{28,0},{1,5},{5... | collective-permute-start | bytes 294920 | tf_op jit(solution)/shard_map/ppermute | solution.py:297
  90.0 8.7 %all-to-all-start.1 = ((f32[2,4,48,128]{3,2,0,1:T(8,128)}), f32[2,4,48,128]{3,2,0,1:T(8,128)S(1)}, u32[]{:S(2)}, u32[]{:S(2)}) async-start(f32[2,4,48,128]{3,2,0,1:T(8,128)} %copy.41), calls=%async_computation.1 | async-start | bytes 393216 | tf_op jit(solution)/shard_map/all_to_all | solution.py:365
  93.4 5.3 %copy-start.7 = (s32[1,1,2,4,16]{4,3,2,1,0:T(4,128)S(1)}, s32[1,1,2,4,16]{4,3,2,1,0:T(4,128)}, u32[]{:S(2)}) copy-start(s32[1,1,2,4,16]{4,3,2,1,0:T(4,128)} %param.15) | copy-start | bytes 1540
  99.7 1.1 copy-start.3
  99.7 1.1 copy-start.10
  118.9 1.3 %copy-start.11 = (f32[3,384,128]{2,1,0:T(8,128)S(1)}, f32[3,384,128]{2,1,0:T(8,128)}, u32[]{:S(2)}) copy-start(f32[3,384,128]{2,1,0:T(8,128)} %param.11) | copy-start | bytes 1769476

commit v2 on v1

v2 whole, which is shorter than its diff:
```python
import math

import jax
import jax.numpy as jnp
import numpy as np
from jax import lax
from jax.experimental import pallas as pl
from jax.experimental.pallas import tpu as pltpu
from jax.sharding import PartitionSpec as P

PB = 128
SB = 128
RUN = 4
NANG = 64
GROUP = 8
RUN_LEN = RUN * SB
ROWS = 8
LOW = 32
HIGH = PB // LOW
F32 = jnp.float32
BF16 = jnp.bfloat16
HIGHEST = lax.Precision.HIGHEST
MIB = 1024 * 1024
TERMS = 8


def vmem_spec():
    return pl.BlockSpec(memory_space=pltpu.VMEM)


def smem_spec():
    return pl.BlockSpec(memory_space=pltpu.SMEM)


def params(mib):
    return pltpu.CompilerParams(vmem_limit_bytes=mib * MIB)


def wave_terms():
    turn = (np.arange(NANG) - NANG // 2).astype(np.float64) / NANG
    powers = np.stack([turn ** (2 * term) for term in range(TERMS)], axis=1)
    even = np.linalg.lstsq(powers, -np.cos(2.0 * math.pi * turn), rcond=None)[0]
    odd = np.linalg.lstsq(powers * turn[:, None], -np.sin(2.0 * math.pi * turn), rcond=None)[0]
    return [float(term) for term in even], [float(term) for term in odd]


EVEN_TERMS, ODD_TERMS = wave_terms()


def waves(angle):
    turn = (angle - NANG // 2).astype(F32) * (1.0 / NANG)
    square = turn * turn
    even = jnp.full_like(turn, EVEN_TERMS[-1])
    odd = jnp.full_like(turn, ODD_TERMS[-1])
    for term in range(TERMS - 2, -1, -1):
        even = even * square + EVEN_TERMS[term]
        odd = odd * square + ODD_TERMS[term]
    return even, odd * turn


def trig_table():
    angles = (np.arange(NANG, dtype=np.float32) * np.float32(2.0 * math.pi / NANG)).astype(np.float64)
    row = np.concatenate([np.cos(angles), np.sin(angles)]).astype(np.float32)
    return jnp.asarray(np.broadcast_to(row[None, :], (GROUP, PB)))


def halves(value):
    first = value.astype(BF16)
    rest = value - first.astype(F32)
    second = rest.astype(BF16)
    return first, second, (rest - second.astype(F32)).astype(BF16)


def lane_pick(table, index):
    return jnp.take_along_axis(table, index, axis=1, mode="promise_in_bounds")


def wide_pick(table, index):
    parts = [
        lane_pick(table, index[:, PB * part : PB * (part + 1)])
        for part in range(index.shape[1] // PB)
    ]
    return jnp.concatenate(parts, axis=1)


def precondition(pre, field):
    return (
        pre[0] * field[0] + pre[3] * field[1] + pre[4] * field[2],
        pre[3] * field[0] + pre[1] * field[1] + pre[5] * field[2],
        pre[4] * field[0] + pre[5] * field[1] + pre[2] * field[2],
    )


def partner(det, hop, flip):
    return det ^ (2 * hop + flip)


def pull_kernel(det_ref, request_ref, direction_ref, own_ref, other_ref):
    _, _, reach_count, group_count, cap_count = request_ref.shape
    det = det_ref[0]
    for flip, ref in ((1, other_ref), (0, own_ref)):
        for reach in range(reach_count):
            for hop in range(group_count // 2):
                group = partner(det, hop, flip)
                for slot in range(cap_count):
                    block = request_ref[0, 0, reach, group, slot]
                    for k in range(3):
                        ref[reach, hop, pl.ds(k * cap_count + slot, 1), :] = direction_ref[
                            k, pl.ds(block, 1), :
                        ]


def pull_blocks(det, pull_index, direction):
    _, _, reach_count, group_count, cap_count = pull_index.shape
    piece = jax.ShapeDtypeStruct((reach_count, group_count // 2, 3 * cap_count, PB), F32)
    return pl.pallas_call(
        pull_kernel,
        out_shape=(piece, piece),
        in_specs=[smem_spec(), smem_spec(), vmem_spec()],
        out_specs=(vmem_spec(), vmem_spec()),
        compiler_params=params(8),
        name="pull_blocks",
    )(det, pull_index, direction)


def mode_kernel(det_ref, template_ref, weight_ref, precision_ref, back_ref, weighted_ref, own_weight_ref):
    det_dev = back_ref.shape[0]
    modes = template_ref.shape[1]
    templates = template_ref[...]
    weight = weight_ref[...]
    first = pl.multiple_of(det_ref[0] * det_dev, det_dev)
    own_templates = template_ref[pl.ds(first, det_dev), :]
    own_weight = weight_ref[pl.ds(first, det_dev), :]
    own_weight_ref[...] = own_weight
    weighted_ref[...] = (own_templates * own_weight).T
    row = lax.broadcasted_iota(jnp.int32, (modes, modes), 0)
    column = lax.broadcasted_iota(jnp.int32, (modes, modes), 1)
    unit = (row == column).astype(F32)
    core = unit * precision_ref[...] + lax.dot_general(
        weight * templates, templates, (((0,), (0,)), ((), ())), precision=HIGHEST, preferred_element_type=F32
    )
    inverse = unit
    line = lax.broadcasted_iota(jnp.int32, (modes, 1), 0)
    for step in range(modes):
        root = 1.0 / jnp.sqrt(core[step : step + 1, step : step + 1])
        factor = jnp.where(line > step, core[:, step : step + 1] * root, 0.0)
        core_row = core[step : step + 1, :] * root
        inverse_row = inverse[step : step + 1, :] * root
        core = core - factor * core_row
        inverse = jnp.where(line == step, inverse_row, inverse - factor * inverse_row)
    solved = lax.dot_general(
        inverse, inverse, (((0,), (0,)), ((), ())), precision=HIGHEST, preferred_element_type=F32
    )
    back_ref[...] = jnp.dot(own_templates, solved, precision=HIGHEST, preferred_element_type=F32)


def mode_matrices(det, det_dev, mode_templates, det_weight, mode_precision):
    modes = mode_templates.shape[1]
    return pl.pallas_call(
        mode_kernel,
        out_shape=(
            jax.ShapeDtypeStruct((det_dev, modes), F32),
            jax.ShapeDtypeStruct((modes, det_dev), F32),
            jax.ShapeDtypeStruct((det_dev, 1), F32),
        ),
        in_specs=[smem_spec(), vmem_spec(), vmem_spec(), vmem_spec()],
        out_specs=(vmem_spec(), vmem_spec(), vmem_spec()),
        compiler_params=params(8),
        name="mode_matrices",
    )(det, mode_templates, det_weight[:, None], mode_precision[None, :])


def timeline_kernel(det_ref, slot_ref, weighted_ref, offset_ref, angle_ref, *refs):
    *piece_refs, time_ref, proj_ref, map_ref, table_ref = refs
    step = pl.program_id(0)
    cap_count = piece_refs[0].shape[1] // 3
    hop_count = len(piece_refs) // 2
    det_count, chunk = offset_ref.shape
    runs = chunk // RUN_LEN

    @pl.when(step == 0)
    def _():
        det = det_ref[0]
        for place, ref in enumerate(piece_refs):
            reach, hop = place // hop_count, place % hop_count
            for flip in range(2):
                block = (reach * 2 * hop_count + partner(det, hop, flip)) * cap_count
                first = pl.multiple_of(block * ROWS, cap_count * ROWS)
                for k in range(3):
                    map_ref[pl.ds(first + k, cap_count, stride=ROWS), :] = ref[
                        flip, pl.ds(k * cap_count, cap_count), :
                    ]

    def body(group, carry):
        first = pl.multiple_of(group * GROUP, GROUP)
        for run in range(runs):
            for det in range(GROUP):
                slot = slot_ref[first + det, (step * runs + run) * RUN]
                table_ref[run, pl.ds(det * ROWS, ROWS), :] = map_ref[
                    pl.ds(pl.multiple_of(slot * ROWS, ROWS), ROWS), :
                ]
            tables = [table_ref[run, pl.ds(k, GROUP, stride=ROWS), :] for k in range(3)]
            for part in range(RUN):
                lanes = pl.ds(run * RUN_LEN + part * SB, SB)
                offset = offset_ref[pl.ds(first, GROUP), lanes]
                angle = angle_ref[pl.ds(first, GROUP), lanes]
                cos_vals, sin_vals = waves(angle)
                time_ref[pl.ds(first, GROUP), lanes] = (
                    lane_pick(tables[0], offset)
                    + cos_vals * lane_pick(tables[1], offset)
                    + sin_vals * lane_pick(tables[2], offset)
                )
        return carry

    lax.fori_loop(0, det_count // GROUP, body, 0, unroll=4)
    proj_ref[...] = jnp.dot(
        weighted_ref[...], time_ref[...], precision=HIGHEST, preferred_element_type=F32
    )


def make_timeline(det, block_slot, weighted, pixel_offset, angle_index, pieces, chunk):
    det_dev, samp_dev = pixel_offset.shape
    modes = weighted.shape[0]
    slot_total = len(pieces) * 2 * (pieces[0].shape[1] // 3)
    runs = chunk // RUN_LEN
    wide = pl.BlockSpec((det_dev, chunk), lambda i: (0, i))
    return pl.pallas_call(
        timeline_kernel,
        grid=(samp_dev // chunk,),
        out_shape=(
            jax.ShapeDtypeStruct((det_dev, samp_dev), F32),
            jax.ShapeDtypeStruct((modes, samp_dev), F32),
        ),
        in_specs=[smem_spec(), smem_spec(), vmem_spec(), wide, wide] + [vmem_spec()] * len(pieces),
        out_specs=(wide, pl.BlockSpec((modes, chunk), lambda i: (0, i))),
        scratch_shapes=[
            pltpu.VMEM((slot_total * ROWS, PB), F32),
            pltpu.VMEM((runs, GROUP * ROWS, PB), F32),
        ],
        compiler_params=params(16),
        name="make_timeline",
    )(det, block_slot, weighted, pixel_offset, angle_index, *pieces)


def bin_kernel(
    det_ref, slot_ref, proj_ref, trig_ref, back_ref, weight_ref, offset_ref, angle_ref, time_ref,
    own_ref, other_ref, map_ref, row_ref, filt_ref,
):
    step = pl.program_id(0)
    reach_count, hop_count, rows, _ = own_ref.shape
    cap_count = rows // 3
    det_count, chunk = offset_ref.shape
    runs = chunk // RUN_LEN

    @pl.when(step == 0)
    def _():
        map_ref[...] = jnp.zeros_like(map_ref)
        row_ref[...] = jnp.zeros_like(row_ref)

    back = halves(back_ref[...])
    proj = halves(proj_ref[...])
    orders = ((0, 0), (0, 1), (1, 0), (0, 2), (1, 1), (2, 0))
    common = jnp.dot(
        jnp.concatenate([back[left] for left, _ in orders], axis=1),
        jnp.concatenate([proj[right] for _, right in orders], axis=0),
        preferred_element_type=F32,
    )
    filt_ref[...] = weight_ref[...] * (time_ref[...] - common)
    trig = trig_ref[...]
    det_iota = lax.broadcasted_iota(jnp.int32, (GROUP, RUN_LEN), 0)
    low_iota = lax.broadcasted_iota(jnp.int32, (LOW, RUN_LEN), 0).astype(F32).astype(BF16)
    row_iota = lax.broadcasted_iota(jnp.int32, (GROUP, PB), 0)
    lane_iota = lax.broadcasted_iota(jnp.int32, (GROUP, PB), 1)
    own_lanes = lane_iota // LOW == row_iota % HIGH
    zero = jnp.zeros((), BF16)
    one = jnp.ones((), BF16)

    def body(group, carry):
        first = pl.multiple_of(group * GROUP, GROUP)
        for run in range(runs):
            lanes = pl.ds(run * RUN_LEN, RUN_LEN)
            offset = offset_ref[pl.ds(first, GROUP), lanes]
            angle = angle_ref[pl.ds(first, GROUP), lanes]
            filtered = filt_ref[pl.ds(first, GROUP), lanes]
            cos_vals = wide_pick(trig, angle)
            sin_vals = wide_pick(trig, angle + NANG)
            packed = []
            for value in (filtered, cos_vals * filtered, sin_vals * filtered):
                upper = value.astype(BF16).astype(F32)
                packed.append(jnp.concatenate([upper, value - upper], axis=0).astype(BF16))
            turn = ((offset // LOW) - det_iota) & (HIGH - 1)
            turn = turn.astype(F32)
            turn = jnp.concatenate([turn, turn], axis=0).astype(BF16)
            left = jnp.concatenate(
                [jnp.where(turn == jnp.asarray(j, BF16), value, zero) for j in range(HIGH) for value in packed],
                axis=0,
            )
            low = (offset & (LOW - 1)).astype(F32)
            hots = []
            for det in range(GROUP):
                line = jnp.broadcast_to(low[det : det + 1, :], (LOW, RUN_LEN)).astype(BF16)
                hots.append(jnp.where(line == low_iota, one, zero))
            right = jnp.concatenate(hots, axis=0)
            product = lax.dot_general(
                left, right, (((1,), (1,)), ((), ())), preferred_element_type=F32
            )
            for k in range(3):
                total = None
                for j in range(HIGH):
                    top = (j * 3 + k) * 2 * GROUP
                    pair = product[top : top + GROUP] + product[top + GROUP : top + 2 * GROUP]
                    part = jnp.where(row_iota < HIGH, pair[:, :PB], pair[:, PB:])
                    part = jnp.where(own_lanes, part, 0.0)
                    if j:
                        part = pltpu.roll(part, LOW * j, 1)
                    total = part if total is None else total + part
                row_ref[run, pl.ds(k, GROUP, stride=ROWS), :] = total
            for det in range(GROUP):
                slot = slot_ref[first + det, (step * runs + run) * RUN]
                at = pl.ds(pl.multiple_of(slot * ROWS, ROWS), ROWS)
                map_ref[at, :] += row_ref[run, pl.ds(det * ROWS, ROWS), :]
        return carry

    lax.fori_loop(0, det_count // GROUP, body, 0, unroll=8)

    @pl.when(step == pl.num_programs(0) - 1)
    def _():
        det = det_ref[0]
        for flip, ref in ((1, other_ref), (0, own_ref)):
            for reach in range(reach_count):
                for hop in range(hop_count):
                    block = (reach * 2 * hop_count + partner(det, hop, flip)) * cap_count
                    start = pl.multiple_of(block * ROWS, cap_count * ROWS)
                    for k in range(3):
                        ref[reach, hop, pl.ds(k * cap_count, cap_count), :] = map_ref[
                            pl.ds(start + k, cap_count, stride=ROWS), :
                        ]


def bin_samples(
    det, block_slot, projection, trig, back, weight, pixel_offset, angle_index, timeline, shape, chunk
):
    det_dev, samp_dev = pixel_offset.shape
    modes = projection.shape[0]
    reach_count, group_count, cap_count = shape
    slot_total = reach_count * group_count * cap_count
    runs = chunk // RUN_LEN
    wide = pl.BlockSpec((det_dev, chunk), lambda i: (0, i))
    piece = jax.ShapeDtypeStruct((reach_count, group_count // 2, 3 * cap_count, PB), F32)
    return pl.pallas_call(
        bin_kernel,
        grid=(samp_dev // chunk,),
        out_shape=(piece, piece),
        in_specs=[smem_spec(), smem_spec(), pl.BlockSpec((modes, chunk), lambda i: (0, i))]
        + [vmem_spec()] * 3
        + [wide, wide, wide],
        out_specs=(vmem_spec(), vmem_spec()),
        scratch_shapes=[
            pltpu.VMEM((slot_total * ROWS, PB), F32),
            pltpu.VMEM((runs, GROUP * ROWS, PB), F32),
            pltpu.VMEM((det_dev, chunk), F32),
        ],
        compiler_params=params(24),
        name="bin_samples",
    )(det, block_slot, projection, trig, back, weight, pixel_offset, angle_index, timeline)


def push_kernel(det_ref, request_ref, direction_ref, residual_ref, pre_ref, *refs):
    *piece_refs, operated_ref, part_ref = refs
    cap_count = request_ref.shape[4]
    hop_count = len(piece_refs) // 2
    det = det_ref[0]
    operated_ref[...] = jnp.zeros_like(operated_ref)
    for place, ref in enumerate(piece_refs):
        reach, hop = place // hop_count, place % hop_count
        for flip in range(2):
            group = partner(det, hop, flip)
            sums = []
            for slot in range(cap_count):
                block = request_ref[0, 0, reach, group, slot]
                for k in range(3):
                    line = operated_ref[k, pl.ds(block, 1), :]
                    sums.append((block, k, line + ref[flip, pl.ds(k * cap_count + slot, 1), :]))
            for block, k, line in sums:
                operated_ref[k, pl.ds(block, 1), :] = line

    blocks = operated_ref.shape[1]

    def body(index, totals):
        rows = pl.ds(pl.multiple_of(index * ROWS, ROWS), ROWS)
        pre = [pre_ref[entry, rows, :] for entry in range(6)]
        old = [residual_ref[k, rows, :] for k in range(3)]
        oper = [operated_ref[k, rows, :] for k in range(3)]
        line = [direction_ref[k, rows, :] for k in range(3)]
        old_applied = precondition(pre, old)
        oper_applied = precondition(pre, oper)

        def dot(left, right):
            return left[0] * right[0] + left[1] * right[1] + left[2] * right[2]

        parts = (dot(old, old_applied), dot(line, oper), dot(oper, old_applied), dot(oper, oper_applied))
        return tuple(total + part for total, part in zip(totals, parts))

    nothing = jnp.zeros((ROWS, PB), F32)
    totals = lax.fori_loop(0, blocks // ROWS, body, (nothing,) * 4, unroll=4)
    lane = lax.broadcasted_iota(jnp.int32, part_ref.shape, 1)
    row = jnp.zeros(part_ref.shape, F32)
    for place, total in enumerate(totals):
        value = jnp.sum(jnp.sum(total, axis=0, keepdims=True), axis=1, keepdims=True)
        row = jnp.where(lane == place, value, row)
    part_ref[...] = row


def push_blocks(det, pull_index, direction, residual, preconditioner, pieces, device_count):
    return pl.pallas_call(
        push_kernel,
        out_shape=(
            jax.ShapeDtypeStruct(direction.shape, F32),
            jax.ShapeDtypeStruct((device_count, PB), F32),
        ),
        in_specs=[smem_spec(), smem_spec()] + [vmem_spec()] * (3 + len(pieces)),
        out_specs=(vmem_spec(), vmem_spec()),
        compiler_params=params(16),
        name="push_blocks",
    )(det, pull_index, direction, residual, preconditioner, *pieces)


def update_kernel(
    part_ref, solution_ref, residual_ref, direction_ref, operated_ref, pre_ref, new_solution_ref, new_residual_ref, new_direction_ref
):
    totals = jnp.sum(part_ref[...], axis=0, keepdims=True)
    rz_old, curv_sum, cross, square = (totals[:, place : place + 1] for place in range(4))
    size = rz_old / curv_sum
    ratio = (rz_old - 2.0 * size * cross + size * size * square) / rz_old
    size = jnp.broadcast_to(size, (ROWS, PB))
    ratio = jnp.broadcast_to(ratio, (ROWS, PB))

    def body(index, carry):
        rows = pl.ds(pl.multiple_of(index * ROWS, ROWS), ROWS)
        line = [direction_ref[k, rows, :] for k in range(3)]
        new = [residual_ref[k, rows, :] - size * operated_ref[k, rows, :] for k in range(3)]
        applied = precondition([pre_ref[entry, rows, :] for entry in range(6)], new)
        for k in range(3):
            new_solution_ref[k, rows, :] = solution_ref[k, rows, :] + size * line[k]
            new_residual_ref[k, rows, :] = new[k]
            new_direction_ref[k, rows, :] = applied[k] + ratio * line[k]
        return carry

    lax.fori_loop(0, solution_ref.shape[1] // ROWS, body, 0, unroll=4)


def update_maps(parts, solution, residual, direction, operated, preconditioner, chunk):
    maps = pl.BlockSpec((3, chunk, PB), lambda i: (0, i, 0))
    wide = pl.BlockSpec((6, chunk, PB), lambda i: (0, i, 0))
    return pl.pallas_call(
        update_kernel,
        grid=(solution.shape[1] // chunk,),
        out_shape=(jax.ShapeDtypeStruct(solution.shape, F32),) * 3,
        in_specs=[vmem_spec()] + [maps] * 4 + [wide],
        out_specs=(maps,) * 3,
        compiler_params=params(16),
        name="update_maps",
    )(parts, solution, residual, direction, operated, preconditioner)


def exchanged(value, axis, bit):
    count = lax.axis_size(axis)
    return lax.ppermute(value, axis, [(source, source ^ bit) for source in range(count)])


def delivered(own, other, sign):
    times, dets = lax.axis_size("tm"), lax.axis_size("det")
    got = exchanged(other, "det", 1)
    pieces = []
    for reach in range(own.shape[0]):
        for hop in range(own.shape[1]):
            pair = jnp.stack([own[reach, hop], got[reach, hop]])
            if reach or hop:
                pair = lax.ppermute(
                    pair,
                    ("tm", "det"),
                    [
                        (time * dets + det, (time + sign * reach) % times * dets + (det ^ (2 * hop)))
                        for time in range(times)
                        for det in range(dets)
                    ],
                )
            pieces.append(pair)
    return pieces


def summed_over_det(value):
    count = lax.axis_size("det")
    half = value.shape[1] // 2
    core = lax.axis_index("det") % 2
    own = lax.dynamic_slice_in_dim(value, core * half, half, 1)
    other = lax.dynamic_slice_in_dim(value, (1 - core) * half, half, 1)
    own = own + exchanged(other, "det", 1)
    bit = 2
    while bit < count:
        own = own + exchanged(own, "det", bit)
        bit *= 2
    other = exchanged(own, "det", 1)
    lower = jnp.where(core == 0, own, other)
    upper = jnp.where(core == 0, other, own)
    return jnp.concatenate([lower, upper], axis=1)


def on_device(
    solution,
    residual,
    direction,
    preconditioner,
    pull_index,
    block_slot,
    pixel_offset,
    angle_index,
    det_weight,
    mode_templates,
    mode_precision,
):
    det_dev = pixel_offset.shape[0]
    device_count = lax.axis_size("tm") * lax.axis_size("det")
    det = lax.axis_index("det").astype(jnp.int32)[None]

    own, other = pull_blocks(det, pull_index, direction)
    pieces = delivered(own, other, -1)
    back, weighted, own_weight = mode_matrices(det, det_dev, mode_templates, det_weight, mode_precision)
    timeline, local_proj = make_timeline(
        det, block_slot, weighted, pixel_offset, angle_index, pieces, 2048
    )
    projection = summed_over_det(local_proj)
    own, other = bin_samples(
        det, block_slot, projection, trig_table(), back, own_weight, pixel_offset, angle_index, timeline,
        pull_index.shape[2:], 1024,
    )
    arrived = delivered(own, other, 1)
    operated, parts = push_blocks(
        det, pull_index, direction, residual, preconditioner, arrived, device_count
    )
    parts = lax.all_to_all(parts, ("tm", "det"), split_axis=0, concat_axis=0, tiled=True)
    return update_maps(parts, solution, residual, direction, operated, preconditioner, 96)


def solution(mesh):
    maps = P(None, ("tm", "det"), None)
    samples = P("det", "tm")
    in_specs = (maps,) * 4 + (P("tm", "det", None, None, None),) + (samples,) * 3 + (P(),) * 3
    return jax.shard_map(
        on_device, mesh=mesh, in_specs=in_specs, out_specs=(maps,) * 3, check_vma=False
    )
```

time: 122 us -> 84.5 us (0.69)
  Pallas kernels: 46.5 us -> 28.7 us
  other arithmetic: 13.6 us -> 0.17 us
  starting transfers between devices: 15 us -> 10.8 us
  between operations: 4.81 us -> 0.92 us
  local copies, waits for them, and re-layouts: 7.51 us -> 11 us
  matrix products: 1.56 us -> 0 us
    pallas_call x3 -> x5, Pallas kernels: 34.1 us -> 21.6 us  [the longest x1 14.8 us: bin_samples(): pl.pallas_call(bin_kernel, grid=(samp_dev // chunk,), out_shape=(piece, p...]
    all_to_all x2 -> x0, starting transfers between devices: 7.57 us -> none  [the longest x1 4.21 us: on_device(): lax.all_to_all(pieces, 'det', split_axis=1, concat_axis=1, tiled=True)]
    another operation x7 -> x8, other arithmetic: 6.65 us -> 0.04 us  [delivered(): pair = jnp.stack([own[reach, hop], got[reach, hop]])]
    unnamed x28 -> x35, local copies, waits for them, and re-layouts: 4.46 us -> 10.1 us
    pallas_call x1, Pallas kernels: 12.4 us -> 7.08 us  [make_timeline(): pl.pallas_call(timeline_kernel, grid=(samp_dev // chunk,), out_shape=(jax...]
    all_to_all x2 -> x0, waiting for transfers between devices: 4.96 us -> none  [the longest x1 4.49 us: on_device(): lax.all_to_all(returning, 'det', split_axis=1, concat_axis=1, tiled=True)]
    ppermute x3 -> x5, waiting for transfers between devices: 7.72 us -> 11.8 us  [exchanged(): lax.ppermute(value, axis, [(source, source ^ bit) for source in range(cou...]
    ppermute x2 -> x6, starting transfers between devices: 5.59 us -> 9 us  [delivered(): lax.ppermute(pair, ('tm', 'det'), [(time * dets + det, (time + sign * rea...]
  transfers between devices with their start and end apart: 7 -> 11, of which waited for: 6 -> 8; matrix products, arithmetic and copies ran while one was open for 7% -> 2% of each run, Pallas kernels for 0% -> 2%
where the time goes in v2:
time: 84.5 us; the launch traced here: 84.1 us
  Pallas kernels  28.7 us (34%)
  waiting for transfers between devices  23.4 us (28%)
  local copies, waits for them, and re-layouts  11 us (13%)
  starting transfers between devices  10.8 us (13%)
  blocking collectives  9.16 us (11%)
  between operations  0.92 us (1%)
    pallas_call x1, Pallas kernels, bin_samples(): pl.pallas_call(bin_kernel, grid=(samp_dev // chunk,), out_shape=(piece, p...  14.8 us
    ppermute x5, waiting for transfers between devices, exchanged(): lax.ppermute(value, axis, [(source, source ^ bit) for source in range(cou...  11.8 us
    ppermute x6, waiting for transfers between devices, delivered(): lax.ppermute(pair, ('tm', 'det'), [(time * dets + det, (time + sign * rea...  11.6 us
    unnamed x35, local copies, waits for them, and re-layouts  10.1 us
    all_to_all x1, blocking collectives, on_device(): lax.all_to_all(parts, ('tm', 'det'), split_axis=0, concat_axis=0, tiled=T...  9.16 us
    ppermute x6, starting transfers between devices, delivered(): lax.ppermute(pair, ('tm', 'det'), [(time * dets + det, (time + sign * rea...  9 us
    pallas_call x1, Pallas kernels, make_timeline(): pl.pallas_call(timeline_kernel, grid=(samp_dev // chunk,), out_shape=(jax...  7.08 us
    pallas_call x1, Pallas kernels, update_maps(): pl.pallas_call(update_kernel, grid=(solution.shape[1] // chunk,), out_sha...  2.4 us
  transfers between devices with their start and end apart: 11, of which 8 were waited for; matrix products, arithmetic and copies ran while one was open for 2% of the time, Pallas kernels for 2%

profile of v2, /device:TPU:0, one launch (start us, length us, event | category | flops | bytes accessed | tf_op | source)
XLA Modules:
  0.0 84.1 jit_solution(3977204957907369578)
XLA Ops:
  0.6 0.0 copy-start.4
  0.6 1.1 %copy-done.4 = f32[3,384,128]{2,1,0:T(8,128)S(1)} copy-done((f32[3,384,128]{2,1,0:T(8,128)S(1)}, f32[3,384,128]{2,1,0:T(8,128)}, u32[]{:S(2)}) %copy-start.4) | copy-done | bytes 589848
  1.7 0.7 copy-done.13
  2.4 0.8 pull_blocks.1
  3.2 0.5 collective-permute-start
  3.7 0.8 copy.18.template_ref
  4.5 0.8 copy.19.weight_ref
  5.4 0.0 copy-start.15
  5.4 0.6 copy-done.15
  6.0 2.1 %mode_matrices.1 = (f32[64,16]{1,0:T(8,128)S(1)}, f32[16,64]{1,0:T(8,128)S(1)}, f32[64,1]{1,0:T(8,128)S(1)}) custom-call(s32[1]{0:T(128)} %bitcast.det_ref, f32[256,16]{1,0:T(8,128)S(1)} %copy.18.template_ref, f32[256,1]{1,0:T(8,128)S(1)} %copy.19.weight_ref, f32[1,16]{1,0:T(1,128)S(1)} %bitcast.41), custom_call_target="tpu_custom_call" | custom-call | tf_op jit(solution)/shard_map/mode_matrices/pallas_call | solution.py:159
  8.1 0.1 collective-permute-done
  8.2 2.6 %collective-permute-start.1 = (f32[2,48,128]{2,1,0:T(8,128)S(1)}, f32[2,48,128]{2,1,0:T(8,128)S(1)}, u32[]{:S(2)}, u32[]{:S(2)}) collective-permute-start(f32[2,48,128]{2,1,0:T(8,128)S(1)} %pad_maximum_fusion.2), channel_id=1, source_target_pairs={{0,2},{1,3},{2,0},{3,1},{4,6},{5,7},{6,4},{7,5},{8,10},{9,11},{10,... | collective-permute-start | bytes 147464 | tf_op jit(solution)/shard_map/ppermute | solution.py:479
  10.8 4.6 %collective-permute-start.2 = (f32[2,48,128]{2,1,0:T(8,128)S(1)}, f32[2,48,128]{2,1,0:T(8,128)S(1)}, u32[]{:S(2)}, u32[]{:S(2)}) collective-permute-start(f32[2,48,128]{2,1,0:T(8,128)S(1)} %pad_maximum_fusion.3), channel_id=1, source_target_pairs={{0,28},{1,29},{2,30},{3,31},{4,0},{5,1},{6,2},{7,3},{8,4},{9,5},{1... | collective-permute-start | bytes 147464 | tf_op jit(solution)/shard_map/ppermute | solution.py:479
  15.3 0.5 collective-permute-start.3
  15.8 0.0 collective-permute-done.1.refs_1_
  15.8 1.4 %collective-permute-done.2.refs_2_ = f32[2,48,128]{2,1,0:T(8,128)S(1)} collective-permute-done((f32[2,48,128]{2,1,0:T(8,128)S(1)}, f32[2,48,128]{2,1,0:T(8,128)S(1)}, u32[]{:S(2)}, u32[]{:S(2)}) %collective-permute-start.2) | collective-permute-done | bytes 49184 | tf_op jit(solution)/shard_map/ppermute | solution.py:479
  17.2 3.1 %collective-permute-done.3.refs_3_ = f32[2,48,128]{2,1,0:T(8,128)S(1)} collective-permute-done((f32[2,48,128]{2,1,0:T(8,128)S(1)}, f32[2,48,128]{2,1,0:T(8,128)S(1)}, u32[]{:S(2)}, u32[]{:S(2)}) %collective-permute-start.3) | collective-permute-done | bytes 49184 | tf_op jit(solution)/shard_map/ppermute | solution.py:479
  20.3 1.6 %copy-done = s32[64,8192]{1,0:T(8,128)S(1)} copy-done((s32[64,8192]{1,0:T(8,128)S(1)}, s32[64,8192]{1,0:T(8,128)}, u32[]{:S(2)}) %copy-start) | copy-done | bytes 2097176
  21.9 1.6 %copy-done.2 = s32[64,8192]{1,0:T(8,128)S(1)} copy-done((s32[64,8192]{1,0:T(8,128)S(1)}, s32[64,8192]{1,0:T(8,128)}, u32[]{:S(2)}) %copy-start.2) | copy-done | bytes 2097176
  23.5 0.8 copy-done.11
  24.3 7.1 %make_timeline.1 = (f32[64,8192]{1,0:T(8,128)S(1)}, f32[16,8192]{1,0:T(8,128)S(1)}) custom-call(s32[1]{0:T(128)} %bitcast.det_ref, s32[64,64]{1,0:T(8,128)S(1)} %copy-done.11, f32[16,64]{1,0:T(8,128)S(1)} %get-tuple-element.14.weighted_ref, s32[64,8192]{1,0:T(8,128)S(1)} %copy-done, s32[64,8192]{1,0:T(8,128)S(1)} %copy-done.2, ...), custom_call_target="tpu_custom_call" | custom-call | tf_op jit(solution)/shard_map/make_timeline/pallas_call | solution.py:227
  31.4 0.0 copy-start.8
  31.4 1.3 %copy-done.8 = f32[64,8192]{1,0:T(8,128)} copy-done((f32[64,8192]{1,0:T(8,128)}, f32[64,8192]{1,0:T(8,128)S(1)}, u32[]{:S(2)}) %copy-start.8) | copy-done | bytes 2097176
  32.7 0.1 collective-permute-start.4
  32.8 1.5 %collective-permute-done.4 = f32[16,4096]{1,0:T(8,128)S(1)} collective-permute-done((f32[16,4096]{1,0:T(8,128)S(1)}, f32[16,4096]{1,0:T(8,128)S(1)}, u32[]{:S(2)}, u32[]{:S(2)}) %collective-permute-start.4) | collective-permute-done | bytes 262176 | tf_op jit(solution)/shard_map/ppermute | solution.py:468
  34.4 0.6 collective-permute-start.5
  35.0 7.8 %collective-permute-done.5 = f32[16,4096]{1,0:T(8,128)S(1)} collective-permute-done((f32[16,4096]{1,0:T(8,128)S(1)}, f32[16,4096]{1,0:T(8,128)S(1)}, u32[]{:S(2)}, u32[]{:S(2)}) %collective-permute-start.5) | collective-permute-done | bytes 262176 | tf_op jit(solution)/shard_map/ppermute | solution.py:468
  42.8 0.1 collective-permute-start.6
  42.9 0.0 copy-start.3
  42.9 1.5 %collective-permute-done.6 = f32[16,4096]{1,0:T(8,128)S(1)} collective-permute-done((f32[16,4096]{1,0:T(8,128)S(1)}, f32[16,4096]{1,0:T(8,128)S(1)}, u32[]{:S(2)}, u32[]{:S(2)}) %collective-permute-start.6) | collective-permute-done | bytes 262176 | tf_op jit(solution)/shard_map/ppermute | solution.py:468
  44.5 0.0 copy-done.16
  44.5 0.0 copy-done.12
  44.5 0.0 copy-done.1
  44.6 0.0 copy-done.3
  44.6 1.6 %copy-done.9 = f32[64,8192]{1,0:T(8,128)S(1)} copy-done((f32[64,8192]{1,0:T(8,128)S(1)}, f32[64,8192]{1,0:T(8,128)}, u32[]{:S(2)}) %copy-start.9) | copy-done | bytes 2097176
  46.2 14.8 %bin_samples.1 = (f32[2,2,48,128]{3,2,1,0:T(8,128)S(1)}, f32[2,2,48,128]{3,2,1,0:T(8,128)S(1)}) custom-call(s32[1]{0:T(128)} %bitcast.det_ref, s32[64,64]{1,0:T(8,128)S(1)} %copy-done.12, f32[16,8192]{1,0:T(8,128)S(1)} %pad_maximum_fusion.proj_ref, f32[8,128]{1,0:T(8,128)S(1)} %jit_solution_.3.trig_ref, f32[64,16]{1,0:T(8,128)S(1)} %get-tuple-element.18.back_ref, ...), custom_call_target="tpu_custom_call" | custom-call | tf_op jit(solution)/shard_map/bin_samples/pallas_call | solution.py:350
  61.0 0.0 copy-start.10
  61.0 0.5 collective-permute-start.7
  61.5 0.9 %collective-permute-done.7 = f32[2,2,48,128]{3,2,1,0:T(8,128)S(1)} collective-permute-done((f32[2,2,48,128]{3,2,1,0:T(8,128)S(1)}, f32[2,2,48,128]{3,2,1,0:T(8,128)S(1)}, u32[]{:S(2)}, u32[]{:S(2)}) %collective-permute-start.7) | collective-permute-done | bytes 98336 | tf_op jit(solution)/shard_map/ppermute | solution.py:468
  62.4 0.1 collective-permute-start.10
  62.5 0.1 collective-permute-start.9
  62.6 1.3 %collective-permute-start.8 = (f32[2,48,128]{2,1,0:T(8,128)S(1)}, f32[2,48,128]{2,1,0:T(8,128)S(1)}, u32[]{:S(2)}, u32[]{:S(2)}) collective-permute-start(f32[2,48,128]{2,1,0:T(8,128)S(1)} %pad_maximum_fusion.6), channel_id=1, source_target_pairs={{0,2},{1,3},{2,0},{3,1},{4,6},{5,7},{6,4},{7,5},{8,10},{9,11},{10,... | collective-permute-start | bytes 147464 | tf_op jit(solution)/shard_map/ppermute | solution.py:479
  63.9 7.1 %collective-permute-done.10.refs_3_ = f32[2,48,128]{2,1,0:T(8,128)S(1)} collective-permute-done((f32[2,48,128]{2,1,0:T(8,128)S(1)}, f32[2,48,128]{2,1,0:T(8,128)S(1)}, u32[]{:S(2)}, u32[]{:S(2)}) %collective-permute-start.10) | collective-permute-done | bytes 49184 | tf_op jit(solution)/shard_map/ppermute | solution.py:479
  70.9 0.0 collective-permute-done.9.refs_2_
  70.9 0.0 collective-permute-done.8.refs_1_
  71.0 1.6 %push_blocks.1 = (f32[3,384,128]{2,1,0:T(8,128)S(1)}, f32[32,128]{1,0:T(8,128)S(1)}) custom-call(s32[1]{0:T(128)} %bitcast.det_ref, s32[1,1,2,4,16]{4,3,2,1,0:T(4,128)S(1)} %copy-done.14, f32[3,384,128]{2,1,0:T(8,128)S(1)} %copy-done.5, f32[3,384,128]{2,1,0:T(8,128)S(1)} %copy-done.7, f32[6,384,128]{2,1,0:T(8,128)S(1)} %copy-done.6, ...), custom_call_target="tpu_custom_call" | custom-call | tf_op jit(solution)/shard_map/push_blocks/pallas_call | solution.py:415
  72.5 9.2 %all_to_all.11 = f32[32,1,128]{2,1,0:T(1,128)S(1)} all-to-all(f32[32,1,128]{2,1,0:T(1,128)S(1)} %bitcast.40), channel_id=1, replica_groups=mesh['tm'=8,'det'=4] {'tm','det'}, dimensions={0} | all-to-all | bytes 32768 | tf_op jit(solution)/shard_map/all_to_all | solution.py:541
  81.7 2.4 %update_maps.1 = (f32[3,384,128]{2,1,0:T(8,128)}, f32[3,384,128]{2,1,0:T(8,128)}, f32[3,384,128]{2,1,0:T(8,128)}) custom-call(f32[32,128]{1,0:T(8,128)S(1)} %bitcast.39, f32[3,384,128]{2,1,0:T(8,128)S(1)} %copy-done.10, f32[3,384,128]{2,1,0:T(8,128)S(1)} %copy-done.7, f32[3,384,128]{2,1,0:T(8,128)S(1)} %copy-done.5, ...), custom_call_target="tpu_custom_call" | custom-call | tf_op jit(solution)/shard_map/update_maps/pallas_call | solution.py:455
  (35 shorter events, 0.3 us)
Async XLA Ops:
  0.6 1.1 %copy-start.4 = (f32[3,384,128]{2,1,0:T(8,128)S(1)}, f32[3,384,128]{2,1,0:T(8,128)}, u32[]{:S(2)}) copy-start(f32[3,384,128]{2,1,0:T(8,128)} %direction_ref.5) | copy-start | bytes 1769476
  1.7 0.7 copy-start.13
  3.2 4.9 %collective-permute-start = (f32[2,2,48,128]{3,2,1,0:T(8,128)S(1)}, f32[2,2,48,128]{3,2,1,0:T(8,128)S(1)}, u32[]{:S(2)}, u32[]{:S(2)}) collective-permute-start(f32[2,2,48,128]{3,2,1,0:T(8,128)S(1)} %get-tuple-element.16), channel_id=1, source_target_pairs={{0,1},{1,0},{2,3},{3,2},{4,5},{5,4},{6,7},{7,6},{8,9},{9,8},{10,11... | collective-permute-start | bytes 294920 | tf_op jit(solution)/shard_map/ppermute | solution.py:468
  5.4 0.7 copy-start.15
  8.2 7.6 %collective-permute-start.1 = (f32[2,48,128]{2,1,0:T(8,128)S(1)}, f32[2,48,128]{2,1,0:T(8,128)S(1)}, u32[]{:S(2)}, u32[]{:S(2)}) collective-permute-start(f32[2,48,128]{2,1,0:T(8,128)S(1)} %pad_maximum_fusion.2), channel_id=1, source_target_pairs={{0,2},{1,3},{2,0},{3,1},{4,6},{5,7},{6,4},{7,5},{8,10},{9,11},{10,... | collective-permute-start | bytes 147464 | tf_op jit(solution)/shard_map/ppermute | solution.py:479
  10.8 6.4 %collective-permute-start.2 = (f32[2,48,128]{2,1,0:T(8,128)S(1)}, f32[2,48,128]{2,1,0:T(8,128)S(1)}, u32[]{:S(2)}, u32[]{:S(2)}) collective-permute-start(f32[2,48,128]{2,1,0:T(8,128)S(1)} %pad_maximum_fusion.3), channel_id=1, source_target_pairs={{0,28},{1,29},{2,30},{3,31},{4,0},{5,1},{6,2},{7,3},{8,4},{9,5},{1... | collective-permute-start | bytes 147464 | tf_op jit(solution)/shard_map/ppermute | solution.py:479
  15.3 5.0 %collective-permute-start.3 = (f32[2,48,128]{2,1,0:T(8,128)S(1)}, f32[2,48,128]{2,1,0:T(8,128)S(1)}, u32[]{:S(2)}, u32[]{:S(2)}) collective-permute-start(f32[2,48,128]{2,1,0:T(8,128)S(1)} %pad_maximum_fusion.4), channel_id=1, source_target_pairs={{0,30},{1,31},{2,28},{3,29},{4,2},{5,3},{6,0},{7,1},{8,6},{9,7},{1... | collective-permute-start | bytes 147464 | tf_op jit(solution)/shard_map/ppermute | solution.py:479
  20.3 1.6 %copy-start = (s32[64,8192]{1,0:T(8,128)S(1)}, s32[64,8192]{1,0:T(8,128)}, u32[]{:S(2)}) copy-start(s32[64,8192]{1,0:T(8,128)} %offset_ref.3) | copy-start | bytes 6291460
  21.9 1.6 %copy-start.2 = (s32[64,8192]{1,0:T(8,128)S(1)}, s32[64,8192]{1,0:T(8,128)}, u32[]{:S(2)}) copy-start(s32[64,8192]{1,0:T(8,128)} %angle_ref.3) | copy-start | bytes 6291460
  23.5 0.8 copy-start.11
  24.3 20.3 %copy-start.12 = (s32[64,64]{1,0:T(8,128)S(1)}, s32[64,64]{1,0:T(8,128)}, u32[]{:S(2)}) copy-start(s32[64,64]{1,0:T(8,128)} %slot_ref.3) | copy-start | bytes 49156
  31.4 1.4 %copy-start.8 = (f32[64,8192]{1,0:T(8,128)}, f32[64,8192]{1,0:T(8,128)S(1)}, u32[]{:S(2)}) copy-start(f32[64,8192]{1,0:T(8,128)S(1)} %get-tuple-element.20.time_ref) | copy-start | bytes 6291460
  32.7 11.8 %copy-start.16 = (f32[128]{0:T(128)S(1)}, f32[128]{0:T(128)}, u32[]{:S(2)}) copy-start(f32[128]{0:T(128)} %constant.25.clone) | copy-start | bytes 1540
  32.7 11.8 %copy-start.1 = (s32[64,8192]{1,0:T(8,128)S(1)}, s32[64,8192]{1,0:T(8,128)}, u32[]{:S(2)}) copy-start(s32[64,8192]{1,0:T(8,128)} %offset_ref.3) | copy-start | bytes 6291460
  32.7 1.6 %collective-permute-start.4 = (f32[16,4096]{1,0:T(8,128)S(1)}, f32[16,4096]{1,0:T(8,128)S(1)}, u32[]{:S(2)}, u32[]{:S(2)}) collective-permute-start(f32[16,4096]{1,0:T(8,128)S(1)} %constant_dynamic-slice_fusion), channel_id=1, source_target_pairs={{0,1},{1,0},{2,3},{3,2},{4,5},{5,4},{6,7},{7,6},{8,9},{9,8},{10,11... | collective-permute-start | bytes 786440 | tf_op jit(solution)/shard_map/ppermute | solution.py:468
  34.4 8.4 %collective-permute-start.5 = (f32[16,4096]{1,0:T(8,128)S(1)}, f32[16,4096]{1,0:T(8,128)S(1)}, u32[]{:S(2)}, u32[]{:S(2)}) collective-permute-start(f32[16,4096]{1,0:T(8,128)S(1)} %dynamic-slice_add_fusion), channel_id=1, source_target_pairs={{0,2},{1,3},{2,0},{3,1},{4,6},{5,7},{6,4},{7,5},{8,10},{9,11},{10,... | collective-permute-start | bytes 786440 | tf_op jit(solution)/shard_map/ppermute | solution.py:468
  42.8 1.6 %collective-permute-start.6 = (f32[16,4096]{1,0:T(8,128)S(1)}, f32[16,4096]{1,0:T(8,128)S(1)}, u32[]{:S(2)}, u32[]{:S(2)}) collective-permute-start(f32[16,4096]{1,0:T(8,128)S(1)} %add.20), channel_id=1, source_target_pairs={{0,1},{1,0},{2,3},{3,2},{4,5},{5,4},{6,7},{7,6},{8,9},{9,8},{10,11... | collective-permute-start | bytes 786440 | tf_op jit(solution)/shard_map/ppermute | solution.py:468
  42.9 1.6 %copy-start.3 = (s32[64,8192]{1,0:T(8,128)S(1)}, s32[64,8192]{1,0:T(8,128)}, u32[]{:S(2)}) copy-start(s32[64,8192]{1,0:T(8,128)} %angle_ref.3) | copy-start | bytes 6291460
  44.6 1.6 %copy-start.9 = (f32[64,8192]{1,0:T(8,128)S(1)}, f32[64,8192]{1,0:T(8,128)}, u32[]{:S(2)}) copy-start(f32[64,8192]{1,0:T(8,128)} %copy-done.8) | copy-start | bytes 6291460
  46.2 24.8 %copy-start.5 = (f32[3,384,128]{2,1,0:T(8,128)S(1)}, f32[3,384,128]{2,1,0:T(8,128)}, u32[]{:S(2)}) copy-start(f32[3,384,128]{2,1,0:T(8,128)} %direction_ref.5) | copy-start | bytes 1769476
  46.2 24.8 %copy-start.6 = (f32[6,384,128]{2,1,0:T(8,128)S(1)}, f32[6,384,128]{2,1,0:T(8,128)}, u32[]{:S(2)}) copy-start(f32[6,384,128]{2,1,0:T(8,128)} %pre_ref.3) | copy-start | bytes 3538948
  46.2 24.8 %copy-start.7 = (f32[3,384,128]{2,1,0:T(8,128)S(1)}, f32[3,384,128]{2,1,0:T(8,128)}, u32[]{:S(2)}) copy-start(f32[3,384,128]{2,1,0:T(8,128)} %residual_ref.3) | copy-start | bytes 1769476
  46.2 24.8 %copy-start.14 = (s32[1,1,2,4,16]{4,3,2,1,0:T(4,128)S(1)}, s32[1,1,2,4,16]{4,3,2,1,0:T(4,128)}, u32[]{:S(2)}) copy-start(s32[1,1,2,4,16]{4,3,2,1,0:T(4,128)} %request_ref.3) | copy-start | bytes 1540
  61.0 20.7 %copy-start.10 = (f32[3,384,128]{2,1,0:T(8,128)S(1)}, f32[3,384,128]{2,1,0:T(8,128)}, u32[]{:S(2)}) copy-start(f32[3,384,128]{2,1,0:T(8,128)} %solution_ref.1) | copy-start | bytes 1769476
  61.0 1.4 %collective-permute-start.7 = (f32[2,2,48,128]{3,2,1,0:T(8,128)S(1)}, f32[2,2,48,128]{3,2,1,0:T(8,128)S(1)}, u32[]{:S(2)}, u32[]{:S(2)}) collective-permute-start(f32[2,2,48,128]{3,2,1,0:T(8,128)S(1)} %get-tuple-element.22), channel_id=1, source_target_pairs={{0,1},{1,0},{2,3},{3,2},{4,5},{5,4},{6,7},{7,6},{8,9},{9,8},{10,11... | collective-permute-start | bytes 294920 | tf_op jit(solution)/shard_map/ppermute | solution.py:468
  62.4 8.5 %collective-permute-start.10 = (f32[2,48,128]{2,1,0:T(8,128)S(1)}, f32[2,48,128]{2,1,0:T(8,128)S(1)}, u32[]{:S(2)}, u32[]{:S(2)}) collective-permute-start(f32[2,48,128]{2,1,0:T(8,128)S(1)} %pad_maximum_fusion.8), channel_id=1, source_target_pairs={{0,6},{1,7},{2,4},{3,5},{4,10},{5,11},{6,8},{7,9},{8,14},{9,15},{1... | collective-permute-start | bytes 147464 | tf_op jit(solution)/shard_map/ppermute | solution.py:479
  62.5 8.4 %collective-permute-start.9 = (f32[2,48,128]{2,1,0:T(8,128)S(1)}, f32[2,48,128]{2,1,0:T(8,128)S(1)}, u32[]{:S(2)}, u32[]{:S(2)}) collective-permute-start(f32[2,48,128]{2,1,0:T(8,128)S(1)} %pad_maximum_fusion.7), channel_id=1, source_target_pairs={{0,4},{1,5},{2,6},{3,7},{4,8},{5,9},{6,10},{7,11},{8,12},{9,13},{1... | collective-permute-start | bytes 147464 | tf_op jit(solution)/shard_map/ppermute | solution.py:479
  62.6 8.3 %collective-permute-start.8 = (f32[2,48,128]{2,1,0:T(8,128)S(1)}, f32[2,48,128]{2,1,0:T(8,128)S(1)}, u32[]{:S(2)}, u32[]{:S(2)}) collective-permute-start(f32[2,48,128]{2,1,0:T(8,128)S(1)} %pad_maximum_fusion.6), channel_id=1, source_target_pairs={{0,2},{1,3},{2,0},{3,1},{4,6},{5,7},{6,4},{7,5},{8,10},{9,11},{10,... | collective-permute-start | bytes 147464 | tf_op jit(solution)/shard_map/ppermute | solution.py:479

commit v3 on v2

--- a/solution.py
+++ b/solution.py
@@ -32,6 +32,10 @@
     return pl.BlockSpec(memory_space=pltpu.SMEM)
 
 
+def in_hbm(*arrays):
+    return tuple(pltpu.with_memory_space_constraint(array, pltpu.HBM) for array in arrays)
+
+
 def params(mib):
     return pltpu.CompilerParams(vmem_limit_bytes=mib * MIB)
 
@@ -59,9 +63,9 @@
 
 
 def trig_table():
-    angles = (np.arange(NANG, dtype=np.float32) * np.float32(2.0 * math.pi / NANG)).astype(np.float64)
-    row = np.concatenate([np.cos(angles), np.sin(angles)]).astype(np.float32)
-    return jnp.asarray(np.broadcast_to(row[None, :], (GROUP, PB)))
+    lane = lax.broadcasted_iota(jnp.int32, (GROUP, PB), 1)
+    cos_vals, sin_vals = waves(lane & (NANG - 1))
+    return jnp.where(lane < NANG, cos_vals, sin_vals)
 
 
 def halves(value):
@@ -118,26 +122,30 @@
         out_shape=(piece, piece),
         in_specs=[smem_spec(), smem_spec(), vmem_spec()],
         out_specs=(vmem_spec(), vmem_spec()),
-        compiler_params=params(8),
+        compiler_params=params(24),
         name="pull_blocks",
-    )(det, pull_index, direction)
-
-
-def mode_kernel(det_ref, template_ref, weight_ref, precision_ref, back_ref, weighted_ref, own_weight_ref):
+    )(det, *in_hbm(pull_index, direction))
+
+
+def own_lanes(ref, first, count):
+    rows, total = ref.shape
+    value = jnp.broadcast_to(ref[...], (max(rows, ROWS), total))
+    return pltpu.roll(value, lax.rem(total - first, total), 1)[:, :count]
+
+
+def mode_kernel(det_ref, template_ref, weight_ref, precision_ref, after_ref, back_ref, own_weight_ref):
+    del after_ref
     det_dev = back_ref.shape[0]
-    modes = template_ref.shape[1]
+    modes = template_ref.shape[0]
     templates = template_ref[...]
-    weight = weight_ref[...]
-    first = pl.multiple_of(det_ref[0] * det_dev, det_dev)
-    own_templates = template_ref[pl.ds(first, det_dev), :]
-    own_weight = weight_ref[pl.ds(first, det_dev), :]
-    own_weight_ref[...] = own_weight
-    weighted_ref[...] = (own_templates * own_weight).T
+    first = det_ref[0] * det_dev
+    own_templates = own_lanes(template_ref, first, det_dev)
+    own_weight_ref[...] = own_lanes(weight_ref, first, det_dev).T[:, :1]
     row = lax.broadcasted_iota(jnp.int32, (modes, modes), 0)
     column = lax.broadcasted_iota(jnp.int32, (modes, modes), 1)
     unit = (row == column).astype(F32)
     core = unit * precision_ref[...] + lax.dot_general(
-        weight * templates, templates, (((0,), (0,)), ((), ())), precision=HIGHEST, preferred_element_type=F32
+        templates * weight_ref[:1, :], templates, (((1,), (1,)), ((), ())), precision=HIGHEST, preferred_element_type=F32
     )
     inverse = unit
     line = lax.broadcasted_iota(jnp.int32, (modes, 1), 0)
@@ -151,27 +159,26 @@
     solved = lax.dot_general(
         inverse, inverse, (((0,), (0,)), ((), ())), precision=HIGHEST, preferred_element_type=F32
     )
-    back_ref[...] = jnp.dot(own_templates, solved, precision=HIGHEST, preferred_element_type=F32)
-
-
-def mode_matrices(det, det_dev, mode_templates, det_weight, mode_precision):
-    modes = mode_templates.shape[1]
+    back_ref[...] = jnp.dot(solved, own_templates, precision=HIGHEST, preferred_element_type=F32).T
+
+
+def mode_matrices(det, det_dev, templates, weight, mode_precision, after):
+    modes = templates.shape[0]
     return pl.pallas_call(
         mode_kernel,
         out_shape=(
             jax.ShapeDtypeStruct((det_dev, modes), F32),
-            jax.ShapeDtypeStruct((modes, det_dev), F32),
             jax.ShapeDtypeStruct((det_dev, 1), F32),
         ),
-        in_specs=[smem_spec(), vmem_spec(), vmem_spec(), vmem_spec()],
-        out_specs=(vmem_spec(), vmem_spec(), vmem_spec()),
+        in_specs=[smem_spec(), vmem_spec(), vmem_spec(), vmem_spec(), pl.BlockSpec(memory_space=pl.ANY)],
+        out_specs=(vmem_spec(), vmem_spec()),
         compiler_params=params(8),
         name="mode_matrices",
-    )(det, mode_templates, det_weight[:, None], mode_precision[None, :])
-
-
-def timeline_kernel(det_ref, slot_ref, weighted_ref, offset_ref, angle_ref, *refs):
-    *piece_refs, time_ref, proj_ref, map_ref, table_ref = refs
+    )(det, *in_hbm(templates, weight, mode_precision[None, :]), after)
+
+
+def timeline_kernel(det_ref, slot_ref, template_ref, weight_ref, offset_ref, angle_ref, *refs):
+    *piece_refs, time_ref, proj_ref, map_ref, table_ref, weighted_ref = refs
     step = pl.program_id(0)
     cap_count = piece_refs[0].shape[1] // 3
     hop_count = len(piece_refs) // 2
@@ -181,6 +188,8 @@
     @pl.when(step == 0)
     def _():
         det = det_ref[0]
+        first = det * det_count
+        weighted_ref[...] = own_lanes(template_ref, first, det_count) * own_lanes(weight_ref, first, det_count)[:1, :]
         for place, ref in enumerate(piece_refs):
             reach, hop = place // hop_count, place % hop_count
             for flip in range(2):
@@ -218,9 +227,9 @@
     )
 
 
-def make_timeline(det, block_slot, weighted, pixel_offset, angle_index, pieces, chunk):
+def make_timeline(det, block_slot, templates, weight, pixel_offset, angle_index, pieces, chunk):
     det_dev, samp_dev = pixel_offset.shape
-    modes = weighted.shape[0]
+    modes = templates.shape[0]
     slot_total = len(pieces) * 2 * (pieces[0].shape[1] // 3)
     runs = chunk // RUN_LEN
     wide = pl.BlockSpec((det_dev, chunk), lambda i: (0, i))
@@ -228,22 +237,23 @@
         timeline_kernel,
         grid=(samp_dev // chunk,),
         out_shape=(
-            jax.ShapeDtypeStruct((det_dev, samp_dev), F32),
+            pltpu.HBM((det_dev, samp_dev), F32),
             jax.ShapeDtypeStruct((modes, samp_dev), F32),
         ),
-        in_specs=[smem_spec(), smem_spec(), vmem_spec(), wide, wide] + [vmem_spec()] * len(pieces),
+        in_specs=[smem_spec(), smem_spec(), vmem_spec(), vmem_spec(), wide, wide] + [vmem_spec()] * len(pieces),
         out_specs=(wide, pl.BlockSpec((modes, chunk), lambda i: (0, i))),
         scratch_shapes=[
             pltpu.VMEM((slot_total * ROWS, PB), F32),
             pltpu.VMEM((runs, GROUP * ROWS, PB), F32),
+            pltpu.VMEM((modes, det_dev), F32),
         ],
-        compiler_params=params(16),
+        compiler_params=params(24),
         name="make_timeline",
-    )(det, block_slot, weighted, pixel_offset, angle_index, *pieces)
+    )(det, *in_hbm(block_slot, templates, weight, pixel_offset, angle_index), *pieces)
 
 
 def bin_kernel(
-    det_ref, slot_ref, proj_ref, trig_ref, back_ref, weight_ref, offset_ref, angle_ref, time_ref,
+    det_ref, slot_ref, proj_ref, back_ref, weight_ref, offset_ref, angle_ref, time_ref,
     own_ref, other_ref, map_ref, row_ref, filt_ref,
 ):
     step = pl.program_id(0)
@@ -266,12 +276,12 @@
         preferred_element_type=F32,
     )
     filt_ref[...] = weight_ref[...] * (time_ref[...] - common)
-    trig = trig_ref[...]
+    trig = trig_table()
     det_iota = lax.broadcasted_iota(jnp.int32, (GROUP, RUN_LEN), 0)
     low_iota = lax.broadcasted_iota(jnp.int32, (LOW, RUN_LEN), 0).astype(F32).astype(BF16)
     row_iota = lax.broadcasted_iota(jnp.int32, (GROUP, PB), 0)
     lane_iota = lax.broadcasted_iota(jnp.int32, (GROUP, PB), 1)
-    own_lanes = lane_iota // LOW == row_iota % HIGH
+    diagonal = lane_iota // LOW == row_iota % HIGH
     zero = jnp.zeros((), BF16)
     one = jnp.ones((), BF16)
 
@@ -310,7 +320,7 @@
                     top = (j * 3 + k) * 2 * GROUP
                     pair = product[top : top + GROUP] + product[top + GROUP : top + 2 * GROUP]
                     part = jnp.where(row_iota < HIGH, pair[:, :PB], pair[:, PB:])
-                    part = jnp.where(own_lanes, part, 0.0)
+                    part = jnp.where(diagonal, part, 0.0)
                     if j:
                         part = pltpu.roll(part, LOW * j, 1)
                     total = part if total is None else total + part
@@ -338,7 +348,7 @@
 
 
 def bin_samples(
-    det, block_slot, projection, trig, back, weight, pixel_offset, angle_index, timeline, shape, chunk
+    det, block_slot, projection, back, weight, pixel_offset, angle_index, timeline, shape, chunk
 ):
     det_dev, samp_dev = pixel_offset.shape
     modes = projection.shape[0]
@@ -352,7 +362,7 @@
         grid=(samp_dev // chunk,),
         out_shape=(piece, piece),
         in_specs=[smem_spec(), smem_spec(), pl.BlockSpec((modes, chunk), lambda i: (0, i))]
-        + [vmem_spec()] * 3
+        + [vmem_spec()] * 2
         + [wide, wide, wide],
         out_specs=(vmem_spec(), vmem_spec()),
         scratch_shapes=[
@@ -362,7 +372,9 @@
         ],
         compiler_params=params(24),
         name="bin_samples",
-    )(det, block_slot, projection, trig, back, weight, pixel_offset, angle_index, timeline)
+    )(
+        det, *in_hbm(block_slot), projection, back, weight, *in_hbm(pixel_offset, angle_index, timeline)
+    )
 
 
 def push_kernel(det_ref, request_ref, direction_ref, residual_ref, pre_ref, *refs):
@@ -435,28 +447,31 @@
     size = jnp.broadcast_to(size, (ROWS, PB))
     ratio = jnp.broadcast_to(ratio, (ROWS, PB))
 
+    chunk = new_solution_ref.shape[1]
+    start = pl.program_id(0) * chunk
+
     def body(index, carry):
-        rows = pl.ds(pl.multiple_of(index * ROWS, ROWS), ROWS)
+        rows = pl.ds(pl.multiple_of(start + index * ROWS, ROWS), ROWS)
+        here = pl.ds(pl.multiple_of(index * ROWS, ROWS), ROWS)
         line = [direction_ref[k, rows, :] for k in range(3)]
         new = [residual_ref[k, rows, :] - size * operated_ref[k, rows, :] for k in range(3)]
         applied = precondition([pre_ref[entry, rows, :] for entry in range(6)], new)
         for k in range(3):
-            new_solution_ref[k, rows, :] = solution_ref[k, rows, :] + size * line[k]
-            new_residual_ref[k, rows, :] = new[k]
-            new_direction_ref[k, rows, :] = applied[k] + ratio * line[k]
+            new_solution_ref[k, here, :] = solution_ref[k, rows, :] + size * line[k]
+            new_residual_ref[k, here, :] = new[k]
+            new_direction_ref[k, here, :] = applied[k] + ratio * line[k]
         return carry
 
-    lax.fori_loop(0, solution_ref.shape[1] // ROWS, body, 0, unroll=4)
+    lax.fori_loop(0, chunk // ROWS, body, 0, unroll=4)
 
 
 def update_maps(parts, solution, residual, direction, operated, preconditioner, chunk):
     maps = pl.BlockSpec((3, chunk, PB), lambda i: (0, i, 0))
-    wide = pl.BlockSpec((6, chunk, PB), lambda i: (0, i, 0))
     return pl.pallas_call(
         update_kernel,
         grid=(solution.shape[1] // chunk,),
         out_shape=(jax.ShapeDtypeStruct(solution.shape, F32),) * 3,
-        in_specs=[vmem_spec()] + [maps] * 4 + [wide],
+        in_specs=[vmem_spec()] * 6,
         out_specs=(maps,) * 3,
         compiler_params=params(16),
         name="update_maps",
@@ -489,7 +504,7 @@
     return pieces
 
 
-def summed_over_det(value):
+def summed_over_det(value, beside):
     count = lax.axis_size("det")
     half = value.shape[1] // 2
     core = lax.axis_index("det") % 2
@@ -500,10 +515,11 @@
     while bit < count:
         own = own + exchanged(own, "det", bit)
         bit *= 2
+    own, beside = lax.optimization_barrier((own, beside))
     other = exchanged(own, "det", 1)
     lower = jnp.where(core == 0, own, other)
     upper = jnp.where(core == 0, other, own)
-    return jnp.concatenate([lower, upper], axis=1)
+    return jnp.concatenate([lower, upper], axis=1), beside
 
 
 def on_device(
@@ -522,16 +538,18 @@
     det_dev = pixel_offset.shape[0]
     device_count = lax.axis_size("tm") * lax.axis_size("det")
     det = lax.axis_index("det").astype(jnp.int32)[None]
+    templates = mode_templates.T
+    weight = det_weight[None, :]
 
     own, other = pull_blocks(det, pull_index, direction)
     pieces = delivered(own, other, -1)
-    back, weighted, own_weight = mode_matrices(det, det_dev, mode_templates, det_weight, mode_precision)
     timeline, local_proj = make_timeline(
-        det, block_slot, weighted, pixel_offset, angle_index, pieces, 2048
-    )
-    projection = summed_over_det(local_proj)
+        det, block_slot, templates, weight, pixel_offset, angle_index, pieces, 2048
+    )
+    matrices = mode_matrices(det, det_dev, templates, weight, mode_precision, local_proj)
+    projection, (back, own_weight) = summed_over_det(local_proj, matrices)
     own, other = bin_samples(
-        det, block_slot, projection, trig_table(), back, own_weight, pixel_offset, angle_index, timeline,
+        det, block_slot, projection, back, own_weight, pixel_offset, angle_index, timeline,
         pull_index.shape[2:], 1024,
     )
     arrived = delivered(own, other, 1)

time: 84.5 us -> 73.2 us (0.87)
  local copies, waits for them, and re-layouts: 11 us -> 0.08 us
  waiting for transfers between devices: 23.4 us -> 19.1 us
  starting transfers between devices: 10.8 us -> 12.5 us
  Pallas kernels: 28.7 us -> 30.2 us
  blocking collectives: 9.16 us -> 10.1 us
    unnamed x35 -> x10, local copies, waits for them, and re-layouts: 10.1 us -> 0.03 us
    ppermute x6, waiting for transfers between devices: 11.6 us -> 8.92 us  [delivered(): lax.ppermute(pair, ('tm', 'det'), [(time * dets + det, (time + sign * rea...]
    ppermute x6, starting transfers between devices: 9 us -> 11 us  [delivered(): lax.ppermute(pair, ('tm', 'det'), [(time * dets + det, (time + sign * rea...]
    ppermute x5, waiting for transfers between devices: 11.8 us -> 10.2 us  [exchanged(): lax.ppermute(value, axis, [(source, source ^ bit) for source in range(cou...]
    all_to_all x1, blocking collectives: 9.16 us -> 10.1 us  [on_device(): lax.all_to_all(parts, ('tm', 'det'), split_axis=0, concat_axis=0, tiled=T...]
  transfers between devices with their start and end apart: 11 -> 11, of which waited for: 8 -> 10; matrix products, arithmetic and copies ran while one was open for 2% -> 0% of each run, Pallas kernels for 2% -> 4%
where the time goes in v3:
time: 73.2 us; the launch traced here: 73 us
  Pallas kernels  30.2 us (41%)
  waiting for transfers between devices  19.1 us (26%)
  starting transfers between devices  12.5 us (17%)
  blocking collectives  10.1 us (14%)
  between operations  0.8 us (1%)
    pallas_call x1, Pallas kernels, bin_samples(): pl.pallas_call(bin_kernel, grid=(samp_dev // chunk,), out_shape=(piece, p...  14.8 us
    ppermute x6, starting transfers between devices, delivered(): lax.ppermute(pair, ('tm', 'det'), [(time * dets + det, (time + sign * rea...  11 us
    ppermute x5, waiting for transfers between devices, exchanged(): lax.ppermute(value, axis, [(source, source ^ bit) for source in range(cou...  10.2 us
    all_to_all x1, blocking collectives, on_device(): lax.all_to_all(parts, ('tm', 'det'), split_axis=0, concat_axis=0, tiled=T...  10.1 us
    ppermute x6, waiting for transfers between devices, delivered(): lax.ppermute(pair, ('tm', 'det'), [(time * dets + det, (time + sign * rea...  8.92 us
    pallas_call x1, Pallas kernels, make_timeline(): pl.pallas_call(timeline_kernel, grid=(samp_dev // chunk,), out_shape=(plt...  7.67 us
    pallas_call x1, Pallas kernels, mode_matrices(): pl.pallas_call(mode_kernel, out_shape=(jax.ShapeDtypeStruct((det_dev, mod...  2.72 us
    pallas_call x1, Pallas kernels, update_maps(): pl.pallas_call(update_kernel, grid=(solution.shape[1] // chunk,), out_sha...  2.18 us
  transfers between devices with their start and end apart: 11, of which 10 were waited for; matrix products, arithmetic and copies ran while one was open for 0% of the time, Pallas kernels for 4%

profile of v3, /device:TPU:0, one launch (start us, length us, event | category | flops | bytes accessed | tf_op | source)
XLA Modules:
  0.0 73.0 jit_solution(5247920067520440413)
XLA Ops:
  0.6 1.3 %pull_blocks.1 = (f32[2,2,48,128]{3,2,1,0:T(8,128)S(1)}, f32[2,2,48,128]{3,2,1,0:T(8,128)S(1)}) custom-call(s32[1]{0:T(128)} %bitcast.det_ref, s32[1,1,2,4,16]{4,3,2,1,0:T(4,128)} %request_ref.3, f32[3,384,128]{2,1,0:T(8,128)} %direction_ref.5), custom_call_target="tpu_custom_call" | custom-call | tf_op jit(solution)/shard_map/pull_blocks/pallas_call | solution.py:120
  1.9 0.5 collective-permute-start
  2.5 0.9 %collective-permute-done = f32[2,2,48,128]{3,2,1,0:T(8,128)S(1)} collective-permute-done((f32[2,2,48,128]{3,2,1,0:T(8,128)S(1)}, f32[2,2,48,128]{3,2,1,0:T(8,128)S(1)}, u32[]{:S(2)}, u32[]{:S(2)}) %collective-permute-start) | collective-permute-done | bytes 98336 | tf_op jit(solution)/shard_map/ppermute | solution.py:483
  3.4 6.9 %collective-permute-start.3 = (f32[2,48,128]{2,1,0:T(8,128)S(1)}, f32[2,48,128]{2,1,0:T(8,128)S(1)}, u32[]{:S(2)}, u32[]{:S(2)}) collective-permute-start(f32[2,48,128]{2,1,0:T(8,128)S(1)} %pad_maximum_fusion.4), channel_id=1, source_target_pairs={{0,30},{1,31},{2,28},{3,29},{4,2},{5,3},{6,0},{7,1},{8,6},{9,7},{1... | collective-permute-start | bytes 147464 | tf_op jit(solution)/shard_map/ppermute | solution.py:494
  10.3 0.5 collective-permute-start.2
  10.8 0.5 collective-permute-start.1
  11.4 0.8 %collective-permute-done.3.refs_3_ = f32[2,48,128]{2,1,0:T(8,128)S(1)} collective-permute-done((f32[2,48,128]{2,1,0:T(8,128)S(1)}, f32[2,48,128]{2,1,0:T(8,128)S(1)}, u32[]{:S(2)}, u32[]{:S(2)}) %collective-permute-start.3) | collective-permute-done | bytes 49184 | tf_op jit(solution)/shard_map/ppermute | solution.py:494
  12.1 2.3 %collective-permute-done.2.refs_2_ = f32[2,48,128]{2,1,0:T(8,128)S(1)} collective-permute-done((f32[2,48,128]{2,1,0:T(8,128)S(1)}, f32[2,48,128]{2,1,0:T(8,128)S(1)}, u32[]{:S(2)}, u32[]{:S(2)}) %collective-permute-start.2) | collective-permute-done | bytes 49184 | tf_op jit(solution)/shard_map/ppermute | solution.py:494
  14.4 0.5 collective-permute-done.1.refs_1_
  14.9 7.7 %make_timeline.1 = (f32[64,8192]{1,0:T(8,128)}, f32[16,8192]{1,0:T(8,128)S(1)}) custom-call(s32[1]{0:T(128)} %bitcast.det_ref, s32[64,64]{1,0:T(8,128)} %slot_ref.3, f32[16,256]{1,0:T(8,128)} %bitcast.42, f32[1,256]{1,0:T(1,128)} %bitcast.44, s32[64,8192]{1,0:T(8,128)} %offset_ref.3, s32[64,8192]{1,0:T(8,128)} %angle_ref.3, ...), custom_call_target="tpu_custom_call" | custom-call | tf_op jit(solution)/shard_map/make_timeline/pallas_call | solution.py:236
  22.6 0.1 collective-permute-start.4
  22.7 1.5 %collective-permute-done.4 = f32[16,4096]{1,0:T(8,128)S(1)} collective-permute-done((f32[16,4096]{1,0:T(8,128)S(1)}, f32[16,4096]{1,0:T(8,128)S(1)}, u32[]{:S(2)}, u32[]{:S(2)}) %collective-permute-start.4) | collective-permute-done | bytes 262176 | tf_op jit(solution)/shard_map/ppermute | solution.py:483
  24.2 0.6 collective-permute-start.5
  24.8 2.7 %mode_matrices.1 = (f32[64,16]{1,0:T(8,128)S(1)}, f32[64,1]{1,0:T(8,128)S(1)}) custom-call(s32[1]{0:T(128)} %bitcast.det_ref, f32[16,256]{1,0:T(8,128)} %bitcast.43, f32[1,256]{1,0:T(1,128)} %bitcast.45, f32[1,16]{1,0:T(1,128)} %bitcast.46, f32[16,8192]{1,0:T(8,128)S(1)} %get-tuple-element.18.after_ref), custom_call_target="tpu_custom_call" | custom-call | tf_op jit(solution)/shard_map/mode_matrices/pallas_call | solution.py:167
  27.6 5.1 %collective-permute-done.5 = f32[16,4096]{1,0:T(8,128)S(1)} collective-permute-done((f32[16,4096]{1,0:T(8,128)S(1)}, f32[16,4096]{1,0:T(8,128)S(1)}, u32[]{:S(2)}, u32[]{:S(2)}) %collective-permute-start.5) | collective-permute-done | bytes 262176 | tf_op jit(solution)/shard_map/ppermute | solution.py:483
  32.7 0.1 collective-permute-start.6
  32.8 1.5 %collective-permute-done.6 = f32[16,4096]{1,0:T(8,128)S(1)} collective-permute-done((f32[16,4096]{1,0:T(8,128)S(1)}, f32[16,4096]{1,0:T(8,128)S(1)}, u32[]{:S(2)}, u32[]{:S(2)}) %collective-permute-start.6) | collective-permute-done | bytes 262176 | tf_op jit(solution)/shard_map/ppermute | solution.py:483
  34.4 0.0 copy-start
  34.4 0.0 copy-start.1
  34.4 0.0 copy-start.2
  34.4 0.0 copy-start.4
  34.4 14.8 %bin_samples.1 = (f32[2,2,48,128]{3,2,1,0:T(8,128)S(1)}, f32[2,2,48,128]{3,2,1,0:T(8,128)S(1)}) custom-call(s32[1]{0:T(128)} %bitcast.det_ref, s32[64,64]{1,0:T(8,128)} %slot_ref.3, f32[16,8192]{1,0:T(8,128)S(1)} %pad_maximum_fusion.proj_ref, f32[64,16]{1,0:T(8,128)S(1)} %get-tuple-element.22.back_ref, f32[64,1]{1,0:T(8,128)S(1)} %get-tuple-element.23.weight_ref, ...), custom_call_target="tpu_custom_call" | custom-call | tf_op jit(solution)/shard_map/bin_samples/pallas_call | solution.py:360
  49.2 0.0 copy-start.3
  49.2 0.2 collective-permute-start.7
  49.5 1.1 %collective-permute-done.7 = f32[2,2,48,128]{3,2,1,0:T(8,128)S(1)} collective-permute-done((f32[2,2,48,128]{3,2,1,0:T(8,128)S(1)}, f32[2,2,48,128]{3,2,1,0:T(8,128)S(1)}, u32[]{:S(2)}, u32[]{:S(2)}) %collective-permute-start.7) | collective-permute-done | bytes 98336 | tf_op jit(solution)/shard_map/ppermute | solution.py:483
  50.6 1.5 %collective-permute-start.10 = (f32[2,48,128]{2,1,0:T(8,128)S(1)}, f32[2,48,128]{2,1,0:T(8,128)S(1)}, u32[]{:S(2)}, u32[]{:S(2)}) collective-permute-start(f32[2,48,128]{2,1,0:T(8,128)S(1)} %pad_maximum_fusion.8), channel_id=1, source_target_pairs={{0,6},{1,7},{2,4},{3,5},{4,10},{5,11},{6,8},{7,9},{8,14},{9,15},{1... | collective-permute-start | bytes 147464 | tf_op jit(solution)/shard_map/ppermute | solution.py:494
  52.2 0.1 collective-permute-start.9
  52.3 1.5 %collective-permute-start.8 = (f32[2,48,128]{2,1,0:T(8,128)S(1)}, f32[2,48,128]{2,1,0:T(8,128)S(1)}, u32[]{:S(2)}, u32[]{:S(2)}) collective-permute-start(f32[2,48,128]{2,1,0:T(8,128)S(1)} %pad_maximum_fusion.6), channel_id=1, source_target_pairs={{0,2},{1,3},{2,0},{3,1},{4,6},{5,7},{6,4},{7,5},{8,10},{9,11},{10,... | collective-permute-start | bytes 147464 | tf_op jit(solution)/shard_map/ppermute | solution.py:494
  53.8 5.0 %collective-permute-done.10.refs_3_ = f32[2,48,128]{2,1,0:T(8,128)S(1)} collective-permute-done((f32[2,48,128]{2,1,0:T(8,128)S(1)}, f32[2,48,128]{2,1,0:T(8,128)S(1)}, u32[]{:S(2)}, u32[]{:S(2)}) %collective-permute-start.10) | collective-permute-done | bytes 49184 | tf_op jit(solution)/shard_map/ppermute | solution.py:494
  58.7 0.4 collective-permute-done.9.refs_2_
  59.1 0.0 collective-permute-done.8.refs_1_
  59.1 0.0 copy-done
  59.1 0.0 copy-done.1
  59.1 0.0 copy-done.2
  59.2 0.0 copy-done.4
  59.2 1.6 %push_blocks.1 = (f32[3,384,128]{2,1,0:T(8,128)S(1)}, f32[32,128]{1,0:T(8,128)S(1)}) custom-call(s32[1]{0:T(128)} %bitcast.det_ref, s32[1,1,2,4,16]{4,3,2,1,0:T(4,128)S(1)} %copy-done.4, f32[3,384,128]{2,1,0:T(8,128)S(1)} %copy-done, f32[3,384,128]{2,1,0:T(8,128)S(1)} %copy-done.2, f32[6,384,128]{2,1,0:T(8,128)S(1)} %copy-done.1, ...), custom_call_target="tpu_custom_call" | custom-call | tf_op jit(solution)/shard_map/push_blocks/pallas_call | solution.py:427
  60.7 10.1 %all_to_all.11 = f32[32,1,128]{2,1,0:T(1,128)S(1)} all-to-all(f32[32,1,128]{2,1,0:T(1,128)S(1)} %bitcast.41), channel_id=1, replica_groups=mesh['tm'=8,'det'=4] {'tm','det'}, dimensions={0} | all-to-all | bytes 32768 | tf_op jit(solution)/shard_map/all_to_all | solution.py:559
  70.8 0.0 copy-done.3
  70.8 2.2 %update_maps.1 = (f32[3,384,128]{2,1,0:T(8,128)}, f32[3,384,128]{2,1,0:T(8,128)}, f32[3,384,128]{2,1,0:T(8,128)}) custom-call(f32[32,128]{1,0:T(8,128)S(1)} %bitcast.40, f32[3,384,128]{2,1,0:T(8,128)S(1)} %copy-done.3, f32[3,384,128]{2,1,0:T(8,128)S(1)} %copy-done.2, f32[3,384,128]{2,1,0:T(8,128)S(1)} %copy-done, ...), custom_call_target="tpu_custom_call" | custom-call | tf_op jit(solution)/shard_map/update_maps/pallas_call | solution.py:470
  (17 shorter events, 0.2 us)
Async XLA Ops:
  1.9 1.5 %collective-permute-start = (f32[2,2,48,128]{3,2,1,0:T(8,128)S(1)}, f32[2,2,48,128]{3,2,1,0:T(8,128)S(1)}, u32[]{:S(2)}, u32[]{:S(2)}) collective-permute-start(f32[2,2,48,128]{3,2,1,0:T(8,128)S(1)} %get-tuple-element.17), channel_id=1, source_target_pairs={{0,1},{1,0},{2,3},{3,2},{4,5},{5,4},{6,7},{7,6},{8,9},{9,8},{10,11... | collective-permute-start | bytes 294920 | tf_op jit(solution)/shard_map/ppermute | solution.py:483
  3.4 8.7 %collective-permute-start.3 = (f32[2,48,128]{2,1,0:T(8,128)S(1)}, f32[2,48,128]{2,1,0:T(8,128)S(1)}, u32[]{:S(2)}, u32[]{:S(2)}) collective-permute-start(f32[2,48,128]{2,1,0:T(8,128)S(1)} %pad_maximum_fusion.4), channel_id=1, source_target_pairs={{0,30},{1,31},{2,28},{3,29},{4,2},{5,3},{6,0},{7,1},{8,6},{9,7},{1... | collective-permute-start | bytes 147464 | tf_op jit(solution)/shard_map/ppermute | solution.py:494
  10.3 4.1 %collective-permute-start.2 = (f32[2,48,128]{2,1,0:T(8,128)S(1)}, f32[2,48,128]{2,1,0:T(8,128)S(1)}, u32[]{:S(2)}, u32[]{:S(2)}) collective-permute-start(f32[2,48,128]{2,1,0:T(8,128)S(1)} %pad_maximum_fusion.3), channel_id=1, source_target_pairs={{0,28},{1,29},{2,30},{3,31},{4,0},{5,1},{6,2},{7,3},{8,4},{9,5},{1... | collective-permute-start | bytes 147464 | tf_op jit(solution)/shard_map/ppermute | solution.py:494
  10.8 4.1 %collective-permute-start.1 = (f32[2,48,128]{2,1,0:T(8,128)S(1)}, f32[2,48,128]{2,1,0:T(8,128)S(1)}, u32[]{:S(2)}, u32[]{:S(2)}) collective-permute-start(f32[2,48,128]{2,1,0:T(8,128)S(1)} %pad_maximum_fusion.2), channel_id=1, source_target_pairs={{0,2},{1,3},{2,0},{3,1},{4,6},{5,7},{6,4},{7,5},{8,10},{9,11},{10,... | collective-permute-start | bytes 147464 | tf_op jit(solution)/shard_map/ppermute | solution.py:494
  22.6 1.6 %collective-permute-start.4 = (f32[16,4096]{1,0:T(8,128)S(1)}, f32[16,4096]{1,0:T(8,128)S(1)}, u32[]{:S(2)}, u32[]{:S(2)}) collective-permute-start(f32[16,4096]{1,0:T(8,128)S(1)} %constant_dynamic-slice_fusion), channel_id=1, source_target_pairs={{0,1},{1,0},{2,3},{3,2},{4,5},{5,4},{6,7},{7,6},{8,9},{9,8},{10,11... | collective-permute-start | bytes 786440 | tf_op jit(solution)/shard_map/ppermute | solution.py:483
  24.2 8.4 %collective-permute-start.5 = (f32[16,4096]{1,0:T(8,128)S(1)}, f32[16,4096]{1,0:T(8,128)S(1)}, u32[]{:S(2)}, u32[]{:S(2)}) collective-permute-start(f32[16,4096]{1,0:T(8,128)S(1)} %dynamic-slice_add_fusion), channel_id=1, source_target_pairs={{0,2},{1,3},{2,0},{3,1},{4,6},{5,7},{6,4},{7,5},{8,10},{9,11},{10,... | collective-permute-start | bytes 786440 | tf_op jit(solution)/shard_map/ppermute | solution.py:483
  32.7 1.6 %collective-permute-start.6 = (f32[16,4096]{1,0:T(8,128)S(1)}, f32[16,4096]{1,0:T(8,128)S(1)}, u32[]{:S(2)}, u32[]{:S(2)}) collective-permute-start(f32[16,4096]{1,0:T(8,128)S(1)} %add.20), channel_id=1, source_target_pairs={{0,1},{1,0},{2,3},{3,2},{4,5},{5,4},{6,7},{7,6},{8,9},{9,8},{10,11... | collective-permute-start | bytes 786440 | tf_op jit(solution)/shard_map/ppermute | solution.py:483
  34.4 24.8 %copy-start = (f32[3,384,128]{2,1,0:T(8,128)S(1)}, f32[3,384,128]{2,1,0:T(8,128)}, u32[]{:S(2)}) copy-start(f32[3,384,128]{2,1,0:T(8,128)} %direction_ref.5) | copy-start | bytes 1769476
  34.4 24.8 %copy-start.1 = (f32[6,384,128]{2,1,0:T(8,128)S(1)}, f32[6,384,128]{2,1,0:T(8,128)}, u32[]{:S(2)}) copy-start(f32[6,384,128]{2,1,0:T(8,128)} %pre_ref.3) | copy-start | bytes 3538948
  34.4 24.7 %copy-start.2 = (f32[3,384,128]{2,1,0:T(8,128)S(1)}, f32[3,384,128]{2,1,0:T(8,128)}, u32[]{:S(2)}) copy-start(f32[3,384,128]{2,1,0:T(8,128)} %residual_ref.3) | copy-start | bytes 1769476
  34.4 24.7 %copy-start.4 = (s32[1,1,2,4,16]{4,3,2,1,0:T(4,128)S(1)}, s32[1,1,2,4,16]{4,3,2,1,0:T(4,128)}, u32[]{:S(2)}) copy-start(s32[1,1,2,4,16]{4,3,2,1,0:T(4,128)} %request_ref.3) | copy-start | bytes 1540
  49.2 21.6 %copy-start.3 = (f32[3,384,128]{2,1,0:T(8,128)S(1)}, f32[3,384,128]{2,1,0:T(8,128)}, u32[]{:S(2)}) copy-start(f32[3,384,128]{2,1,0:T(8,128)} %solution_ref.1) | copy-start | bytes 1769476
  49.2 1.4 %collective-permute-start.7 = (f32[2,2,48,128]{3,2,1,0:T(8,128)S(1)}, f32[2,2,48,128]{3,2,1,0:T(8,128)S(1)}, u32[]{:S(2)}, u32[]{:S(2)}) collective-permute-start(f32[2,2,48,128]{3,2,1,0:T(8,128)S(1)} %get-tuple-element.26), channel_id=1, source_target_pairs={{0,1},{1,0},{2,3},{3,2},{4,5},{5,4},{6,7},{7,6},{8,9},{9,8},{10,11... | collective-permute-start | bytes 294920 | tf_op jit(solution)/shard_map/ppermute | solution.py:483
  50.6 8.1 %collective-permute-start.10 = (f32[2,48,128]{2,1,0:T(8,128)S(1)}, f32[2,48,128]{2,1,0:T(8,128)S(1)}, u32[]{:S(2)}, u32[]{:S(2)}) collective-permute-start(f32[2,48,128]{2,1,0:T(8,128)S(1)} %pad_maximum_fusion.8), channel_id=1, source_target_pairs={{0,6},{1,7},{2,4},{3,5},{4,10},{5,11},{6,8},{7,9},{8,14},{9,15},{1... | collective-permute-start | bytes 147464 | tf_op jit(solution)/shard_map/ppermute | solution.py:494
  52.2 7.0 %collective-permute-start.9 = (f32[2,48,128]{2,1,0:T(8,128)S(1)}, f32[2,48,128]{2,1,0:T(8,128)S(1)}, u32[]{:S(2)}, u32[]{:S(2)}) collective-permute-start(f32[2,48,128]{2,1,0:T(8,128)S(1)} %pad_maximum_fusion.7), channel_id=1, source_target_pairs={{0,4},{1,5},{2,6},{3,7},{4,8},{5,9},{6,10},{7,11},{8,12},{9,13},{1... | collective-permute-start | bytes 147464 | tf_op jit(solution)/shard_map/ppermute | solution.py:494
  52.3 6.8 %collective-permute-start.8 = (f32[2,48,128]{2,1,0:T(8,128)S(1)}, f32[2,48,128]{2,1,0:T(8,128)S(1)}, u32[]{:S(2)}, u32[]{:S(2)}) collective-permute-start(f32[2,48,128]{2,1,0:T(8,128)S(1)} %pad_maximum_fusion.6), channel_id=1, source_target_pairs={{0,2},{1,3},{2,0},{3,1},{4,6},{5,7},{6,4},{7,5},{8,10},{9,11},{10,... | collective-permute-start | bytes 147464 | tf_op jit(solution)/shard_map/ppermute | solution.py:494

commit v4 on v3

--- a/solution.py
+++ b/solution.py
@@ -221,7 +221,7 @@
                 )
         return carry
 
-    lax.fori_loop(0, det_count // GROUP, body, 0, unroll=4)
+    lax.fori_loop(0, det_count // GROUP, body, 0, unroll=8)
     proj_ref[...] = jnp.dot(
         weighted_ref[...], time_ref[...], precision=HIGHEST, preferred_element_type=F32
     )
@@ -281,7 +281,7 @@
     low_iota = lax.broadcasted_iota(jnp.int32, (LOW, RUN_LEN), 0).astype(F32).astype(BF16)
     row_iota = lax.broadcasted_iota(jnp.int32, (GROUP, PB), 0)
     lane_iota = lax.broadcasted_iota(jnp.int32, (GROUP, PB), 1)
-    diagonal = lane_iota // LOW == row_iota % HIGH
+    places = [((lane_iota // LOW) - row_iota - j) % HIGH == 0 for j in range(HIGH)]
     zero = jnp.zeros((), BF16)
     one = jnp.ones((), BF16)
 
@@ -320,10 +320,9 @@
                     top = (j * 3 + k) * 2 * GROUP
                     pair = product[top : top + GROUP] + product[top + GROUP : top + 2 * GROUP]
                     part = jnp.where(row_iota < HIGH, pair[:, :PB], pair[:, PB:])
-                    part = jnp.where(diagonal, part, 0.0)
                     if j:
                         part = pltpu.roll(part, LOW * j, 1)
-                    total = part if total is None else total + part
+                    total = part if total is None else jnp.where(places[j], part, total)
                 row_ref[run, pl.ds(k, GROUP, stride=ROWS), :] = total
             for det in range(GROUP):
                 slot = slot_ref[first + det, (step * runs + run) * RUN]
@@ -550,7 +549,7 @@
     projection, (back, own_weight) = summed_over_det(local_proj, matrices)
     own, other = bin_samples(
         det, block_slot, projection, back, own_weight, pixel_offset, angle_index, timeline,
-        pull_index.shape[2:], 1024,
+        pull_index.shape[2:], 2048,
     )
     arrived = delivered(own, other, 1)
     operated, parts = push_blocks(

time: 73.2 us -> 70.9 us (0.969)
  Pallas kernels: 30.2 us -> 27.8 us
    pallas_call x1, Pallas kernels: 14.8 us -> 13.1 us  [bin_samples(): pl.pallas_call(bin_kernel, grid=(samp_dev // chunk,), out_shape=(piece, p...]
    pallas_call x1, Pallas kernels: 7.67 us -> 6.93 us  [make_timeline(): pl.pallas_call(timeline_kernel, grid=(samp_dev // chunk,), out_shape=(plt...]
where the time goes in v4:
time: 70.9 us; the launch traced here: 70.6 us
  Pallas kernels  27.8 us (39%)
  waiting for transfers between devices  19.1 us (27%)
  starting transfers between devices  12.5 us (18%)
  blocking collectives  10.1 us (14%)
  between operations  0.8 us (1%)
    pallas_call x1, Pallas kernels, bin_samples(): pl.pallas_call(bin_kernel, grid=(samp_dev // chunk,), out_shape=(piece, p...  13.1 us
    ppermute x6, starting transfers between devices, delivered(): lax.ppermute(pair, ('tm', 'det'), [(time * dets + det, (time + sign * rea...  11.1 us
    ppermute x5, waiting for transfers between devices, exchanged(): lax.ppermute(value, axis, [(source, source ^ bit) for source in range(cou...  10.2 us
    all_to_all x1, blocking collectives, on_device(): lax.all_to_all(parts, ('tm', 'det'), split_axis=0, concat_axis=0, tiled=T...  10.1 us
    ppermute x6, waiting for transfers between devices, delivered(): lax.ppermute(pair, ('tm', 'det'), [(time * dets + det, (time + sign * rea...  8.9 us
    pallas_call x1, Pallas kernels, make_timeline(): pl.pallas_call(timeline_kernel, grid=(samp_dev // chunk,), out_shape=(plt...  6.93 us
    pallas_call x1, Pallas kernels, mode_matrices(): pl.pallas_call(mode_kernel, out_shape=(jax.ShapeDtypeStruct((det_dev, mod...  2.72 us
    pallas_call x1, Pallas kernels, update_maps(): pl.pallas_call(update_kernel, grid=(solution.shape[1] // chunk,), out_sha...  2.18 us
  transfers between devices with their start and end apart: 11, of which 10 were waited for; matrix products, arithmetic and copies ran while one was open for 0% of the time, Pallas kernels for 4%

profile of v4, /device:TPU:0, one launch (start us, length us, event | category | flops | bytes accessed | tf_op | source)
XLA Modules:
  0.0 70.6 jit_solution(17607102271335477873)
XLA Ops:
  0.6 1.3 %pull_blocks.1 = (f32[2,2,48,128]{3,2,1,0:T(8,128)S(1)}, f32[2,2,48,128]{3,2,1,0:T(8,128)S(1)}) custom-call(s32[1]{0:T(128)} %bitcast.det_ref, s32[1,1,2,4,16]{4,3,2,1,0:T(4,128)} %request_ref.3, f32[3,384,128]{2,1,0:T(8,128)} %direction_ref.5), custom_call_target="tpu_custom_call" | custom-call | tf_op jit(solution)/shard_map/pull_blocks/pallas_call | solution.py:120
  1.9 0.5 collective-permute-start
  2.5 0.9 %collective-permute-done = f32[2,2,48,128]{3,2,1,0:T(8,128)S(1)} collective-permute-done((f32[2,2,48,128]{3,2,1,0:T(8,128)S(1)}, f32[2,2,48,128]{3,2,1,0:T(8,128)S(1)}, u32[]{:S(2)}, u32[]{:S(2)}) %collective-permute-start) | collective-permute-done | bytes 98336 | tf_op jit(solution)/shard_map/ppermute | solution.py:482
  3.4 6.9 %collective-permute-start.3 = (f32[2,48,128]{2,1,0:T(8,128)S(1)}, f32[2,48,128]{2,1,0:T(8,128)S(1)}, u32[]{:S(2)}, u32[]{:S(2)}) collective-permute-start(f32[2,48,128]{2,1,0:T(8,128)S(1)} %pad_maximum_fusion.4), channel_id=1, source_target_pairs={{0,30},{1,31},{2,28},{3,29},{4,2},{5,3},{6,0},{7,1},{8,6},{9,7},{1... | collective-permute-start | bytes 147464 | tf_op jit(solution)/shard_map/ppermute | solution.py:493
  10.3 0.5 collective-permute-start.2
  10.8 0.5 collective-permute-start.1
  11.4 0.8 %collective-permute-done.3.refs_3_ = f32[2,48,128]{2,1,0:T(8,128)S(1)} collective-permute-done((f32[2,48,128]{2,1,0:T(8,128)S(1)}, f32[2,48,128]{2,1,0:T(8,128)S(1)}, u32[]{:S(2)}, u32[]{:S(2)}) %collective-permute-start.3) | collective-permute-done | bytes 49184 | tf_op jit(solution)/shard_map/ppermute | solution.py:493
  12.1 2.3 %collective-permute-done.2.refs_2_ = f32[2,48,128]{2,1,0:T(8,128)S(1)} collective-permute-done((f32[2,48,128]{2,1,0:T(8,128)S(1)}, f32[2,48,128]{2,1,0:T(8,128)S(1)}, u32[]{:S(2)}, u32[]{:S(2)}) %collective-permute-start.2) | collective-permute-done | bytes 49184 | tf_op jit(solution)/shard_map/ppermute | solution.py:493
  14.4 0.5 collective-permute-done.1.refs_1_
  14.9 6.9 %make_timeline.1 = (f32[64,8192]{1,0:T(8,128)}, f32[16,8192]{1,0:T(8,128)S(1)}) custom-call(s32[1]{0:T(128)} %bitcast.det_ref, s32[64,64]{1,0:T(8,128)} %slot_ref.3, f32[16,256]{1,0:T(8,128)} %bitcast.42, f32[1,256]{1,0:T(1,128)} %bitcast.44, s32[64,8192]{1,0:T(8,128)} %offset_ref.3, s32[64,8192]{1,0:T(8,128)} %angle_ref.3, ...), custom_call_target="tpu_custom_call" | custom-call | tf_op jit(solution)/shard_map/make_timeline/pallas_call | solution.py:236
  21.9 0.1 collective-permute-start.4
  22.0 1.5 %collective-permute-done.4 = f32[16,4096]{1,0:T(8,128)S(1)} collective-permute-done((f32[16,4096]{1,0:T(8,128)S(1)}, f32[16,4096]{1,0:T(8,128)S(1)}, u32[]{:S(2)}, u32[]{:S(2)}) %collective-permute-start.4) | collective-permute-done | bytes 262176 | tf_op jit(solution)/shard_map/ppermute | solution.py:482
  23.5 0.6 collective-permute-start.5
  24.1 2.7 %mode_matrices.1 = (f32[64,16]{1,0:T(8,128)S(1)}, f32[64,1]{1,0:T(8,128)S(1)}) custom-call(s32[1]{0:T(128)} %bitcast.det_ref, f32[16,256]{1,0:T(8,128)} %bitcast.43, f32[1,256]{1,0:T(1,128)} %bitcast.45, f32[1,16]{1,0:T(1,128)} %bitcast.46, f32[16,8192]{1,0:T(8,128)S(1)} %get-tuple-element.18.after_ref), custom_call_target="tpu_custom_call" | custom-call | tf_op jit(solution)/shard_map/mode_matrices/pallas_call | solution.py:167
  26.8 5.1 %collective-permute-done.5 = f32[16,4096]{1,0:T(8,128)S(1)} collective-permute-done((f32[16,4096]{1,0:T(8,128)S(1)}, f32[16,4096]{1,0:T(8,128)S(1)}, u32[]{:S(2)}, u32[]{:S(2)}) %collective-permute-start.5) | collective-permute-done | bytes 262176 | tf_op jit(solution)/shard_map/ppermute | solution.py:482
  31.9 0.1 collective-permute-start.6
  32.0 1.5 %collective-permute-done.6 = f32[16,4096]{1,0:T(8,128)S(1)} collective-permute-done((f32[16,4096]{1,0:T(8,128)S(1)}, f32[16,4096]{1,0:T(8,128)S(1)}, u32[]{:S(2)}, u32[]{:S(2)}) %collective-permute-start.6) | collective-permute-done | bytes 262176 | tf_op jit(solution)/shard_map/ppermute | solution.py:482
  33.6 0.0 copy-start
  33.6 0.0 copy-start.1
  33.7 0.0 copy-start.2
  33.7 0.0 copy-start.4
  33.7 13.1 %bin_samples.1 = (f32[2,2,48,128]{3,2,1,0:T(8,128)S(1)}, f32[2,2,48,128]{3,2,1,0:T(8,128)S(1)}) custom-call(s32[1]{0:T(128)} %bitcast.det_ref, s32[64,64]{1,0:T(8,128)} %slot_ref.3, f32[16,8192]{1,0:T(8,128)S(1)} %pad_maximum_fusion.proj_ref, f32[64,16]{1,0:T(8,128)S(1)} %get-tuple-element.22.back_ref, f32[64,1]{1,0:T(8,128)S(1)} %get-tuple-element.23.weight_ref, ...), custom_call_target="tpu_custom_call" | custom-call | tf_op jit(solution)/shard_map/bin_samples/pallas_call | solution.py:359
  46.8 0.0 copy-start.3
  46.8 0.2 collective-permute-start.7
  47.0 1.2 %collective-permute-done.7 = f32[2,2,48,128]{3,2,1,0:T(8,128)S(1)} collective-permute-done((f32[2,2,48,128]{3,2,1,0:T(8,128)S(1)}, f32[2,2,48,128]{3,2,1,0:T(8,128)S(1)}, u32[]{:S(2)}, u32[]{:S(2)}) %collective-permute-start.7) | collective-permute-done | bytes 98336 | tf_op jit(solution)/shard_map/ppermute | solution.py:482
  48.2 1.6 %collective-permute-start.10 = (f32[2,48,128]{2,1,0:T(8,128)S(1)}, f32[2,48,128]{2,1,0:T(8,128)S(1)}, u32[]{:S(2)}, u32[]{:S(2)}) collective-permute-start(f32[2,48,128]{2,1,0:T(8,128)S(1)} %pad_maximum_fusion.8), channel_id=1, source_target_pairs={{0,6},{1,7},{2,4},{3,5},{4,10},{5,11},{6,8},{7,9},{8,14},{9,15},{1... | collective-permute-start | bytes 147464 | tf_op jit(solution)/shard_map/ppermute | solution.py:493
  49.8 0.1 collective-permute-start.9
  49.9 1.5 %collective-permute-start.8 = (f32[2,48,128]{2,1,0:T(8,128)S(1)}, f32[2,48,128]{2,1,0:T(8,128)S(1)}, u32[]{:S(2)}, u32[]{:S(2)}) collective-permute-start(f32[2,48,128]{2,1,0:T(8,128)S(1)} %pad_maximum_fusion.6), channel_id=1, source_target_pairs={{0,2},{1,3},{2,0},{3,1},{4,6},{5,7},{6,4},{7,5},{8,10},{9,11},{10,... | collective-permute-start | bytes 147464 | tf_op jit(solution)/shard_map/ppermute | solution.py:493
  51.4 4.9 %collective-permute-done.10.refs_3_ = f32[2,48,128]{2,1,0:T(8,128)S(1)} collective-permute-done((f32[2,48,128]{2,1,0:T(8,128)S(1)}, f32[2,48,128]{2,1,0:T(8,128)S(1)}, u32[]{:S(2)}, u32[]{:S(2)}) %collective-permute-start.10) | collective-permute-done | bytes 49184 | tf_op jit(solution)/shard_map/ppermute | solution.py:493
  56.3 0.4 collective-permute-done.9.refs_2_
  56.7 0.0 collective-permute-done.8.refs_1_
  56.7 0.0 copy-done
  56.7 0.0 copy-done.1
  56.7 0.0 copy-done.2
  56.7 0.0 copy-done.4
  56.7 1.6 %push_blocks.1 = (f32[3,384,128]{2,1,0:T(8,128)S(1)}, f32[32,128]{1,0:T(8,128)S(1)}) custom-call(s32[1]{0:T(128)} %bitcast.det_ref, s32[1,1,2,4,16]{4,3,2,1,0:T(4,128)S(1)} %copy-done.4, f32[3,384,128]{2,1,0:T(8,128)S(1)} %copy-done, f32[3,384,128]{2,1,0:T(8,128)S(1)} %copy-done.2, f32[6,384,128]{2,1,0:T(8,128)S(1)} %copy-done.1, ...), custom_call_target="tpu_custom_call" | custom-call | tf_op jit(solution)/shard_map/push_blocks/pallas_call | solution.py:426
  58.3 10.1 %all_to_all.11 = f32[32,1,128]{2,1,0:T(1,128)S(1)} all-to-all(f32[32,1,128]{2,1,0:T(1,128)S(1)} %bitcast.41), channel_id=1, replica_groups=mesh['tm'=8,'det'=4] {'tm','det'}, dimensions={0} | all-to-all | bytes 32768 | tf_op jit(solution)/shard_map/all_to_all | solution.py:558
  68.4 0.0 copy-done.3
  68.4 2.2 %update_maps.1 = (f32[3,384,128]{2,1,0:T(8,128)}, f32[3,384,128]{2,1,0:T(8,128)}, f32[3,384,128]{2,1,0:T(8,128)}) custom-call(f32[32,128]{1,0:T(8,128)S(1)} %bitcast.40, f32[3,384,128]{2,1,0:T(8,128)S(1)} %copy-done.3, f32[3,384,128]{2,1,0:T(8,128)S(1)} %copy-done.2, f32[3,384,128]{2,1,0:T(8,128)S(1)} %copy-done, ...), custom_call_target="tpu_custom_call" | custom-call | tf_op jit(solution)/shard_map/update_maps/pallas_call | solution.py:469
  (17 shorter events, 0.2 us)
Async XLA Ops:
  1.9 1.5 %collective-permute-start = (f32[2,2,48,128]{3,2,1,0:T(8,128)S(1)}, f32[2,2,48,128]{3,2,1,0:T(8,128)S(1)}, u32[]{:S(2)}, u32[]{:S(2)}) collective-permute-start(f32[2,2,48,128]{3,2,1,0:T(8,128)S(1)} %get-tuple-element.17), channel_id=1, source_target_pairs={{0,1},{1,0},{2,3},{3,2},{4,5},{5,4},{6,7},{7,6},{8,9},{9,8},{10,11... | collective-permute-start | bytes 294920 | tf_op jit(solution)/shard_map/ppermute | solution.py:482
  3.4 8.7 %collective-permute-start.3 = (f32[2,48,128]{2,1,0:T(8,128)S(1)}, f32[2,48,128]{2,1,0:T(8,128)S(1)}, u32[]{:S(2)}, u32[]{:S(2)}) collective-permute-start(f32[2,48,128]{2,1,0:T(8,128)S(1)} %pad_maximum_fusion.4), channel_id=1, source_target_pairs={{0,30},{1,31},{2,28},{3,29},{4,2},{5,3},{6,0},{7,1},{8,6},{9,7},{1... | collective-permute-start | bytes 147464 | tf_op jit(solution)/shard_map/ppermute | solution.py:493
  10.3 4.1 %collective-permute-start.2 = (f32[2,48,128]{2,1,0:T(8,128)S(1)}, f32[2,48,128]{2,1,0:T(8,128)S(1)}, u32[]{:S(2)}, u32[]{:S(2)}) collective-permute-start(f32[2,48,128]{2,1,0:T(8,128)S(1)} %pad_maximum_fusion.3), channel_id=1, source_target_pairs={{0,28},{1,29},{2,30},{3,31},{4,0},{5,1},{6,2},{7,3},{8,4},{9,5},{1... | collective-permute-start | bytes 147464 | tf_op jit(solution)/shard_map/ppermute | solution.py:493
  10.8 4.1 %collective-permute-start.1 = (f32[2,48,128]{2,1,0:T(8,128)S(1)}, f32[2,48,128]{2,1,0:T(8,128)S(1)}, u32[]{:S(2)}, u32[]{:S(2)}) collective-permute-start(f32[2,48,128]{2,1,0:T(8,128)S(1)} %pad_maximum_fusion.2), channel_id=1, source_target_pairs={{0,2},{1,3},{2,0},{3,1},{4,6},{5,7},{6,4},{7,5},{8,10},{9,11},{10,... | collective-permute-start | bytes 147464 | tf_op jit(solution)/shard_map/ppermute | solution.py:493
  21.9 1.6 %collective-permute-start.4 = (f32[16,4096]{1,0:T(8,128)S(1)}, f32[16,4096]{1,0:T(8,128)S(1)}, u32[]{:S(2)}, u32[]{:S(2)}) collective-permute-start(f32[16,4096]{1,0:T(8,128)S(1)} %constant_dynamic-slice_fusion), channel_id=1, source_target_pairs={{0,1},{1,0},{2,3},{3,2},{4,5},{5,4},{6,7},{7,6},{8,9},{9,8},{10,11... | collective-permute-start | bytes 786440 | tf_op jit(solution)/shard_map/ppermute | solution.py:482
  23.5 8.4 %collective-permute-start.5 = (f32[16,4096]{1,0:T(8,128)S(1)}, f32[16,4096]{1,0:T(8,128)S(1)}, u32[]{:S(2)}, u32[]{:S(2)}) collective-permute-start(f32[16,4096]{1,0:T(8,128)S(1)} %dynamic-slice_add_fusion), channel_id=1, source_target_pairs={{0,2},{1,3},{2,0},{3,1},{4,6},{5,7},{6,4},{7,5},{8,10},{9,11},{10,... | collective-permute-start | bytes 786440 | tf_op jit(solution)/shard_map/ppermute | solution.py:482
  31.9 1.6 %collective-permute-start.6 = (f32[16,4096]{1,0:T(8,128)S(1)}, f32[16,4096]{1,0:T(8,128)S(1)}, u32[]{:S(2)}, u32[]{:S(2)}) collective-permute-start(f32[16,4096]{1,0:T(8,128)S(1)} %add.20), channel_id=1, source_target_pairs={{0,1},{1,0},{2,3},{3,2},{4,5},{5,4},{6,7},{7,6},{8,9},{9,8},{10,11... | collective-permute-start | bytes 786440 | tf_op jit(solution)/shard_map/ppermute | solution.py:482
  33.6 23.1 %copy-start = (f32[3,384,128]{2,1,0:T(8,128)S(1)}, f32[3,384,128]{2,1,0:T(8,128)}, u32[]{:S(2)}) copy-start(f32[3,384,128]{2,1,0:T(8,128)} %direction_ref.5) | copy-start | bytes 1769476
  33.6 23.1 %copy-start.1 = (f32[6,384,128]{2,1,0:T(8,128)S(1)}, f32[6,384,128]{2,1,0:T(8,128)}, u32[]{:S(2)}) copy-start(f32[6,384,128]{2,1,0:T(8,128)} %pre_ref.3) | copy-start | bytes 3538948
  33.7 23.1 %copy-start.2 = (f32[3,384,128]{2,1,0:T(8,128)S(1)}, f32[3,384,128]{2,1,0:T(8,128)}, u32[]{:S(2)}) copy-start(f32[3,384,128]{2,1,0:T(8,128)} %residual_ref.3) | copy-start | bytes 1769476
  33.7 23.1 %copy-start.4 = (s32[1,1,2,4,16]{4,3,2,1,0:T(4,128)S(1)}, s32[1,1,2,4,16]{4,3,2,1,0:T(4,128)}, u32[]{:S(2)}) copy-start(s32[1,1,2,4,16]{4,3,2,1,0:T(4,128)} %request_ref.3) | copy-start | bytes 1540
  46.8 21.6 %copy-start.3 = (f32[3,384,128]{2,1,0:T(8,128)S(1)}, f32[3,384,128]{2,1,0:T(8,128)}, u32[]{:S(2)}) copy-start(f32[3,384,128]{2,1,0:T(8,128)} %solution_ref.1) | copy-start | bytes 1769476
  46.8 1.4 %collective-permute-start.7 = (f32[2,2,48,128]{3,2,1,0:T(8,128)S(1)}, f32[2,2,48,128]{3,2,1,0:T(8,128)S(1)}, u32[]{:S(2)}, u32[]{:S(2)}) collective-permute-start(f32[2,2,48,128]{3,2,1,0:T(8,128)S(1)} %get-tuple-element.26), channel_id=1, source_target_pairs={{0,1},{1,0},{2,3},{3,2},{4,5},{5,4},{6,7},{7,6},{8,9},{9,8},{10,11... | collective-permute-start | bytes 294920 | tf_op jit(solution)/shard_map/ppermute | solution.py:482
  48.2 8.0 %collective-permute-start.10 = (f32[2,48,128]{2,1,0:T(8,128)S(1)}, f32[2,48,128]{2,1,0:T(8,128)S(1)}, u32[]{:S(2)}, u32[]{:S(2)}) collective-permute-start(f32[2,48,128]{2,1,0:T(8,128)S(1)} %pad_maximum_fusion.8), channel_id=1, source_target_pairs={{0,6},{1,7},{2,4},{3,5},{4,10},{5,11},{6,8},{7,9},{8,14},{9,15},{1... | collective-permute-start | bytes 147464 | tf_op jit(solution)/shard_map/ppermute | solution.py:493
  49.8 6.9 %collective-permute-start.9 = (f32[2,48,128]{2,1,0:T(8,128)S(1)}, f32[2,48,128]{2,1,0:T(8,128)S(1)}, u32[]{:S(2)}, u32[]{:S(2)}) collective-permute-start(f32[2,48,128]{2,1,0:T(8,128)S(1)} %pad_maximum_fusion.7), channel_id=1, source_target_pairs={{0,4},{1,5},{2,6},{3,7},{4,8},{5,9},{6,10},{7,11},{8,12},{9,13},{1... | collective-permute-start | bytes 147464 | tf_op jit(solution)/shard_map/ppermute | solution.py:493
  49.9 6.8 %collective-permute-start.8 = (f32[2,48,128]{2,1,0:T(8,128)S(1)}, f32[2,48,128]{2,1,0:T(8,128)S(1)}, u32[]{:S(2)}, u32[]{:S(2)}) collective-permute-start(f32[2,48,128]{2,1,0:T(8,128)S(1)} %pad_maximum_fusion.6), channel_id=1, source_target_pairs={{0,2},{1,3},{2,0},{3,1},{4,6},{5,7},{6,4},{7,5},{8,10},{9,11},{10,... | collective-permute-start | bytes 147464 | tf_op jit(solution)/shard_map/ppermute | solution.py:493

commit v5 on v4

--- a/solution.py
+++ b/solution.py
@@ -413,7 +413,7 @@
         return tuple(total + part for total, part in zip(totals, parts))
 
     nothing = jnp.zeros((ROWS, PB), F32)
-    totals = lax.fori_loop(0, blocks // ROWS, body, (nothing,) * 4, unroll=4)
+    totals = lax.fori_loop(0, blocks // ROWS, body, (nothing,) * 4, unroll=8)
     lane = lax.broadcasted_iota(jnp.int32, part_ref.shape, 1)
     row = jnp.zeros(part_ref.shape, F32)
     for place, total in enumerate(totals):
@@ -543,7 +543,7 @@
     own, other = pull_blocks(det, pull_index, direction)
     pieces = delivered(own, other, -1)
     timeline, local_proj = make_timeline(
-        det, block_slot, templates, weight, pixel_offset, angle_index, pieces, 2048
+        det, block_slot, templates, weight, pixel_offset, angle_index, pieces, 4096
     )
     matrices = mode_matrices(det, det_dev, templates, weight, mode_precision, local_proj)
     projection, (back, own_weight) = summed_over_det(local_proj, matrices)
@@ -556,7 +556,7 @@
         det, pull_index, direction, residual, preconditioner, arrived, device_count
     )
     parts = lax.all_to_all(parts, ("tm", "det"), split_axis=0, concat_axis=0, tiled=True)
-    return update_maps(parts, solution, residual, direction, operated, preconditioner, 96)
+    return update_maps(parts, solution, residual, direction, operated, preconditioner, 192)
 
 
 def solution(mesh):

time: 70.9 us -> 69.9 us (0.986)
  Pallas kernels: 27.8 us -> 26.9 us
where the time goes in v5:
time: 69.9 us; the launch traced here: 69.7 us
  Pallas kernels  26.9 us (38%)
  waiting for transfers between devices  19.1 us (27%)
  starting transfers between devices  12.5 us (18%)
  blocking collectives  10.1 us (14%)
  between operations  0.8 us (1%)
    pallas_call x1, Pallas kernels, bin_samples(): pl.pallas_call(bin_kernel, grid=(samp_dev // chunk,), out_shape=(piece, p...  13.1 us
    ppermute x6, starting transfers between devices, delivered(): lax.ppermute(pair, ('tm', 'det'), [(time * dets + det, (time + sign * rea...  11 us
    ppermute x5, waiting for transfers between devices, exchanged(): lax.ppermute(value, axis, [(source, source ^ bit) for source in range(cou...  10.2 us
    all_to_all x1, blocking collectives, on_device(): lax.all_to_all(parts, ('tm', 'det'), split_axis=0, concat_axis=0, tiled=T...  10.1 us
    ppermute x6, waiting for transfers between devices, delivered(): lax.ppermute(pair, ('tm', 'det'), [(time * dets + det, (time + sign * rea...  8.92 us
    pallas_call x1, Pallas kernels, make_timeline(): pl.pallas_call(timeline_kernel, grid=(samp_dev // chunk,), out_shape=(plt...  6.72 us
    pallas_call x1, Pallas kernels, mode_matrices(): pl.pallas_call(mode_kernel, out_shape=(jax.ShapeDtypeStruct((det_dev, mod...  2.72 us
    pallas_call x1, Pallas kernels, update_maps(): pl.pallas_call(update_kernel, grid=(solution.shape[1] // chunk,), out_sha...  1.53 us
  transfers between devices with their start and end apart: 11, of which 10 were waited for; matrix products, arithmetic and copies ran while one was open for 0% of the time, Pallas kernels for 4%

profile of v5, /device:TPU:0, one launch (start us, length us, event | category | flops | bytes accessed | tf_op | source)
XLA Modules:
  0.0 69.7 jit_solution(16160090709122279802)
XLA Ops:
  0.6 1.3 %pull_blocks.1 = (f32[2,2,48,128]{3,2,1,0:T(8,128)S(1)}, f32[2,2,48,128]{3,2,1,0:T(8,128)S(1)}) custom-call(s32[1]{0:T(128)} %bitcast.det_ref, s32[1,1,2,4,16]{4,3,2,1,0:T(4,128)} %request_ref.3, f32[3,384,128]{2,1,0:T(8,128)} %direction_ref.5), custom_call_target="tpu_custom_call" | custom-call | tf_op jit(solution)/shard_map/pull_blocks/pallas_call | solution.py:120
  1.9 0.5 collective-permute-start
  2.5 0.9 %collective-permute-done = f32[2,2,48,128]{3,2,1,0:T(8,128)S(1)} collective-permute-done((f32[2,2,48,128]{3,2,1,0:T(8,128)S(1)}, f32[2,2,48,128]{3,2,1,0:T(8,128)S(1)}, u32[]{:S(2)}, u32[]{:S(2)}) %collective-permute-start) | collective-permute-done | bytes 98336 | tf_op jit(solution)/shard_map/ppermute | solution.py:482
  3.4 6.9 %collective-permute-start.3 = (f32[2,48,128]{2,1,0:T(8,128)S(1)}, f32[2,48,128]{2,1,0:T(8,128)S(1)}, u32[]{:S(2)}, u32[]{:S(2)}) collective-permute-start(f32[2,48,128]{2,1,0:T(8,128)S(1)} %pad_maximum_fusion.4), channel_id=1, source_target_pairs={{0,30},{1,31},{2,28},{3,29},{4,2},{5,3},{6,0},{7,1},{8,6},{9,7},{1... | collective-permute-start | bytes 147464 | tf_op jit(solution)/shard_map/ppermute | solution.py:493
  10.3 0.5 collective-permute-start.2
  10.8 0.5 collective-permute-start.1
  11.4 0.8 %collective-permute-done.3.refs_3_ = f32[2,48,128]{2,1,0:T(8,128)S(1)} collective-permute-done((f32[2,48,128]{2,1,0:T(8,128)S(1)}, f32[2,48,128]{2,1,0:T(8,128)S(1)}, u32[]{:S(2)}, u32[]{:S(2)}) %collective-permute-start.3) | collective-permute-done | bytes 49184 | tf_op jit(solution)/shard_map/ppermute | solution.py:493
  12.1 2.3 %collective-permute-done.2.refs_2_ = f32[2,48,128]{2,1,0:T(8,128)S(1)} collective-permute-done((f32[2,48,128]{2,1,0:T(8,128)S(1)}, f32[2,48,128]{2,1,0:T(8,128)S(1)}, u32[]{:S(2)}, u32[]{:S(2)}) %collective-permute-start.2) | collective-permute-done | bytes 49184 | tf_op jit(solution)/shard_map/ppermute | solution.py:493
  14.4 0.5 collective-permute-done.1.refs_1_
  14.9 6.7 %make_timeline.1 = (f32[64,8192]{1,0:T(8,128)}, f32[16,8192]{1,0:T(8,128)S(1)}) custom-call(s32[1]{0:T(128)} %bitcast.det_ref, s32[64,64]{1,0:T(8,128)} %slot_ref.3, f32[16,256]{1,0:T(8,128)} %bitcast.42, f32[1,256]{1,0:T(1,128)} %bitcast.44, s32[64,8192]{1,0:T(8,128)} %offset_ref.3, s32[64,8192]{1,0:T(8,128)} %angle_ref.3, ...), custom_call_target="tpu_custom_call" | custom-call | tf_op jit(solution)/shard_map/make_timeline/pallas_call | solution.py:236
  21.7 0.1 collective-permute-start.4
  21.7 1.5 %collective-permute-done.4 = f32[16,4096]{1,0:T(8,128)S(1)} collective-permute-done((f32[16,4096]{1,0:T(8,128)S(1)}, f32[16,4096]{1,0:T(8,128)S(1)}, u32[]{:S(2)}, u32[]{:S(2)}) %collective-permute-start.4) | collective-permute-done | bytes 262176 | tf_op jit(solution)/shard_map/ppermute | solution.py:482
  23.3 0.6 collective-permute-start.5
  23.9 2.7 %mode_matrices.1 = (f32[64,16]{1,0:T(8,128)S(1)}, f32[64,1]{1,0:T(8,128)S(1)}) custom-call(s32[1]{0:T(128)} %bitcast.det_ref, f32[16,256]{1,0:T(8,128)} %bitcast.43, f32[1,256]{1,0:T(1,128)} %bitcast.45, f32[1,16]{1,0:T(1,128)} %bitcast.46, f32[16,8192]{1,0:T(8,128)S(1)} %get-tuple-element.18.after_ref), custom_call_target="tpu_custom_call" | custom-call | tf_op jit(solution)/shard_map/mode_matrices/pallas_call | solution.py:167
  26.6 5.1 %collective-permute-done.5 = f32[16,4096]{1,0:T(8,128)S(1)} collective-permute-done((f32[16,4096]{1,0:T(8,128)S(1)}, f32[16,4096]{1,0:T(8,128)S(1)}, u32[]{:S(2)}, u32[]{:S(2)}) %collective-permute-start.5) | collective-permute-done | bytes 262176 | tf_op jit(solution)/shard_map/ppermute | solution.py:482
  31.7 0.1 collective-permute-start.6
  31.8 1.5 %collective-permute-done.6 = f32[16,4096]{1,0:T(8,128)S(1)} collective-permute-done((f32[16,4096]{1,0:T(8,128)S(1)}, f32[16,4096]{1,0:T(8,128)S(1)}, u32[]{:S(2)}, u32[]{:S(2)}) %collective-permute-start.6) | collective-permute-done | bytes 262176 | tf_op jit(solution)/shard_map/ppermute | solution.py:482
  33.4 0.0 copy-start
  33.4 0.0 copy-start.1
  33.4 0.0 copy-start.2
  33.5 0.0 copy-start.4
  33.5 13.1 %bin_samples.1 = (f32[2,2,48,128]{3,2,1,0:T(8,128)S(1)}, f32[2,2,48,128]{3,2,1,0:T(8,128)S(1)}) custom-call(s32[1]{0:T(128)} %bitcast.det_ref, s32[64,64]{1,0:T(8,128)} %slot_ref.3, f32[16,8192]{1,0:T(8,128)S(1)} %pad_maximum_fusion.proj_ref, f32[64,16]{1,0:T(8,128)S(1)} %get-tuple-element.22.back_ref, f32[64,1]{1,0:T(8,128)S(1)} %get-tuple-element.23.weight_ref, ...), custom_call_target="tpu_custom_call" | custom-call | tf_op jit(solution)/shard_map/bin_samples/pallas_call | solution.py:359
  46.6 0.0 copy-start.3
  46.6 0.2 collective-permute-start.7
  46.8 1.2 %collective-permute-done.7 = f32[2,2,48,128]{3,2,1,0:T(8,128)S(1)} collective-permute-done((f32[2,2,48,128]{3,2,1,0:T(8,128)S(1)}, f32[2,2,48,128]{3,2,1,0:T(8,128)S(1)}, u32[]{:S(2)}, u32[]{:S(2)}) %collective-permute-start.7) | collective-permute-done | bytes 98336 | tf_op jit(solution)/shard_map/ppermute | solution.py:482
  48.0 1.5 %collective-permute-start.10 = (f32[2,48,128]{2,1,0:T(8,128)S(1)}, f32[2,48,128]{2,1,0:T(8,128)S(1)}, u32[]{:S(2)}, u32[]{:S(2)}) collective-permute-start(f32[2,48,128]{2,1,0:T(8,128)S(1)} %pad_maximum_fusion.8), channel_id=1, source_target_pairs={{0,6},{1,7},{2,4},{3,5},{4,10},{5,11},{6,8},{7,9},{8,14},{9,15},{1... | collective-permute-start | bytes 147464 | tf_op jit(solution)/shard_map/ppermute | solution.py:493
  49.5 0.1 collective-permute-start.9
  49.7 1.5 %collective-permute-start.8 = (f32[2,48,128]{2,1,0:T(8,128)S(1)}, f32[2,48,128]{2,1,0:T(8,128)S(1)}, u32[]{:S(2)}, u32[]{:S(2)}) collective-permute-start(f32[2,48,128]{2,1,0:T(8,128)S(1)} %pad_maximum_fusion.6), channel_id=1, source_target_pairs={{0,2},{1,3},{2,0},{3,1},{4,6},{5,7},{6,4},{7,5},{8,10},{9,11},{10,... | collective-permute-start | bytes 147464 | tf_op jit(solution)/shard_map/ppermute | solution.py:493
  51.1 5.0 %collective-permute-done.10.refs_3_ = f32[2,48,128]{2,1,0:T(8,128)S(1)} collective-permute-done((f32[2,48,128]{2,1,0:T(8,128)S(1)}, f32[2,48,128]{2,1,0:T(8,128)S(1)}, u32[]{:S(2)}, u32[]{:S(2)}) %collective-permute-start.10) | collective-permute-done | bytes 49184 | tf_op jit(solution)/shard_map/ppermute | solution.py:493
  56.1 0.4 collective-permute-done.9.refs_2_
  56.5 0.0 collective-permute-done.8.refs_1_
  56.5 0.0 copy-done
  56.5 0.0 copy-done.1
  56.5 0.0 copy-done.2
  56.5 0.0 copy-done.4
  56.5 1.5 %push_blocks.1 = (f32[3,384,128]{2,1,0:T(8,128)S(1)}, f32[32,128]{1,0:T(8,128)S(1)}) custom-call(s32[1]{0:T(128)} %bitcast.det_ref, s32[1,1,2,4,16]{4,3,2,1,0:T(4,128)S(1)} %copy-done.4, f32[3,384,128]{2,1,0:T(8,128)S(1)} %copy-done, f32[3,384,128]{2,1,0:T(8,128)S(1)} %copy-done.2, f32[6,384,128]{2,1,0:T(8,128)S(1)} %copy-done.1, ...), custom_call_target="tpu_custom_call" | custom-call | tf_op jit(solution)/shard_map/push_blocks/pallas_call | solution.py:426
  58.0 10.1 %all_to_all.11 = f32[32,1,128]{2,1,0:T(1,128)S(1)} all-to-all(f32[32,1,128]{2,1,0:T(1,128)S(1)} %bitcast.41), channel_id=1, replica_groups=mesh['tm'=8,'det'=4] {'tm','det'}, dimensions={0} | all-to-all | bytes 32768 | tf_op jit(solution)/shard_map/all_to_all | solution.py:558
  68.1 0.0 copy-done.3
  68.1 1.5 %update_maps.1 = (f32[3,384,128]{2,1,0:T(8,128)}, f32[3,384,128]{2,1,0:T(8,128)}, f32[3,384,128]{2,1,0:T(8,128)}) custom-call(f32[32,128]{1,0:T(8,128)S(1)} %bitcast.40, f32[3,384,128]{2,1,0:T(8,128)S(1)} %copy-done.3, f32[3,384,128]{2,1,0:T(8,128)S(1)} %copy-done.2, f32[3,384,128]{2,1,0:T(8,128)S(1)} %copy-done, ...), custom_call_target="tpu_custom_call" | custom-call | tf_op jit(solution)/shard_map/update_maps/pallas_call | solution.py:469
  (17 shorter events, 0.2 us)
Async XLA Ops:
  1.9 1.5 %collective-permute-start = (f32[2,2,48,128]{3,2,1,0:T(8,128)S(1)}, f32[2,2,48,128]{3,2,1,0:T(8,128)S(1)}, u32[]{:S(2)}, u32[]{:S(2)}) collective-permute-start(f32[2,2,48,128]{3,2,1,0:T(8,128)S(1)} %get-tuple-element.17), channel_id=1, source_target_pairs={{0,1},{1,0},{2,3},{3,2},{4,5},{5,4},{6,7},{7,6},{8,9},{9,8},{10,11... | collective-permute-start | bytes 294920 | tf_op jit(solution)/shard_map/ppermute | solution.py:482
  3.4 8.7 %collective-permute-start.3 = (f32[2,48,128]{2,1,0:T(8,128)S(1)}, f32[2,48,128]{2,1,0:T(8,128)S(1)}, u32[]{:S(2)}, u32[]{:S(2)}) collective-permute-start(f32[2,48,128]{2,1,0:T(8,128)S(1)} %pad_maximum_fusion.4), channel_id=1, source_target_pairs={{0,30},{1,31},{2,28},{3,29},{4,2},{5,3},{6,0},{7,1},{8,6},{9,7},{1... | collective-permute-start | bytes 147464 | tf_op jit(solution)/shard_map/ppermute | solution.py:493
  10.3 4.1 %collective-permute-start.2 = (f32[2,48,128]{2,1,0:T(8,128)S(1)}, f32[2,48,128]{2,1,0:T(8,128)S(1)}, u32[]{:S(2)}, u32[]{:S(2)}) collective-permute-start(f32[2,48,128]{2,1,0:T(8,128)S(1)} %pad_maximum_fusion.3), channel_id=1, source_target_pairs={{0,28},{1,29},{2,30},{3,31},{4,0},{5,1},{6,2},{7,3},{8,4},{9,5},{1... | collective-permute-start | bytes 147464 | tf_op jit(solution)/shard_map/ppermute | solution.py:493
  10.8 4.1 %collective-permute-start.1 = (f32[2,48,128]{2,1,0:T(8,128)S(1)}, f32[2,48,128]{2,1,0:T(8,128)S(1)}, u32[]{:S(2)}, u32[]{:S(2)}) collective-permute-start(f32[2,48,128]{2,1,0:T(8,128)S(1)} %pad_maximum_fusion.2), channel_id=1, source_target_pairs={{0,2},{1,3},{2,0},{3,1},{4,6},{5,7},{6,4},{7,5},{8,10},{9,11},{10,... | collective-permute-start | bytes 147464 | tf_op jit(solution)/shard_map/ppermute | solution.py:493
  21.7 1.6 %collective-permute-start.4 = (f32[16,4096]{1,0:T(8,128)S(1)}, f32[16,4096]{1,0:T(8,128)S(1)}, u32[]{:S(2)}, u32[]{:S(2)}) collective-permute-start(f32[16,4096]{1,0:T(8,128)S(1)} %constant_dynamic-slice_fusion), channel_id=1, source_target_pairs={{0,1},{1,0},{2,3},{3,2},{4,5},{5,4},{6,7},{7,6},{8,9},{9,8},{10,11... | collective-permute-start | bytes 786440 | tf_op jit(solution)/shard_map/ppermute | solution.py:482
  23.3 8.4 %collective-permute-start.5 = (f32[16,4096]{1,0:T(8,128)S(1)}, f32[16,4096]{1,0:T(8,128)S(1)}, u32[]{:S(2)}, u32[]{:S(2)}) collective-permute-start(f32[16,4096]{1,0:T(8,128)S(1)} %dynamic-slice_add_fusion), channel_id=1, source_target_pairs={{0,2},{1,3},{2,0},{3,1},{4,6},{5,7},{6,4},{7,5},{8,10},{9,11},{10,... | collective-permute-start | bytes 786440 | tf_op jit(solution)/shard_map/ppermute | solution.py:482
  31.7 1.6 %collective-permute-start.6 = (f32[16,4096]{1,0:T(8,128)S(1)}, f32[16,4096]{1,0:T(8,128)S(1)}, u32[]{:S(2)}, u32[]{:S(2)}) collective-permute-start(f32[16,4096]{1,0:T(8,128)S(1)} %add.20), channel_id=1, source_target_pairs={{0,1},{1,0},{2,3},{3,2},{4,5},{5,4},{6,7},{7,6},{8,9},{9,8},{10,11... | collective-permute-start | bytes 786440 | tf_op jit(solution)/shard_map/ppermute | solution.py:482
  33.4 23.1 %copy-start = (f32[3,384,128]{2,1,0:T(8,128)S(1)}, f32[3,384,128]{2,1,0:T(8,128)}, u32[]{:S(2)}) copy-start(f32[3,384,128]{2,1,0:T(8,128)} %direction_ref.5) | copy-start | bytes 1769476
  33.4 23.1 %copy-start.1 = (f32[6,384,128]{2,1,0:T(8,128)S(1)}, f32[6,384,128]{2,1,0:T(8,128)}, u32[]{:S(2)}) copy-start(f32[6,384,128]{2,1,0:T(8,128)} %pre_ref.3) | copy-start | bytes 3538948
  33.4 23.1 %copy-start.2 = (f32[3,384,128]{2,1,0:T(8,128)S(1)}, f32[3,384,128]{2,1,0:T(8,128)}, u32[]{:S(2)}) copy-start(f32[3,384,128]{2,1,0:T(8,128)} %residual_ref.3) | copy-start | bytes 1769476
  33.5 23.1 %copy-start.4 = (s32[1,1,2,4,16]{4,3,2,1,0:T(4,128)S(1)}, s32[1,1,2,4,16]{4,3,2,1,0:T(4,128)}, u32[]{:S(2)}) copy-start(s32[1,1,2,4,16]{4,3,2,1,0:T(4,128)} %request_ref.3) | copy-start | bytes 1540
  46.6 21.5 %copy-start.3 = (f32[3,384,128]{2,1,0:T(8,128)S(1)}, f32[3,384,128]{2,1,0:T(8,128)}, u32[]{:S(2)}) copy-start(f32[3,384,128]{2,1,0:T(8,128)} %solution_ref.1) | copy-start | bytes 1769476
  46.6 1.4 %collective-permute-start.7 = (f32[2,2,48,128]{3,2,1,0:T(8,128)S(1)}, f32[2,2,48,128]{3,2,1,0:T(8,128)S(1)}, u32[]{:S(2)}, u32[]{:S(2)}) collective-permute-start(f32[2,2,48,128]{3,2,1,0:T(8,128)S(1)} %get-tuple-element.26), channel_id=1, source_target_pairs={{0,1},{1,0},{2,3},{3,2},{4,5},{5,4},{6,7},{7,6},{8,9},{9,8},{10,11... | collective-permute-start | bytes 294920 | tf_op jit(solution)/shard_map/ppermute | solution.py:482
  48.0 8.1 %collective-permute-start.10 = (f32[2,48,128]{2,1,0:T(8,128)S(1)}, f32[2,48,128]{2,1,0:T(8,128)S(1)}, u32[]{:S(2)}, u32[]{:S(2)}) collective-permute-start(f32[2,48,128]{2,1,0:T(8,128)S(1)} %pad_maximum_fusion.8), channel_id=1, source_target_pairs={{0,6},{1,7},{2,4},{3,5},{4,10},{5,11},{6,8},{7,9},{8,14},{9,15},{1... | collective-permute-start | bytes 147464 | tf_op jit(solution)/shard_map/ppermute | solution.py:493
  49.5 7.0 %collective-permute-start.9 = (f32[2,48,128]{2,1,0:T(8,128)S(1)}, f32[2,48,128]{2,1,0:T(8,128)S(1)}, u32[]{:S(2)}, u32[]{:S(2)}) collective-permute-start(f32[2,48,128]{2,1,0:T(8,128)S(1)} %pad_maximum_fusion.7), channel_id=1, source_target_pairs={{0,4},{1,5},{2,6},{3,7},{4,8},{5,9},{6,10},{7,11},{8,12},{9,13},{1... | collective-permute-start | bytes 147464 | tf_op jit(solution)/shard_map/ppermute | solution.py:493
  49.7 6.8 %collective-permute-start.8 = (f32[2,48,128]{2,1,0:T(8,128)S(1)}, f32[2,48,128]{2,1,0:T(8,128)S(1)}, u32[]{:S(2)}, u32[]{:S(2)}) collective-permute-start(f32[2,48,128]{2,1,0:T(8,128)S(1)} %pad_maximum_fusion.6), channel_id=1, source_target_pairs={{0,2},{1,3},{2,0},{3,1},{4,6},{5,7},{6,4},{7,5},{8,10},{9,11},{10,... | collective-permute-start | bytes 147464 | tf_op jit(solution)/shard_map/ppermute | solution.py:493

commit v6 on v5

--- a/solution.py
+++ b/solution.py
@@ -1,3 +1,4 @@
+import functools
 import math
 
 import jax
@@ -21,6 +22,7 @@
 BF16 = jnp.bfloat16
 HIGHEST = lax.Precision.HIGHEST
 MIB = 1024 * 1024
+COST = 8192
 TERMS = 8
 
 
@@ -34,6 +36,10 @@
 
 def in_hbm(*arrays):
     return tuple(pltpu.with_memory_space_constraint(array, pltpu.HBM) for array in arrays)
+
+
+def cost(flops):
+    return pl.CostEstimate(flops=flops, bytes_accessed=4 * MIB, transcendentals=0)
 
 
 def params(mib):
@@ -162,7 +168,7 @@
     back_ref[...] = jnp.dot(solved, own_templates, precision=HIGHEST, preferred_element_type=F32).T
 
 
-def mode_matrices(det, det_dev, templates, weight, mode_precision, after):
+def mode_matrices(det, det_dev, templates, weight, mode_precision, waited):
     modes = templates.shape[0]
     return pl.pallas_call(
         mode_kernel,
@@ -174,10 +180,10 @@
         out_specs=(vmem_spec(), vmem_spec()),
         compiler_params=params(8),
         name="mode_matrices",
-    )(det, *in_hbm(templates, weight, mode_precision[None, :]), after)
-
-
-def timeline_kernel(det_ref, slot_ref, template_ref, weight_ref, offset_ref, angle_ref, *refs):
+    )(det, *in_hbm(templates, weight, mode_precision[None, :]), waited)
+
+
+def timeline_kernel(first_step, det_ref, slot_ref, template_ref, weight_ref, offset_ref, angle_ref, *refs):
     *piece_refs, time_ref, proj_ref, map_ref, table_ref, weighted_ref = refs
     step = pl.program_id(0)
     cap_count = piece_refs[0].shape[1] // 3
@@ -204,7 +210,7 @@
         first = pl.multiple_of(group * GROUP, GROUP)
         for run in range(runs):
             for det in range(GROUP):
-                slot = slot_ref[first + det, (step * runs + run) * RUN]
+                slot = slot_ref[first + det, ((first_step + step) * runs + run) * RUN]
                 table_ref[run, pl.ds(det * ROWS, ROWS), :] = map_ref[
                     pl.ds(pl.multiple_of(slot * ROWS, ROWS), ROWS), :
                 ]
@@ -227,44 +233,55 @@
     )
 
 
-def make_timeline(det, block_slot, templates, weight, pixel_offset, angle_index, pieces, chunk):
+def make_timeline(det, block_slot, templates, weight, pixel_offset, angle_index, pieces, chunk, part, parts):
     det_dev, samp_dev = pixel_offset.shape
+    steps = samp_dev // parts // chunk
+    first_step = part * steps
     modes = templates.shape[0]
     slot_total = len(pieces) * 2 * (pieces[0].shape[1] // 3)
     runs = chunk // RUN_LEN
-    wide = pl.BlockSpec((det_dev, chunk), lambda i: (0, i))
+    wide = pl.BlockSpec((det_dev, chunk), lambda i: (0, first_step + i))
     return pl.pallas_call(
-        timeline_kernel,
-        grid=(samp_dev // chunk,),
+        functools.partial(timeline_kernel, first_step),
+        grid=(steps,),
         out_shape=(
-            pltpu.HBM((det_dev, samp_dev), F32),
-            jax.ShapeDtypeStruct((modes, samp_dev), F32),
+            pltpu.HBM((det_dev, steps * chunk), F32),
+            jax.ShapeDtypeStruct((modes, steps * chunk), F32),
         ),
         in_specs=[smem_spec(), smem_spec(), vmem_spec(), vmem_spec(), wide, wide] + [vmem_spec()] * len(pieces),
-        out_specs=(wide, pl.BlockSpec((modes, chunk), lambda i: (0, i))),
+        out_specs=(
+            pl.BlockSpec((det_dev, chunk), lambda i: (0, i)),
+            pl.BlockSpec((modes, chunk), lambda i: (0, i)),
+        ),
         scratch_shapes=[
             pltpu.VMEM((slot_total * ROWS, PB), F32),
             pltpu.VMEM((runs, GROUP * ROWS, PB), F32),
             pltpu.VMEM((modes, det_dev), F32),
         ],
         compiler_params=params(24),
+        cost_estimate=cost(det_dev * steps * chunk * COST),
         name="make_timeline",
     )(det, *in_hbm(block_slot, templates, weight, pixel_offset, angle_index), *pieces)
 
 
 def bin_kernel(
-    det_ref, slot_ref, proj_ref, back_ref, weight_ref, offset_ref, angle_ref, time_ref,
-    own_ref, other_ref, map_ref, row_ref, filt_ref,
+    first_step, shape, begins, ends, det_ref, slot_ref, proj_ref, back_ref, weight_ref, offset_ref, angle_ref, time_ref, *refs
 ):
+    *refs, row_ref, filt_ref = refs
+    begin_ref = None if begins else refs.pop(0)
+    if ends:
+        own_ref, other_ref, map_ref = refs
+    else:
+        (map_ref,) = refs
     step = pl.program_id(0)
-    reach_count, hop_count, rows, _ = own_ref.shape
-    cap_count = rows // 3
+    reach_count, group_count, cap_count = shape
+    hop_count = group_count // 2
     det_count, chunk = offset_ref.shape
     runs = chunk // RUN_LEN
 
     @pl.when(step == 0)
     def _():
-        map_ref[...] = jnp.zeros_like(map_ref)
+        map_ref[...] = jnp.zeros_like(map_ref) if begins else begin_ref[...]
         row_ref[...] = jnp.zeros_like(row_ref)
 
     back = halves(back_ref[...])
@@ -325,12 +342,15 @@
                     total = part if total is None else jnp.where(places[j], part, total)
                 row_ref[run, pl.ds(k, GROUP, stride=ROWS), :] = total
             for det in range(GROUP):
-                slot = slot_ref[first + det, (step * runs + run) * RUN]
+                slot = slot_ref[first + det, ((first_step + step) * runs + run) * RUN]
                 at = pl.ds(pl.multiple_of(slot * ROWS, ROWS), ROWS)
                 map_ref[at, :] += row_ref[run, pl.ds(det * ROWS, ROWS), :]
         return carry
 
     lax.fori_loop(0, det_count // GROUP, body, 0, unroll=8)
+
+    if not ends:
+        return
 
     @pl.when(step == pl.num_programs(0) - 1)
     def _():
@@ -347,32 +367,39 @@
 
 
 def bin_samples(
-    det, block_slot, projection, back, weight, pixel_offset, angle_index, timeline, shape, chunk
+    det, block_slot, projection, back, weight, pixel_offset, angle_index, timeline, shape, chunk, part, parts, begin
 ):
     det_dev, samp_dev = pixel_offset.shape
     modes = projection.shape[0]
     reach_count, group_count, cap_count = shape
     slot_total = reach_count * group_count * cap_count
     runs = chunk // RUN_LEN
-    wide = pl.BlockSpec((det_dev, chunk), lambda i: (0, i))
+    steps = samp_dev // parts // chunk
+    first_step = part * steps
+    begins, ends = part == 0, part == parts - 1
+    wide = pl.BlockSpec((det_dev, chunk), lambda i: (0, first_step + i))
     piece = jax.ShapeDtypeStruct((reach_count, group_count // 2, 3 * cap_count, PB), F32)
+    sums = (slot_total * ROWS, PB)
     return pl.pallas_call(
-        bin_kernel,
-        grid=(samp_dev // chunk,),
-        out_shape=(piece, piece),
+        functools.partial(bin_kernel, first_step, shape, begins, ends),
+        grid=(steps,),
+        out_shape=(piece, piece) if ends else jax.ShapeDtypeStruct(sums, F32),
         in_specs=[smem_spec(), smem_spec(), pl.BlockSpec((modes, chunk), lambda i: (0, i))]
         + [vmem_spec()] * 2
-        + [wide, wide, wide],
-        out_specs=(vmem_spec(), vmem_spec()),
-        scratch_shapes=[
-            pltpu.VMEM((slot_total * ROWS, PB), F32),
+        + [wide, wide, pl.BlockSpec((det_dev, chunk), lambda i: (0, i))]
+        + ([] if begins else [vmem_spec()]),
+        out_specs=(vmem_spec(), vmem_spec()) if ends else vmem_spec(),
+        scratch_shapes=([pltpu.VMEM(sums, F32)] if ends else [])
+        + [
             pltpu.VMEM((runs, GROUP * ROWS, PB), F32),
             pltpu.VMEM((det_dev, chunk), F32),
         ],
         compiler_params=params(24),
+        cost_estimate=cost(2 * det_dev * steps * chunk * COST),
         name="bin_samples",
     )(
-        det, *in_hbm(block_slot), projection, back, weight, *in_hbm(pixel_offset, angle_index, timeline)
+        det, *in_hbm(block_slot), projection, back, weight, *in_hbm(pixel_offset, angle_index, timeline),
+        *(() if begins else (begin,)),
     )
 
 
@@ -503,22 +530,32 @@
     return pieces
 
 
-def summed_over_det(value, beside):
-    count = lax.axis_size("det")
+def core_sum(value):
     half = value.shape[1] // 2
     core = lax.axis_index("det") % 2
     own = lax.dynamic_slice_in_dim(value, core * half, half, 1)
     other = lax.dynamic_slice_in_dim(value, (1 - core) * half, half, 1)
-    own = own + exchanged(other, "det", 1)
+    return own + exchanged(other, "det", 1)
+
+
+def x_sum(own):
     bit = 2
-    while bit < count:
+    while bit < lax.axis_size("det"):
         own = own + exchanged(own, "det", bit)
         bit *= 2
-    own, beside = lax.optimization_barrier((own, beside))
+    return own
+
+
+def both_halves(own):
+    core = lax.axis_index("det") % 2
     other = exchanged(own, "det", 1)
     lower = jnp.where(core == 0, own, other)
     upper = jnp.where(core == 0, other, own)
-    return jnp.concatenate([lower, upper], axis=1), beside
+    return jnp.concatenate([lower, upper], axis=1)
+
+
+def after(value, *others):
+    return lax.optimization_barrier((value, *others))[0]
 
 
 def on_device(
@@ -542,14 +579,26 @@
 
     own, other = pull_blocks(det, pull_index, direction)
     pieces = delivered(own, other, -1)
-    timeline, local_proj = make_timeline(
-        det, block_slot, templates, weight, pixel_offset, angle_index, pieces, 4096
-    )
-    matrices = mode_matrices(det, det_dev, templates, weight, mode_precision, local_proj)
-    projection, (back, own_weight) = summed_over_det(local_proj, matrices)
+    back, own_weight = mode_matrices(det, det_dev, templates, weight, mode_precision, pieces[1])
+    times, projections = [], []
+    ready = (back,)
+    for part in range(2):
+        timeline, local_proj = make_timeline(
+            det, block_slot, after(templates, *ready), weight, pixel_offset, angle_index, pieces, 2048, part, 2
+        )
+        half = core_sum(local_proj)
+        ready = (half,)
+        times.append(timeline)
+        projections.append((x_sum(half), half, local_proj))
+    first = both_halves(after(projections[0][0], projections[1][2]))
+    sums = bin_samples(
+        det, block_slot, after(first, projections[1][1]), back, own_weight, pixel_offset, angle_index, times[0],
+        pull_index.shape[2:], 2048, 0, 2, None,
+    )
+    second = both_halves(after(projections[1][0], sums))
     own, other = bin_samples(
-        det, block_slot, projection, back, own_weight, pixel_offset, angle_index, timeline,
-        pull_index.shape[2:], 2048,
+        det, block_slot, second, back, own_weight, pixel_offset, angle_index, times[1],
+        pull_index.shape[2:], 2048, 1, 2, sums,
     )
     arrived = delivered(own, other, 1)
     operated, parts = push_blocks(

time: 69.9 us -> 69.3 us (level)
  waiting for transfers between devices: 19.1 us -> 15.3 us
  Pallas kernels: 26.9 us -> 30.5 us
    ppermute x5 -> x8, waiting for transfers between devices: 10.2 us -> 5.92 us  [exchanged(): lax.ppermute(value, axis, [(source, source ^ bit) for source in range(cou...]
    pallas_call x2 -> x4, Pallas kernels: 19.8 us -> 23.5 us  [the longest x2 14.5 us: bin_samples(): pl.pallas_call(functools.partial(bin_kernel, first_step, shape, begins, e...]
    ppermute x5 -> x8, starting transfers between devices: 1.47 us -> 3.24 us  [exchanged(): lax.ppermute(value, axis, [(source, source ^ bit) for source in range(cou...]
    ppermute x6, starting transfers between devices: 11 us -> 9.38 us  [delivered(): lax.ppermute(pair, ('tm', 'det'), [(time * dets + det, (time + sign * rea...]
  transfers between devices with their start and end apart: 11 -> 14, of which waited for: 10 -> 10; matrix products, arithmetic and copies ran while one was open for 0% -> 0% of each run, Pallas kernels for 4% -> 21%
where the time goes in v6:
time: 69.3 us; the launch traced here: 69.1 us
  Pallas kernels  30.5 us (44%)
  waiting for transfers between devices  15.3 us (22%)
  starting transfers between devices  12.6 us (18%)
  blocking collectives  9.47 us (14%)
  between operations  0.85 us (1%)
    pallas_call x2, Pallas kernels, bin_samples(): pl.pallas_call(functools.partial(bin_kernel, first_step, shape, begins, e...  14.5 us
    all_to_all x1, blocking collectives, on_device(): lax.all_to_all(parts, ('tm', 'det'), split_axis=0, concat_axis=0, tiled=T...  9.47 us
    ppermute x6, waiting for transfers between devices, delivered(): lax.ppermute(pair, ('tm', 'det'), [(time * dets + det, (time + sign * rea...  9.42 us
    ppermute x6, starting transfers between devices, delivered(): lax.ppermute(pair, ('tm', 'det'), [(time * dets + det, (time + sign * rea...  9.38 us
    pallas_call x2, Pallas kernels, make_timeline(): pl.pallas_call(functools.partial(timeline_kernel, first_step), grid=(step...  8.97 us
    ppermute x8, waiting for transfers between devices, exchanged(): lax.ppermute(value, axis, [(source, source ^ bit) for source in range(cou...  5.92 us
    ppermute x8, starting transfers between devices, exchanged(): lax.ppermute(value, axis, [(source, source ^ bit) for source in range(cou...  3.24 us
    pallas_call x1, Pallas kernels, mode_matrices(): pl.pallas_call(mode_kernel, out_shape=(jax.ShapeDtypeStruct((det_dev, mod...  2.72 us
  transfers between devices with their start and end apart: 14, of which 10 were waited for; matrix products, arithmetic and copies ran while one was open for 0% of the time, Pallas kernels for 21%

profile of v6, /device:TPU:0, one launch (start us, length us, event | category | flops | bytes accessed | tf_op | source)
XLA Modules:
  0.0 69.1 jit_solution(16474410962564369738)
XLA Ops:
  0.6 1.3 %pull_blocks.1 = (f32[2,2,48,128]{3,2,1,0:T(8,128)S(1)}, f32[2,2,48,128]{3,2,1,0:T(8,128)S(1)}) custom-call(s32[1]{0:T(128)} %bitcast.det_ref, s32[1,1,2,4,16]{4,3,2,1,0:T(4,128)} %request_ref.3, f32[3,384,128]{2,1,0:T(8,128)} %direction_ref.5), custom_call_target="tpu_custom_call" | custom-call | tf_op jit(solution)/shard_map/pull_blocks/pallas_call | solution.py:126
  1.9 0.5 collective-permute-start
  2.5 0.9 %collective-permute-done = f32[2,2,48,128]{3,2,1,0:T(8,128)S(1)} collective-permute-done((f32[2,2,48,128]{3,2,1,0:T(8,128)S(1)}, f32[2,2,48,128]{3,2,1,0:T(8,128)S(1)}, u32[]{:S(2)}, u32[]{:S(2)}) %collective-permute-start) | collective-permute-done | bytes 98336 | tf_op jit(solution)/shard_map/ppermute | solution.py:509
  3.4 2.9 %collective-permute-start.1 = (f32[2,48,128]{2,1,0:T(8,128)S(1)}, f32[2,48,128]{2,1,0:T(8,128)S(1)}, u32[]{:S(2)}, u32[]{:S(2)}) collective-permute-start(f32[2,48,128]{2,1,0:T(8,128)S(1)} %pad_maximum_fusion.2), channel_id=1, source_target_pairs={{0,2},{1,3},{2,0},{3,1},{4,6},{5,7},{6,4},{7,5},{8,10},{9,11},{10,... | collective-permute-start | bytes 147464 | tf_op jit(solution)/shard_map/ppermute | solution.py:520
  6.3 4.6 %collective-permute-start.2 = (f32[2,48,128]{2,1,0:T(8,128)S(1)}, f32[2,48,128]{2,1,0:T(8,128)S(1)}, u32[]{:S(2)}, u32[]{:S(2)}) collective-permute-start(f32[2,48,128]{2,1,0:T(8,128)S(1)} %pad_maximum_fusion.4), channel_id=1, source_target_pairs={{0,28},{1,29},{2,30},{3,31},{4,0},{5,1},{6,2},{7,3},{8,4},{9,5},{1... | collective-permute-start | bytes 147464 | tf_op jit(solution)/shard_map/ppermute | solution.py:520
  10.9 0.5 collective-permute-start.3
  11.4 0.0 collective-permute-done.1.after_ref.refs_1_
  11.4 2.7 %mode_matrices.1 = (f32[64,16]{1,0:T(8,128)S(1)}, f32[64,1]{1,0:T(8,128)S(1)}) custom-call(s32[1]{0:T(128)} %bitcast.det_ref, f32[16,256]{1,0:T(8,128)} %bitcast.42, f32[1,256]{1,0:T(1,128)} %bitcast.45, f32[1,16]{1,0:T(1,128)} %bitcast.48, f32[2,48,128]{2,1,0:T(8,128)S(1)} %collective-permute-done.1.after_ref.refs_1_), custom_call_target="tpu_custom_call" | custom-call | tf_op jit(solution)/shard_map/mode_matrices/pallas_call | solution.py:173
  14.1 0.0 collective-permute-done.2.refs_2_
  14.1 1.8 %collective-permute-done.3.refs_3_ = f32[2,48,128]{2,1,0:T(8,128)S(1)} collective-permute-done((f32[2,48,128]{2,1,0:T(8,128)S(1)}, f32[2,48,128]{2,1,0:T(8,128)S(1)}, u32[]{:S(2)}, u32[]{:S(2)}) %collective-permute-start.3) | collective-permute-done | bytes 49184 | tf_op jit(solution)/shard_map/ppermute | solution.py:520
  15.9 4.5 %make_timeline.2 = (f32[64,4096]{1,0:T(8,128)}, f32[16,4096]{1,0:T(8,128)S(1)}) custom-call(s32[1]{0:T(128)} %bitcast.det_ref, s32[64,64]{1,0:T(8,128)} %slot_ref.7, f32[16,256]{1,0:T(8,128)} %bitcast.43, f32[1,256]{1,0:T(1,128)} %bitcast.46, s32[64,8192]{1,0:T(8,128)} %offset_ref.7, s32[64,8192]{1,0:T(8,128)} %angle_ref.7, ...), custom_call_target="tpu_custom_call" | custom-call | flops 2147483648 | bytes 4194304 | tf_op jit(solution)/shard_map/make_timeline/pallas_call | solution.py:244
  20.4 0.1 collective-permute-start.4
  20.5 1.3 %collective-permute-done.4 = f32[16,2048]{1,0:T(8,128)S(1)} collective-permute-done((f32[16,2048]{1,0:T(8,128)S(1)}, f32[16,2048]{1,0:T(8,128)S(1)}, u32[]{:S(2)}, u32[]{:S(2)}) %collective-permute-start.4) | collective-permute-done | bytes 131104 | tf_op jit(solution)/shard_map/ppermute | solution.py:509
  21.8 0.6 collective-permute-start.7
  22.4 4.5 %make_timeline.3 = (f32[64,4096]{1,0:T(8,128)}, f32[16,4096]{1,0:T(8,128)S(1)}) custom-call(s32[1]{0:T(128)} %bitcast.det_ref, s32[64,64]{1,0:T(8,128)} %slot_ref.7, f32[16,256]{1,0:T(8,128)} %bitcast.44, f32[1,256]{1,0:T(1,128)} %bitcast.47, s32[64,8192]{1,0:T(8,128)} %offset_ref.7, s32[64,8192]{1,0:T(8,128)} %angle_ref.7, ...), custom_call_target="tpu_custom_call" | custom-call | flops 2147483648 | bytes 4194304 | tf_op jit(solution)/shard_map/make_timeline/pallas_call | solution.py:244
  26.9 0.1 collective-permute-start.5
  27.0 0.4 collective-permute-done.7
  27.4 0.1 collective-permute-start.8
  27.6 0.7 %collective-permute-done.5 = f32[16,2048]{1,0:T(8,128)S(1)} collective-permute-done((f32[16,2048]{1,0:T(8,128)S(1)}, f32[16,2048]{1,0:T(8,128)S(1)}, u32[]{:S(2)}, u32[]{:S(2)}) %collective-permute-start.5) | collective-permute-done | bytes 131104 | tf_op jit(solution)/shard_map/ppermute | solution.py:509
  28.3 1.6 %collective-permute-start.6 = (f32[16,2048]{1,0:T(8,128)S(1)}, f32[16,2048]{1,0:T(8,128)S(1)}, u32[]{:S(2)}, u32[]{:S(2)}) collective-permute-start(f32[16,2048]{1,0:T(8,128)S(1)} %dynamic-slice_add_fusion), channel_id=1, source_target_pairs={{0,2},{1,3},{2,0},{3,1},{4,6},{5,7},{6,4},{7,5},{8,10},{9,11},{10,... | collective-permute-start | bytes 393224 | tf_op jit(solution)/shard_map/ppermute | solution.py:509
  29.9 0.0 collective-permute-done.8
  30.0 7.2 %bin_samples.2.refs_0_ = f32[1024,128]{1,0:T(8,128)S(1)} custom-call(s32[1]{0:T(128)} %bitcast.det_ref, s32[64,64]{1,0:T(8,128)} %slot_ref.7, f32[16,4096]{1,0:T(8,128)S(1)} %pad_maximum_fusion.proj_ref, f32[64,16]{1,0:T(8,128)S(1)} %get-tuple-element.22.back_ref, f32[64,1]{1,0:T(8,128)S(1)} %get-tuple-element.29.weight_ref, s32[64,8192]{1,0:T(8,128)} %offset_ref.7, ...), custom_call_target="tpu_custom_call" | custom-call | flops 4294967296 | bytes 4194304 | tf_op jit(solution)/shard_map/bin_samples/pallas_call | solution.py:383
  37.1 0.0 collective-permute-done.6
  37.2 0.1 collective-permute-start.9
  37.2 1.3 %collective-permute-done.9 = f32[16,2048]{1,0:T(8,128)S(1)} collective-permute-done((f32[16,2048]{1,0:T(8,128)S(1)}, f32[16,2048]{1,0:T(8,128)S(1)}, u32[]{:S(2)}, u32[]{:S(2)}) %collective-permute-start.9) | collective-permute-done | bytes 131104 | tf_op jit(solution)/shard_map/ppermute | solution.py:509
  38.6 0.0 copy-start
  38.6 0.0 copy-start.1
  38.7 0.0 copy-start.2
  38.7 0.0 copy-start.4
  38.7 7.4 %bin_samples.3 = (f32[2,2,48,128]{3,2,1,0:T(8,128)S(1)}, f32[2,2,48,128]{3,2,1,0:T(8,128)S(1)}) custom-call(s32[1]{0:T(128)} %bitcast.det_ref, s32[64,64]{1,0:T(8,128)} %slot_ref.7, f32[16,4096]{1,0:T(8,128)S(1)} %pad_maximum_fusion.1.proj_ref, f32[64,16]{1,0:T(8,128)S(1)} %get-tuple-element.22.back_ref, f32[64,1]{1,0:T(8,128)S(1)} %get-tuple-element.29.weight_ref, ...), custom_call_target="tpu_custom_call" | custom-call | flops 4294967296 | bytes 4194304 | tf_op jit(solution)/shard_map/bin_samples/pallas_call | solution.py:383
  46.1 0.0 copy-start.3
  46.1 0.2 collective-permute-start.10
  46.3 1.1 %collective-permute-done.10 = f32[2,2,48,128]{3,2,1,0:T(8,128)S(1)} collective-permute-done((f32[2,2,48,128]{3,2,1,0:T(8,128)S(1)}, f32[2,2,48,128]{3,2,1,0:T(8,128)S(1)}, u32[]{:S(2)}, u32[]{:S(2)}) %collective-permute-start.10) | collective-permute-done | bytes 98336 | tf_op jit(solution)/shard_map/ppermute | solution.py:509
  47.5 0.6 collective-permute-start.11
  48.1 0.8 %collective-permute-start.12 = (f32[2,48,128]{2,1,0:T(8,128)S(1)}, f32[2,48,128]{2,1,0:T(8,128)S(1)}, u32[]{:S(2)}, u32[]{:S(2)}) collective-permute-start(f32[2,48,128]{2,1,0:T(8,128)S(1)} %pad_maximum_fusion.8), channel_id=1, source_target_pairs={{0,4},{1,5},{2,6},{3,7},{4,8},{5,9},{6,10},{7,11},{8,12},{9,13},{1... | collective-permute-start | bytes 147464 | tf_op jit(solution)/shard_map/ppermute | solution.py:520
  48.9 0.0 collective-permute-start.13
  48.9 3.0 %collective-permute-done.11.refs_1_ = f32[2,48,128]{2,1,0:T(8,128)S(1)} collective-permute-done((f32[2,48,128]{2,1,0:T(8,128)S(1)}, f32[2,48,128]{2,1,0:T(8,128)S(1)}, u32[]{:S(2)}, u32[]{:S(2)}) %collective-permute-start.11) | collective-permute-done | bytes 49184 | tf_op jit(solution)/shard_map/ppermute | solution.py:520
  51.9 3.7 %collective-permute-done.12.refs_2_ = f32[2,48,128]{2,1,0:T(8,128)S(1)} collective-permute-done((f32[2,48,128]{2,1,0:T(8,128)S(1)}, f32[2,48,128]{2,1,0:T(8,128)S(1)}, u32[]{:S(2)}, u32[]{:S(2)}) %collective-permute-start.12) | collective-permute-done | bytes 49184 | tf_op jit(solution)/shard_map/ppermute | solution.py:520
  55.6 1.0 %collective-permute-done.13.refs_3_ = f32[2,48,128]{2,1,0:T(8,128)S(1)} collective-permute-done((f32[2,48,128]{2,1,0:T(8,128)S(1)}, f32[2,48,128]{2,1,0:T(8,128)S(1)}, u32[]{:S(2)}, u32[]{:S(2)}) %collective-permute-start.13) | collective-permute-done | bytes 49184 | tf_op jit(solution)/shard_map/ppermute | solution.py:520
  56.6 0.0 copy-done
  56.6 0.0 copy-done.1
  56.6 0.0 copy-done.2
  56.6 0.0 copy-done.4
  56.6 1.5 %push_blocks.1 = (f32[3,384,128]{2,1,0:T(8,128)S(1)}, f32[32,128]{1,0:T(8,128)S(1)}) custom-call(s32[1]{0:T(128)} %bitcast.det_ref, s32[1,1,2,4,16]{4,3,2,1,0:T(4,128)S(1)} %copy-done.4, f32[3,384,128]{2,1,0:T(8,128)S(1)} %copy-done, f32[3,384,128]{2,1,0:T(8,128)S(1)} %copy-done.2, f32[6,384,128]{2,1,0:T(8,128)S(1)} %copy-done.1, ...), custom_call_target="tpu_custom_call" | custom-call | tf_op jit(solution)/shard_map/push_blocks/pallas_call | solution.py:453
  58.1 9.5 %all_to_all.11 = f32[32,1,128]{2,1,0:T(1,128)S(1)} all-to-all(f32[32,1,128]{2,1,0:T(1,128)S(1)} %bitcast.41), channel_id=1, replica_groups=mesh['tm'=8,'det'=4] {'tm','det'}, dimensions={0} | all-to-all | bytes 32768 | tf_op jit(solution)/shard_map/all_to_all | solution.py:607
  67.5 0.0 copy-done.3
  67.5 1.5 %update_maps.1 = (f32[3,384,128]{2,1,0:T(8,128)}, f32[3,384,128]{2,1,0:T(8,128)}, f32[3,384,128]{2,1,0:T(8,128)}) custom-call(f32[32,128]{1,0:T(8,128)S(1)} %bitcast.40, f32[3,384,128]{2,1,0:T(8,128)S(1)} %copy-done.3, f32[3,384,128]{2,1,0:T(8,128)S(1)} %copy-done.2, f32[3,384,128]{2,1,0:T(8,128)S(1)} %copy-done, ...), custom_call_target="tpu_custom_call" | custom-call | tf_op jit(solution)/shard_map/update_maps/pallas_call | solution.py:496
  (22 shorter events, 0.2 us)
Async XLA Ops:
  1.9 1.5 %collective-permute-start = (f32[2,2,48,128]{3,2,1,0:T(8,128)S(1)}, f32[2,2,48,128]{3,2,1,0:T(8,128)S(1)}, u32[]{:S(2)}, u32[]{:S(2)}) collective-permute-start(f32[2,2,48,128]{3,2,1,0:T(8,128)S(1)} %get-tuple-element.21), channel_id=1, source_target_pairs={{0,1},{1,0},{2,3},{3,2},{4,5},{5,4},{6,7},{7,6},{8,9},{9,8},{10,11... | collective-permute-start | bytes 294920 | tf_op jit(solution)/shard_map/ppermute | solution.py:509
  3.4 8.0 %collective-permute-start.1 = (f32[2,48,128]{2,1,0:T(8,128)S(1)}, f32[2,48,128]{2,1,0:T(8,128)S(1)}, u32[]{:S(2)}, u32[]{:S(2)}) collective-permute-start(f32[2,48,128]{2,1,0:T(8,128)S(1)} %pad_maximum_fusion.2), channel_id=1, source_target_pairs={{0,2},{1,3},{2,0},{3,1},{4,6},{5,7},{6,4},{7,5},{8,10},{9,11},{10,... | collective-permute-start | bytes 147464 | tf_op jit(solution)/shard_map/ppermute | solution.py:520
  6.3 7.8 %collective-permute-start.2 = (f32[2,48,128]{2,1,0:T(8,128)S(1)}, f32[2,48,128]{2,1,0:T(8,128)S(1)}, u32[]{:S(2)}, u32[]{:S(2)}) collective-permute-start(f32[2,48,128]{2,1,0:T(8,128)S(1)} %pad_maximum_fusion.4), channel_id=1, source_target_pairs={{0,28},{1,29},{2,30},{3,31},{4,0},{5,1},{6,2},{7,3},{8,4},{9,5},{1... | collective-permute-start | bytes 147464 | tf_op jit(solution)/shard_map/ppermute | solution.py:520
  10.9 5.0 %collective-permute-start.3 = (f32[2,48,128]{2,1,0:T(8,128)S(1)}, f32[2,48,128]{2,1,0:T(8,128)S(1)}, u32[]{:S(2)}, u32[]{:S(2)}) collective-permute-start(f32[2,48,128]{2,1,0:T(8,128)S(1)} %pad_maximum_fusion.5), channel_id=1, source_target_pairs={{0,30},{1,31},{2,28},{3,29},{4,2},{5,3},{6,0},{7,1},{8,6},{9,7},{1... | collective-permute-start | bytes 147464 | tf_op jit(solution)/shard_map/ppermute | solution.py:520
  20.4 1.4 %collective-permute-start.4 = (f32[16,2048]{1,0:T(8,128)S(1)}, f32[16,2048]{1,0:T(8,128)S(1)}, u32[]{:S(2)}, u32[]{:S(2)}) collective-permute-start(f32[16,2048]{1,0:T(8,128)S(1)} %constant_dynamic-slice_fusion.1), channel_id=1, source_target_pairs={{0,1},{1,0},{2,3},{3,2},{4,5},{5,4},{6,7},{7,6},{8,9},{9,8},{10,11... | collective-permute-start | bytes 393224 | tf_op jit(solution)/shard_map/ppermute | solution.py:509
  21.8 5.6 %collective-permute-start.7 = (f32[16,2048]{1,0:T(8,128)S(1)}, f32[16,2048]{1,0:T(8,128)S(1)}, u32[]{:S(2)}, u32[]{:S(2)}) collective-permute-start(f32[16,2048]{1,0:T(8,128)S(1)} %dynamic-slice_add_fusion.1), channel_id=1, source_target_pairs={{0,2},{1,3},{2,0},{3,1},{4,6},{5,7},{6,4},{7,5},{8,10},{9,11},{10,... | collective-permute-start | bytes 393224 | tf_op jit(solution)/shard_map/ppermute | solution.py:509
  26.9 1.4 %collective-permute-start.5 = (f32[16,2048]{1,0:T(8,128)S(1)}, f32[16,2048]{1,0:T(8,128)S(1)}, u32[]{:S(2)}, u32[]{:S(2)}) collective-permute-start(f32[16,2048]{1,0:T(8,128)S(1)} %constant_dynamic-slice_fusion), channel_id=1, source_target_pairs={{0,1},{1,0},{2,3},{3,2},{4,5},{5,4},{6,7},{7,6},{8,9},{9,8},{10,11... | collective-permute-start | bytes 393224 | tf_op jit(solution)/shard_map/ppermute | solution.py:509
  27.4 2.5 %collective-permute-start.8 = (f32[16,2048]{1,0:T(8,128)S(1)}, f32[16,2048]{1,0:T(8,128)S(1)}, u32[]{:S(2)}, u32[]{:S(2)}) collective-permute-start(f32[16,2048]{1,0:T(8,128)S(1)} %add.33), channel_id=1, source_target_pairs={{0,1},{1,0},{2,3},{3,2},{4,5},{5,4},{6,7},{7,6},{8,9},{9,8},{10,11... | collective-permute-start | bytes 393224 | tf_op jit(solution)/shard_map/ppermute | solution.py:509
  28.3 8.8 %collective-permute-start.6 = (f32[16,2048]{1,0:T(8,128)S(1)}, f32[16,2048]{1,0:T(8,128)S(1)}, u32[]{:S(2)}, u32[]{:S(2)}) collective-permute-start(f32[16,2048]{1,0:T(8,128)S(1)} %dynamic-slice_add_fusion), channel_id=1, source_target_pairs={{0,2},{1,3},{2,0},{3,1},{4,6},{5,7},{6,4},{7,5},{8,10},{9,11},{10,... | collective-permute-start | bytes 393224 | tf_op jit(solution)/shard_map/ppermute | solution.py:509
  37.2 1.4 %collective-permute-start.9 = (f32[16,2048]{1,0:T(8,128)S(1)}, f32[16,2048]{1,0:T(8,128)S(1)}, u32[]{:S(2)}, u32[]{:S(2)}) collective-permute-start(f32[16,2048]{1,0:T(8,128)S(1)} %add.32), channel_id=1, source_target_pairs={{0,1},{1,0},{2,3},{3,2},{4,5},{5,4},{6,7},{7,6},{8,9},{9,8},{10,11... | collective-permute-start | bytes 393224 | tf_op jit(solution)/shard_map/ppermute | solution.py:509
  38.6 17.9 %copy-start = (f32[3,384,128]{2,1,0:T(8,128)S(1)}, f32[3,384,128]{2,1,0:T(8,128)}, u32[]{:S(2)}) copy-start(f32[3,384,128]{2,1,0:T(8,128)} %direction_ref.5) | copy-start | bytes 1769476
  38.6 17.9 %copy-start.1 = (f32[6,384,128]{2,1,0:T(8,128)S(1)}, f32[6,384,128]{2,1,0:T(8,128)}, u32[]{:S(2)}) copy-start(f32[6,384,128]{2,1,0:T(8,128)} %pre_ref.3) | copy-start | bytes 3538948
  38.7 17.9 %copy-start.2 = (f32[3,384,128]{2,1,0:T(8,128)S(1)}, f32[3,384,128]{2,1,0:T(8,128)}, u32[]{:S(2)}) copy-start(f32[3,384,128]{2,1,0:T(8,128)} %residual_ref.3) | copy-start | bytes 1769476
  38.7 17.9 %copy-start.4 = (s32[1,1,2,4,16]{4,3,2,1,0:T(4,128)S(1)}, s32[1,1,2,4,16]{4,3,2,1,0:T(4,128)}, u32[]{:S(2)}) copy-start(s32[1,1,2,4,16]{4,3,2,1,0:T(4,128)} %request_ref.3) | copy-start | bytes 1540
  46.1 21.5 %copy-start.3 = (f32[3,384,128]{2,1,0:T(8,128)S(1)}, f32[3,384,128]{2,1,0:T(8,128)}, u32[]{:S(2)}) copy-start(f32[3,384,128]{2,1,0:T(8,128)} %solution_ref.1) | copy-start | bytes 1769476
  46.1 1.4 %collective-permute-start.10 = (f32[2,2,48,128]{3,2,1,0:T(8,128)S(1)}, f32[2,2,48,128]{3,2,1,0:T(8,128)S(1)}, u32[]{:S(2)}, u32[]{:S(2)}) collective-permute-start(f32[2,2,48,128]{3,2,1,0:T(8,128)S(1)} %get-tuple-element.34), channel_id=1, source_target_pairs={{0,1},{1,0},{2,3},{3,2},{4,5},{5,4},{6,7},{7,6},{8,9},{9,8},{10,11... | collective-permute-start | bytes 294920 | tf_op jit(solution)/shard_map/ppermute | solution.py:509
  47.5 4.4 %collective-permute-start.11 = (f32[2,48,128]{2,1,0:T(8,128)S(1)}, f32[2,48,128]{2,1,0:T(8,128)S(1)}, u32[]{:S(2)}, u32[]{:S(2)}) collective-permute-start(f32[2,48,128]{2,1,0:T(8,128)S(1)} %pad_maximum_fusion.7), channel_id=1, source_target_pairs={{0,2},{1,3},{2,0},{3,1},{4,6},{5,7},{6,4},{7,5},{8,10},{9,11},{10,... | collective-permute-start | bytes 147464 | tf_op jit(solution)/shard_map/ppermute | solution.py:520
  48.1 7.5 %collective-permute-start.12 = (f32[2,48,128]{2,1,0:T(8,128)S(1)}, f32[2,48,128]{2,1,0:T(8,128)S(1)}, u32[]{:S(2)}, u32[]{:S(2)}) collective-permute-start(f32[2,48,128]{2,1,0:T(8,128)S(1)} %pad_maximum_fusion.8), channel_id=1, source_target_pairs={{0,4},{1,5},{2,6},{3,7},{4,8},{5,9},{6,10},{7,11},{8,12},{9,13},{1... | collective-permute-start | bytes 147464 | tf_op jit(solution)/shard_map/ppermute | solution.py:520
  48.9 7.7 %collective-permute-start.13 = (f32[2,48,128]{2,1,0:T(8,128)S(1)}, f32[2,48,128]{2,1,0:T(8,128)S(1)}, u32[]{:S(2)}, u32[]{:S(2)}) collective-permute-start(f32[2,48,128]{2,1,0:T(8,128)S(1)} %pad_maximum_fusion.9), channel_id=1, source_target_pairs={{0,6},{1,7},{2,4},{3,5},{4,10},{5,11},{6,8},{7,9},{8,14},{9,15},{1... | collective-permute-start | bytes 147464 | tf_op jit(solution)/shard_map/ppermute | solution.py:520

commit v7 on v6

--- a/solution.py
+++ b/solution.py
@@ -527,7 +527,7 @@
                     ],
                 )
             pieces.append(pair)
-    return pieces
+    return pieces, got
 
 
 def core_sum(value):
@@ -578,8 +578,8 @@
     weight = det_weight[None, :]
 
     own, other = pull_blocks(det, pull_index, direction)
-    pieces = delivered(own, other, -1)
-    back, own_weight = mode_matrices(det, det_dev, templates, weight, mode_precision, pieces[1])
+    pieces, got = delivered(own, other, -1)
+    back, own_weight = mode_matrices(det, det_dev, templates, weight, mode_precision, got)
     times, projections = [], []
     ready = (back,)
     for part in range(2):
@@ -600,7 +600,7 @@
         det, block_slot, second, back, own_weight, pixel_offset, angle_index, times[1],
         pull_index.shape[2:], 2048, 1, 2, sums,
     )
-    arrived = delivered(own, other, 1)
+    arrived, _ = delivered(own, other, 1)
     operated, parts = push_blocks(
         det, pull_index, direction, residual, preconditioner, arrived, device_count
     )

time: 69.3 us -> 69.3 us (level)
  no operation moved by 1% of the time
where the time goes in v7:
time: 69.3 us; the launch traced here: 69.1 us
  Pallas kernels  30.5 us (44%)
  waiting for transfers between devices  15.3 us (22%)
  starting transfers between devices  12.6 us (18%)
  blocking collectives  9.47 us (14%)
  between operations  0.86 us (1%)
    pallas_call x2, Pallas kernels, bin_samples(): pl.pallas_call(functools.partial(bin_kernel, first_step, shape, begins, e...  14.5 us
    all_to_all x1, blocking collectives, on_device(): lax.all_to_all(parts, ('tm', 'det'), split_axis=0, concat_axis=0, tiled=T...  9.47 us
    ppermute x6, waiting for transfers between devices, delivered(): lax.ppermute(pair, ('tm', 'det'), [(time * dets + det, (time + sign * rea...  9.4 us
    ppermute x6, starting transfers between devices, delivered(): lax.ppermute(pair, ('tm', 'det'), [(time * dets + det, (time + sign * rea...  9.39 us
    pallas_call x2, Pallas kernels, make_timeline(): pl.pallas_call(functools.partial(timeline_kernel, first_step), grid=(step...  8.96 us
    ppermute x8, waiting for transfers between devices, exchanged(): lax.ppermute(value, axis, [(source, source ^ bit) for source in range(cou...  5.94 us
    ppermute x8, starting transfers between devices, exchanged(): lax.ppermute(value, axis, [(source, source ^ bit) for source in range(cou...  3.22 us
    pallas_call x1, Pallas kernels, mode_matrices(): pl.pallas_call(mode_kernel, out_shape=(jax.ShapeDtypeStruct((det_dev, mod...  2.72 us
  transfers between devices with their start and end apart: 14, of which 10 were waited for; matrix products, arithmetic and copies ran while one was open for 0% of the time, Pallas kernels for 21%

profile of v7, /device:TPU:0, one launch (start us, length us, event | category | flops | bytes accessed | tf_op | source)
XLA Modules:
  0.0 69.1 jit_solution(12674119228064897794)
XLA Ops:
  0.6 1.3 %pull_blocks.1 = (f32[2,2,48,128]{3,2,1,0:T(8,128)S(1)}, f32[2,2,48,128]{3,2,1,0:T(8,128)S(1)}) custom-call(s32[1]{0:T(128)} %bitcast.det_ref, s32[1,1,2,4,16]{4,3,2,1,0:T(4,128)} %request_ref.3, f32[3,384,128]{2,1,0:T(8,128)} %direction_ref.5), custom_call_target="tpu_custom_call" | custom-call | tf_op jit(solution)/shard_map/pull_blocks/pallas_call | solution.py:126
  1.9 0.5 collective-permute-start
  2.5 0.9 %collective-permute-done.after_ref = f32[2,2,48,128]{3,2,1,0:T(8,128)S(1)} collective-permute-done((f32[2,2,48,128]{3,2,1,0:T(8,128)S(1)}, f32[2,2,48,128]{3,2,1,0:T(8,128)S(1)}, u32[]{:S(2)}, u32[]{:S(2)}) %collective-permute-start) | collective-permute-done | bytes 98336 | tf_op jit(solution)/shard_map/ppermute | solution.py:509
  3.4 2.9 %collective-permute-start.1 = (f32[2,48,128]{2,1,0:T(8,128)S(1)}, f32[2,48,128]{2,1,0:T(8,128)S(1)}, u32[]{:S(2)}, u32[]{:S(2)}) collective-permute-start(f32[2,48,128]{2,1,0:T(8,128)S(1)} %pad_maximum_fusion.3), channel_id=1, source_target_pairs={{0,2},{1,3},{2,0},{3,1},{4,6},{5,7},{6,4},{7,5},{8,10},{9,11},{10,... | collective-permute-start | bytes 147464 | tf_op jit(solution)/shard_map/ppermute | solution.py:520
  6.3 4.6 %collective-permute-start.2 = (f32[2,48,128]{2,1,0:T(8,128)S(1)}, f32[2,48,128]{2,1,0:T(8,128)S(1)}, u32[]{:S(2)}, u32[]{:S(2)}) collective-permute-start(f32[2,48,128]{2,1,0:T(8,128)S(1)} %pad_maximum_fusion.4), channel_id=1, source_target_pairs={{0,28},{1,29},{2,30},{3,31},{4,0},{5,1},{6,2},{7,3},{8,4},{9,5},{1... | collective-permute-start | bytes 147464 | tf_op jit(solution)/shard_map/ppermute | solution.py:520
  10.9 0.5 collective-permute-start.3
  11.4 2.7 %mode_matrices.1 = (f32[64,16]{1,0:T(8,128)S(1)}, f32[64,1]{1,0:T(8,128)S(1)}) custom-call(s32[1]{0:T(128)} %bitcast.det_ref, f32[16,256]{1,0:T(8,128)} %bitcast.42, f32[1,256]{1,0:T(1,128)} %bitcast.45, f32[1,16]{1,0:T(1,128)} %bitcast.48, f32[2,2,48,128]{3,2,1,0:T(8,128)S(1)} %collective-permute-done.after_ref), custom_call_target="tpu_custom_call" | custom-call | tf_op jit(solution)/shard_map/mode_matrices/pallas_call | solution.py:173
  14.1 0.0 collective-permute-done.1.refs_1_
  14.1 0.0 collective-permute-done.2.refs_2_
  14.1 1.8 %collective-permute-done.3.refs_3_ = f32[2,48,128]{2,1,0:T(8,128)S(1)} collective-permute-done((f32[2,48,128]{2,1,0:T(8,128)S(1)}, f32[2,48,128]{2,1,0:T(8,128)S(1)}, u32[]{:S(2)}, u32[]{:S(2)}) %collective-permute-start.3) | collective-permute-done | bytes 49184 | tf_op jit(solution)/shard_map/ppermute | solution.py:520
  15.9 4.5 %make_timeline.2 = (f32[64,4096]{1,0:T(8,128)}, f32[16,4096]{1,0:T(8,128)S(1)}) custom-call(s32[1]{0:T(128)} %bitcast.det_ref, s32[64,64]{1,0:T(8,128)} %slot_ref.7, f32[16,256]{1,0:T(8,128)} %bitcast.43, f32[1,256]{1,0:T(1,128)} %bitcast.46, s32[64,8192]{1,0:T(8,128)} %offset_ref.7, s32[64,8192]{1,0:T(8,128)} %angle_ref.7, ...), custom_call_target="tpu_custom_call" | custom-call | flops 2147483648 | bytes 4194304 | tf_op jit(solution)/shard_map/make_timeline/pallas_call | solution.py:244
  20.4 0.1 collective-permute-start.4
  20.5 1.3 %collective-permute-done.4 = f32[16,2048]{1,0:T(8,128)S(1)} collective-permute-done((f32[16,2048]{1,0:T(8,128)S(1)}, f32[16,2048]{1,0:T(8,128)S(1)}, u32[]{:S(2)}, u32[]{:S(2)}) %collective-permute-start.4) | collective-permute-done | bytes 131104 | tf_op jit(solution)/shard_map/ppermute | solution.py:509
  21.8 0.6 collective-permute-start.7
  22.4 4.5 %make_timeline.3 = (f32[64,4096]{1,0:T(8,128)}, f32[16,4096]{1,0:T(8,128)S(1)}) custom-call(s32[1]{0:T(128)} %bitcast.det_ref, s32[64,64]{1,0:T(8,128)} %slot_ref.7, f32[16,256]{1,0:T(8,128)} %bitcast.44, f32[1,256]{1,0:T(1,128)} %bitcast.47, s32[64,8192]{1,0:T(8,128)} %offset_ref.7, s32[64,8192]{1,0:T(8,128)} %angle_ref.7, ...), custom_call_target="tpu_custom_call" | custom-call | flops 2147483648 | bytes 4194304 | tf_op jit(solution)/shard_map/make_timeline/pallas_call | solution.py:244
  26.9 0.1 collective-permute-start.5
  27.0 0.4 collective-permute-done.7
  27.4 0.1 collective-permute-start.8
  27.6 0.7 %collective-permute-done.5 = f32[16,2048]{1,0:T(8,128)S(1)} collective-permute-done((f32[16,2048]{1,0:T(8,128)S(1)}, f32[16,2048]{1,0:T(8,128)S(1)}, u32[]{:S(2)}, u32[]{:S(2)}) %collective-permute-start.5) | collective-permute-done | bytes 131104 | tf_op jit(solution)/shard_map/ppermute | solution.py:509
  28.3 1.6 %collective-permute-start.6 = (f32[16,2048]{1,0:T(8,128)S(1)}, f32[16,2048]{1,0:T(8,128)S(1)}, u32[]{:S(2)}, u32[]{:S(2)}) collective-permute-start(f32[16,2048]{1,0:T(8,128)S(1)} %dynamic-slice_add_fusion), channel_id=1, source_target_pairs={{0,2},{1,3},{2,0},{3,1},{4,6},{5,7},{6,4},{7,5},{8,10},{9,11},{10,... | collective-permute-start | bytes 393224 | tf_op jit(solution)/shard_map/ppermute | solution.py:509
  29.9 0.0 collective-permute-done.8
  29.9 7.2 %bin_samples.2.refs_0_ = f32[1024,128]{1,0:T(8,128)S(1)} custom-call(s32[1]{0:T(128)} %bitcast.det_ref, s32[64,64]{1,0:T(8,128)} %slot_ref.7, f32[16,4096]{1,0:T(8,128)S(1)} %pad_maximum_fusion.proj_ref, f32[64,16]{1,0:T(8,128)S(1)} %get-tuple-element.21.back_ref, f32[64,1]{1,0:T(8,128)S(1)} %get-tuple-element.29.weight_ref, s32[64,8192]{1,0:T(8,128)} %offset_ref.7, ...), custom_call_target="tpu_custom_call" | custom-call | flops 4294967296 | bytes 4194304 | tf_op jit(solution)/shard_map/bin_samples/pallas_call | solution.py:383
  37.1 0.0 collective-permute-done.6
  37.2 0.1 collective-permute-start.9
  37.2 1.3 %collective-permute-done.9 = f32[16,2048]{1,0:T(8,128)S(1)} collective-permute-done((f32[16,2048]{1,0:T(8,128)S(1)}, f32[16,2048]{1,0:T(8,128)S(1)}, u32[]{:S(2)}, u32[]{:S(2)}) %collective-permute-start.9) | collective-permute-done | bytes 131104 | tf_op jit(solution)/shard_map/ppermute | solution.py:509
  38.6 0.0 copy-start
  38.6 0.0 copy-start.1
  38.6 0.0 copy-start.2
  38.7 0.0 copy-start.4
  38.7 7.4 %bin_samples.3 = (f32[2,2,48,128]{3,2,1,0:T(8,128)S(1)}, f32[2,2,48,128]{3,2,1,0:T(8,128)S(1)}) custom-call(s32[1]{0:T(128)} %bitcast.det_ref, s32[64,64]{1,0:T(8,128)} %slot_ref.7, f32[16,4096]{1,0:T(8,128)S(1)} %pad_maximum_fusion.1.proj_ref, f32[64,16]{1,0:T(8,128)S(1)} %get-tuple-element.21.back_ref, f32[64,1]{1,0:T(8,128)S(1)} %get-tuple-element.29.weight_ref, ...), custom_call_target="tpu_custom_call" | custom-call | flops 4294967296 | bytes 4194304 | tf_op jit(solution)/shard_map/bin_samples/pallas_call | solution.py:383
  46.1 0.0 copy-start.3
  46.1 0.2 collective-permute-start.10
  46.3 1.2 %collective-permute-done.10 = f32[2,2,48,128]{3,2,1,0:T(8,128)S(1)} collective-permute-done((f32[2,2,48,128]{3,2,1,0:T(8,128)S(1)}, f32[2,2,48,128]{3,2,1,0:T(8,128)S(1)}, u32[]{:S(2)}, u32[]{:S(2)}) %collective-permute-start.10) | collective-permute-done | bytes 98336 | tf_op jit(solution)/shard_map/ppermute | solution.py:509
  47.5 0.6 collective-permute-start.11
  48.1 0.8 %collective-permute-start.12 = (f32[2,48,128]{2,1,0:T(8,128)S(1)}, f32[2,48,128]{2,1,0:T(8,128)S(1)}, u32[]{:S(2)}, u32[]{:S(2)}) collective-permute-start(f32[2,48,128]{2,1,0:T(8,128)S(1)} %pad_maximum_fusion.8), channel_id=1, source_target_pairs={{0,4},{1,5},{2,6},{3,7},{4,8},{5,9},{6,10},{7,11},{8,12},{9,13},{1... | collective-permute-start | bytes 147464 | tf_op jit(solution)/shard_map/ppermute | solution.py:520
  48.9 0.0 collective-permute-start.13
  48.9 3.0 %collective-permute-done.11.refs_1_ = f32[2,48,128]{2,1,0:T(8,128)S(1)} collective-permute-done((f32[2,48,128]{2,1,0:T(8,128)S(1)}, f32[2,48,128]{2,1,0:T(8,128)S(1)}, u32[]{:S(2)}, u32[]{:S(2)}) %collective-permute-start.11) | collective-permute-done | bytes 49184 | tf_op jit(solution)/shard_map/ppermute | solution.py:520
  51.9 3.7 %collective-permute-done.12.refs_2_ = f32[2,48,128]{2,1,0:T(8,128)S(1)} collective-permute-done((f32[2,48,128]{2,1,0:T(8,128)S(1)}, f32[2,48,128]{2,1,0:T(8,128)S(1)}, u32[]{:S(2)}, u32[]{:S(2)}) %collective-permute-start.12) | collective-permute-done | bytes 49184 | tf_op jit(solution)/shard_map/ppermute | solution.py:520
  55.6 1.0 %collective-permute-done.13.refs_3_ = f32[2,48,128]{2,1,0:T(8,128)S(1)} collective-permute-done((f32[2,48,128]{2,1,0:T(8,128)S(1)}, f32[2,48,128]{2,1,0:T(8,128)S(1)}, u32[]{:S(2)}, u32[]{:S(2)}) %collective-permute-start.13) | collective-permute-done | bytes 49184 | tf_op jit(solution)/shard_map/ppermute | solution.py:520
  56.6 0.0 copy-done
  56.6 0.0 copy-done.1
  56.6 0.0 copy-done.2
  56.6 0.0 copy-done.4
  56.6 1.5 %push_blocks.1 = (f32[3,384,128]{2,1,0:T(8,128)S(1)}, f32[32,128]{1,0:T(8,128)S(1)}) custom-call(s32[1]{0:T(128)} %bitcast.det_ref, s32[1,1,2,4,16]{4,3,2,1,0:T(4,128)S(1)} %copy-done.4, f32[3,384,128]{2,1,0:T(8,128)S(1)} %copy-done, f32[3,384,128]{2,1,0:T(8,128)S(1)} %copy-done.2, f32[6,384,128]{2,1,0:T(8,128)S(1)} %copy-done.1, ...), custom_call_target="tpu_custom_call" | custom-call | tf_op jit(solution)/shard_map/push_blocks/pallas_call | solution.py:453
  58.1 9.5 %all_to_all.11 = f32[32,1,128]{2,1,0:T(1,128)S(1)} all-to-all(f32[32,1,128]{2,1,0:T(1,128)S(1)} %bitcast.41), channel_id=1, replica_groups=mesh['tm'=8,'det'=4] {'tm','det'}, dimensions={0} | all-to-all | bytes 32768 | tf_op jit(solution)/shard_map/all_to_all | solution.py:607
  67.5 0.0 copy-done.3
  67.5 1.5 %update_maps.1 = (f32[3,384,128]{2,1,0:T(8,128)}, f32[3,384,128]{2,1,0:T(8,128)}, f32[3,384,128]{2,1,0:T(8,128)}) custom-call(f32[32,128]{1,0:T(8,128)S(1)} %bitcast.40, f32[3,384,128]{2,1,0:T(8,128)S(1)} %copy-done.3, f32[3,384,128]{2,1,0:T(8,128)S(1)} %copy-done.2, f32[3,384,128]{2,1,0:T(8,128)S(1)} %copy-done, ...), custom_call_target="tpu_custom_call" | custom-call | tf_op jit(solution)/shard_map/update_maps/pallas_call | solution.py:496
  (22 shorter events, 0.2 us)
Async XLA Ops:
  1.9 1.5 %collective-permute-start = (f32[2,2,48,128]{3,2,1,0:T(8,128)S(1)}, f32[2,2,48,128]{3,2,1,0:T(8,128)S(1)}, u32[]{:S(2)}, u32[]{:S(2)}) collective-permute-start(f32[2,2,48,128]{3,2,1,0:T(8,128)S(1)} %get-tuple-element.20), channel_id=1, source_target_pairs={{0,1},{1,0},{2,3},{3,2},{4,5},{5,4},{6,7},{7,6},{8,9},{9,8},{10,11... | collective-permute-start | bytes 294920 | tf_op jit(solution)/shard_map/ppermute | solution.py:509
  3.4 10.7 %collective-permute-start.1 = (f32[2,48,128]{2,1,0:T(8,128)S(1)}, f32[2,48,128]{2,1,0:T(8,128)S(1)}, u32[]{:S(2)}, u32[]{:S(2)}) collective-permute-start(f32[2,48,128]{2,1,0:T(8,128)S(1)} %pad_maximum_fusion.3), channel_id=1, source_target_pairs={{0,2},{1,3},{2,0},{3,1},{4,6},{5,7},{6,4},{7,5},{8,10},{9,11},{10,... | collective-permute-start | bytes 147464 | tf_op jit(solution)/shard_map/ppermute | solution.py:520
  6.3 7.8 %collective-permute-start.2 = (f32[2,48,128]{2,1,0:T(8,128)S(1)}, f32[2,48,128]{2,1,0:T(8,128)S(1)}, u32[]{:S(2)}, u32[]{:S(2)}) collective-permute-start(f32[2,48,128]{2,1,0:T(8,128)S(1)} %pad_maximum_fusion.4), channel_id=1, source_target_pairs={{0,28},{1,29},{2,30},{3,31},{4,0},{5,1},{6,2},{7,3},{8,4},{9,5},{1... | collective-permute-start | bytes 147464 | tf_op jit(solution)/shard_map/ppermute | solution.py:520
  10.9 5.0 %collective-permute-start.3 = (f32[2,48,128]{2,1,0:T(8,128)S(1)}, f32[2,48,128]{2,1,0:T(8,128)S(1)}, u32[]{:S(2)}, u32[]{:S(2)}) collective-permute-start(f32[2,48,128]{2,1,0:T(8,128)S(1)} %pad_maximum_fusion.5), channel_id=1, source_target_pairs={{0,30},{1,31},{2,28},{3,29},{4,2},{5,3},{6,0},{7,1},{8,6},{9,7},{1... | collective-permute-start | bytes 147464 | tf_op jit(solution)/shard_map/ppermute | solution.py:520
  20.4 1.4 %collective-permute-start.4 = (f32[16,2048]{1,0:T(8,128)S(1)}, f32[16,2048]{1,0:T(8,128)S(1)}, u32[]{:S(2)}, u32[]{:S(2)}) collective-permute-start(f32[16,2048]{1,0:T(8,128)S(1)} %constant_dynamic-slice_fusion.1), channel_id=1, source_target_pairs={{0,1},{1,0},{2,3},{3,2},{4,5},{5,4},{6,7},{7,6},{8,9},{9,8},{10,11... | collective-permute-start | bytes 393224 | tf_op jit(solution)/shard_map/ppermute | solution.py:509
  21.8 5.6 %collective-permute-start.7 = (f32[16,2048]{1,0:T(8,128)S(1)}, f32[16,2048]{1,0:T(8,128)S(1)}, u32[]{:S(2)}, u32[]{:S(2)}) collective-permute-start(f32[16,2048]{1,0:T(8,128)S(1)} %dynamic-slice_add_fusion.1), channel_id=1, source_target_pairs={{0,2},{1,3},{2,0},{3,1},{4,6},{5,7},{6,4},{7,5},{8,10},{9,11},{10,... | collective-permute-start | bytes 393224 | tf_op jit(solution)/shard_map/ppermute | solution.py:509
  26.9 1.4 %collective-permute-start.5 = (f32[16,2048]{1,0:T(8,128)S(1)}, f32[16,2048]{1,0:T(8,128)S(1)}, u32[]{:S(2)}, u32[]{:S(2)}) collective-permute-start(f32[16,2048]{1,0:T(8,128)S(1)} %constant_dynamic-slice_fusion), channel_id=1, source_target_pairs={{0,1},{1,0},{2,3},{3,2},{4,5},{5,4},{6,7},{7,6},{8,9},{9,8},{10,11... | collective-permute-start | bytes 393224 | tf_op jit(solution)/shard_map/ppermute | solution.py:509
  27.4 2.5 %collective-permute-start.8 = (f32[16,2048]{1,0:T(8,128)S(1)}, f32[16,2048]{1,0:T(8,128)S(1)}, u32[]{:S(2)}, u32[]{:S(2)}) collective-permute-start(f32[16,2048]{1,0:T(8,128)S(1)} %add.33), channel_id=1, source_target_pairs={{0,1},{1,0},{2,3},{3,2},{4,5},{5,4},{6,7},{7,6},{8,9},{9,8},{10,11... | collective-permute-start | bytes 393224 | tf_op jit(solution)/shard_map/ppermute | solution.py:509
  28.3 8.8 %collective-permute-start.6 = (f32[16,2048]{1,0:T(8,128)S(1)}, f32[16,2048]{1,0:T(8,128)S(1)}, u32[]{:S(2)}, u32[]{:S(2)}) collective-permute-start(f32[16,2048]{1,0:T(8,128)S(1)} %dynamic-slice_add_fusion), channel_id=1, source_target_pairs={{0,2},{1,3},{2,0},{3,1},{4,6},{5,7},{6,4},{7,5},{8,10},{9,11},{10,... | collective-permute-start | bytes 393224 | tf_op jit(solution)/shard_map/ppermute | solution.py:509
  37.2 1.4 %collective-permute-start.9 = (f32[16,2048]{1,0:T(8,128)S(1)}, f32[16,2048]{1,0:T(8,128)S(1)}, u32[]{:S(2)}, u32[]{:S(2)}) collective-permute-start(f32[16,2048]{1,0:T(8,128)S(1)} %add.32), channel_id=1, source_target_pairs={{0,1},{1,0},{2,3},{3,2},{4,5},{5,4},{6,7},{7,6},{8,9},{9,8},{10,11... | collective-permute-start | bytes 393224 | tf_op jit(solution)/shard_map/ppermute | solution.py:509
  38.6 17.9 %copy-start = (f32[3,384,128]{2,1,0:T(8,128)S(1)}, f32[3,384,128]{2,1,0:T(8,128)}, u32[]{:S(2)}) copy-start(f32[3,384,128]{2,1,0:T(8,128)} %direction_ref.5) | copy-start | bytes 1769476
  38.6 17.9 %copy-start.1 = (f32[6,384,128]{2,1,0:T(8,128)S(1)}, f32[6,384,128]{2,1,0:T(8,128)}, u32[]{:S(2)}) copy-start(f32[6,384,128]{2,1,0:T(8,128)} %pre_ref.3) | copy-start | bytes 3538948
  38.6 17.9 %copy-start.2 = (f32[3,384,128]{2,1,0:T(8,128)S(1)}, f32[3,384,128]{2,1,0:T(8,128)}, u32[]{:S(2)}) copy-start(f32[3,384,128]{2,1,0:T(8,128)} %residual_ref.3) | copy-start | bytes 1769476
  38.7 17.9 %copy-start.4 = (s32[1,1,2,4,16]{4,3,2,1,0:T(4,128)S(1)}, s32[1,1,2,4,16]{4,3,2,1,0:T(4,128)}, u32[]{:S(2)}) copy-start(s32[1,1,2,4,16]{4,3,2,1,0:T(4,128)} %request_ref.3) | copy-start | bytes 1540
  46.1 21.5 %copy-start.3 = (f32[3,384,128]{2,1,0:T(8,128)S(1)}, f32[3,384,128]{2,1,0:T(8,128)}, u32[]{:S(2)}) copy-start(f32[3,384,128]{2,1,0:T(8,128)} %solution_ref.1) | copy-start | bytes 1769476
  46.1 1.4 %collective-permute-start.10 = (f32[2,2,48,128]{3,2,1,0:T(8,128)S(1)}, f32[2,2,48,128]{3,2,1,0:T(8,128)S(1)}, u32[]{:S(2)}, u32[]{:S(2)}) collective-permute-start(f32[2,2,48,128]{3,2,1,0:T(8,128)S(1)} %get-tuple-element.34), channel_id=1, source_target_pairs={{0,1},{1,0},{2,3},{3,2},{4,5},{5,4},{6,7},{7,6},{8,9},{9,8},{10,11... | collective-permute-start | bytes 294920 | tf_op jit(solution)/shard_map/ppermute | solution.py:509
  47.5 4.4 %collective-permute-start.11 = (f32[2,48,128]{2,1,0:T(8,128)S(1)}, f32[2,48,128]{2,1,0:T(8,128)S(1)}, u32[]{:S(2)}, u32[]{:S(2)}) collective-permute-start(f32[2,48,128]{2,1,0:T(8,128)S(1)} %pad_maximum_fusion.7), channel_id=1, source_target_pairs={{0,2},{1,3},{2,0},{3,1},{4,6},{5,7},{6,4},{7,5},{8,10},{9,11},{10,... | collective-permute-start | bytes 147464 | tf_op jit(solution)/shard_map/ppermute | solution.py:520
  48.1 7.5 %collective-permute-start.12 = (f32[2,48,128]{2,1,0:T(8,128)S(1)}, f32[2,48,128]{2,1,0:T(8,128)S(1)}, u32[]{:S(2)}, u32[]{:S(2)}) collective-permute-start(f32[2,48,128]{2,1,0:T(8,128)S(1)} %pad_maximum_fusion.8), channel_id=1, source_target_pairs={{0,4},{1,5},{2,6},{3,7},{4,8},{5,9},{6,10},{7,11},{8,12},{9,13},{1... | collective-permute-start | bytes 147464 | tf_op jit(solution)/shard_map/ppermute | solution.py:520
  48.9 7.7 %collective-permute-start.13 = (f32[2,48,128]{2,1,0:T(8,128)S(1)}, f32[2,48,128]{2,1,0:T(8,128)S(1)}, u32[]{:S(2)}, u32[]{:S(2)}) collective-permute-start(f32[2,48,128]{2,1,0:T(8,128)S(1)} %pad_maximum_fusion.9), channel_id=1, source_target_pairs={{0,6},{1,7},{2,4},{3,5},{4,10},{5,11},{6,8},{7,9},{8,14},{9,15},{1... | collective-permute-start | bytes 147464 | tf_op jit(solution)/shard_map/ppermute | solution.py:520
